TPU v7x, 32 devices: a whole 2x2x4 slice. The times are simulated.
32 devices in a mesh: shard: 4 (over z), dp: 4 (over y, x), mp: 2 (over core).
Axes of the slice: x: 2, y: 2, z: 4, core: 2. Of those that a mesh axis runs over, the one named last changes fastest.
Arguments:
- tokens_in: bfloat16 [2048, 2560], P(('shard', 'dp')), may hold values from -6 to 6
- segment_ids: int32 [2048], P(('shard', 'dp')), may hold values from 0 to 3, never falling along the last dimension, each value on 1 to 1024 neighbouring positions
- block_cotangent: bfloat16 [2048, 2560], P(('shard', 'dp')), may hold values from -6 to 6
- query_weight: bfloat16 [2560, 2560], P(('shard', 'dp'), 'mp'), may hold values from -0.125 to 0.125
- keyval_weight: bfloat16 [2560, 512], P(('shard', 'dp')), may hold values from -0.125 to 0.125
- outproj_weight: bfloat16 [2560, 2560], P('mp', ('shard', 'dp')), may hold values from -2 to 2
- gateup_weight: bfloat16 [2560, 2, 7680], P(('shard', 'dp'), None, 'mp'), may hold values from -0.125 to 0.125
- down_weight: bfloat16 [7680, 2560], P('mp', ('shard', 'dp')), may hold values from -0.0625 to 0.0625
- norm_gains: bfloat16 [2, 2560], P(None, ('shard', 'dp')), may hold values from 0.5 to 1.5
- query_first: float32 [2560, 2560], P(('shard', 'dp'), 'mp'), may hold values from -40 to 40
- keyval_first: float32 [2560, 512], P(('shard', 'dp')), may hold values from -96 to 96
- outproj_first: float32 [2560, 2560], P('mp', ('shard', 'dp')), may hold values from -3 to 3
- gateup_first: float32 [2560, 2, 7680], P(('shard', 'dp'), None, 'mp'), may hold values from -12 to 12
- down_first: float32 [7680, 2560], P('mp', ('shard', 'dp')), may hold values from -20 to 20
- gains_first: float32 [2, 2560], P(None, ('shard', 'dp')), may hold values from -40 to 40
- query_second: float32 [2560, 2560], P(('shard', 'dp'), 'mp'), may hold values from 65.536 to 491.52
- keyval_second: float32 [2560, 512], P(('shard', 'dp')), may hold values from 409.6 to 3072
- outproj_second: float32 [2560, 2560], P('mp', ('shard', 'dp')), may hold values from 0.4096 to 3.072
- gateup_second: float32 [2560, 2, 7680], P(('shard', 'dp'), None, 'mp'), may hold values from 6.144 to 45.056
- down_second: float32 [7680, 2560], P('mp', ('shard', 'dp')), may hold values from 16.384 to 122.88
- gains_second: float32 [2, 2560], P(None, ('shard', 'dp')), may hold values from 65.536 to 491.52
- step_count: int32 [1], replicated, may hold values from 1 to 20
Outputs:
- block_out: bfloat16 [2048, 2560], P(('shard', 'dp'))
- input_grad: float32 [2048, 2560], P(('shard', 'dp'))
- query_grad: float32 [2560, 2560], P(('shard', 'dp'), 'mp')
- keyval_grad: float32 [2560, 512], P(('shard', 'dp'))
- outproj_grad: float32 [2560, 2560], P('mp', ('shard', 'dp'))
- gateup_grad: float32 [2560, 2, 7680], P(('shard', 'dp'), None, 'mp')
- down_grad: float32 [7680, 2560], P('mp', ('shard', 'dp'))
- gains_grad: float32 [2, 2560], P(None, ('shard', 'dp'))
- query_first_new: float32 [2560, 2560], P(('shard', 'dp'), 'mp')
- keyval_first_new: float32 [2560, 512], P(('shard', 'dp'))
- outproj_first_new: float32 [2560, 2560], P('mp', ('shard', 'dp'))
- gateup_first_new: float32 [2560, 2, 7680], P(('shard', 'dp'), None, 'mp')
- down_first_new: float32 [7680, 2560], P('mp', ('shard', 'dp'))
- gains_first_new: float32 [2, 2560], P(None, ('shard', 'dp'))
- query_second_new: float32 [2560, 2560], P(('shard', 'dp'), 'mp')
- keyval_second_new: float32 [2560, 512], P(('shard', 'dp'))
- outproj_second_new: float32 [2560, 2560], P('mp', ('shard', 'dp'))
- gateup_second_new: float32 [2560, 2, 7680], P(('shard', 'dp'), None, 'mp')
- down_second_new: float32 [7680, 2560], P('mp', ('shard', 'dp'))
- gains_second_new: float32 [2, 2560], P(None, ('shard', 'dp'))
- query_update: float32 [2560, 2560], P(('shard', 'dp'), 'mp')
- keyval_update: float32 [2560, 512], P(('shard', 'dp'))
- outproj_update: float32 [2560, 2560], P('mp', ('shard', 'dp'))
- gateup_update: float32 [2560, 2, 7680], P(('shard', 'dp'), None, 'mp')
- down_update: float32 [7680, 2560], P('mp', ('shard', 'dp'))
- gains_update: float32 [2, 2560], P(None, ('shard', 'dp'))
Inputs may be any that keep to these rules, and one draw needn't show every extreme that they name: `segment_ids`: segment ids never fall along the tokens; every document has 1 to 1024 tokens and one has exactly 1024.
All inputs are finite; a program needn't handle non-finite values.
Results may differ from a plain program's by a relative error of at most 0.028.
Values may be sent and summed in bfloat16 or wider, within the bound.
A program may use at most 576 MiB of HBM per device.

v0:
```python
from functools import partial

import jax
import jax.numpy as jnp
from jax import lax
from jax.sharding import PartitionSpec as P

HEAD_DIM = 256
KV_BLOCKS = 8


EPS_NORM = 1e-06
BETA_ONE = 0.9
BETA_TWO = 0.95
ADAM_EPS = 1e-08
LEARN_RATE = 0.01
DECAY_RATE = 0.1
ROPE_BASE = 10000.0


def shifted(value, axis, steps):
    count = lax.axis_size(axis)
    initial, last = (max(0, -steps), min(count, count - steps))
    return lax.ppermute(value, axis, [(source, source + steps) for source in range(initial, last)])


def rms_scale(values, gain_row):
    inverse = lax.rsqrt(jnp.mean(values * values, axis=1, keepdims=True) + EPS_NORM)
    return values * inverse * gain_row


def rope_tables(positions):
    half_dim = HEAD_DIM // 2
    exponent = jnp.arange(half_dim, dtype=jnp.float32) * (-2.0 / HEAD_DIM)
    angles = positions.astype(jnp.float32)[:, None] * jnp.power(ROPE_BASE, exponent)[None, :]
    return (jnp.cos(angles), jnp.sin(angles))


def rotate(values, cosine, sine_rows):
    half_dim = values.shape[-1] // 2
    front_half = values[..., :half_dim]
    back_half = values[..., half_dim:]
    cos_heads = cosine[:, None, :]
    sin_heads = sine_rows[:, None, :]
    return jnp.concatenate(
        [
            front_half * cos_heads - back_half * sin_heads,
            back_half * cos_heads + front_half * sin_heads,
        ],
        axis=-1,
    )


def unrotate(grad_in, cosine, sine_rows):
    half_dim = grad_in.shape[-1] // 2
    front_half = grad_in[..., :half_dim]
    back_half = grad_in[..., half_dim:]
    cos_heads = cosine[:, None, :]
    sin_heads = sine_rows[:, None, :]
    return jnp.concatenate(
        [
            front_half * cos_heads + back_half * sin_heads,
            back_half * cos_heads - front_half * sin_heads,
        ],
        axis=-1,
    )


def rows_product(left_side, right_side):
    return lax.dot_general(
        left_side, right_side, (((0,), (0,)), ((), ())), preferred_element_type=jnp.float32
    )


def cols_product(left_side, right_side):
    return lax.dot_general(
        left_side, right_side, (((1,), (1,)), ((), ())), preferred_element_type=jnp.float32
    )


def adam_update(grad_own, weight, first_old, second_old, bias_first, bias_second, decay):
    first_new = BETA_ONE * first_old + (1.0 - BETA_ONE) * grad_own
    second_new = BETA_TWO * second_old + (1.0 - BETA_TWO) * grad_own * grad_own
    direction = first_new / bias_first / (jnp.sqrt(second_new / bias_second) + ADAM_EPS)
    return (first_new, second_new, -LEARN_RATE * (direction + decay * weight.astype(jnp.float32)))


def shards(
    tokens_in,
    segment_ids,
    block_cotangent,
    query_weight,
    keyval_weight,
    outproj_weight,
    gateup_weight,
    down_weight,
    norm_gains,
    query_first,
    keyval_first,
    outproj_first,
    gateup_first,
    down_first,
    gains_first,
    query_second,
    keyval_second,
    outproj_second,
    gateup_second,
    down_second,
    gains_second,
    step_count,
):
    full_query, full_keyval, full_outproj, full_gateup, full_down, full_gains = (
        lax.all_gather(query_weight, ("shard", "dp"), axis=0, tiled=True),
        lax.all_gather(keyval_weight, ("shard", "dp"), axis=0, tiled=True),
        lax.all_gather(outproj_weight, ("shard", "dp"), axis=1, tiled=True),
        lax.all_gather(gateup_weight, ("shard", "dp"), axis=0, tiled=True),
        lax.all_gather(down_weight, ("shard", "dp"), axis=1, tiled=True),
        lax.all_gather(norm_gains, ("shard", "dp"), axis=1, tiled=True),
    )
    tok_rows = tokens_in.shape[0]
    model_width = tokens_in.shape[1]
    ff_local = full_down.shape[0]
    heads_local = full_query.shape[1] // HEAD_DIM
    key_span = (KV_BLOCKS + 1) * tok_rows
    score_scale = HEAD_DIM ** (-0.5)
    seg_tags = segment_ids + 1
    earlier_tags = []
    for offset in range(KV_BLOCKS, 0, -1):
        earlier_tags.append(shifted(seg_tags, ("shard", "dp"), offset))
    key_tags = jnp.concatenate(earlier_tags + [seg_tags], axis=0)
    query_index = jnp.arange(tok_rows, dtype=jnp.int32) + KV_BLOCKS * tok_rows
    key_index = jnp.arange(key_span, dtype=jnp.int32)
    same_segment = key_tags[None, :] == seg_tags[:, None]
    allowed = same_segment & (key_index[None, :] <= query_index[:, None])
    before_count = (same_segment & (key_index[None, :] < query_index[:, None])).astype(jnp.int32)
    positions = jnp.sum(before_count, axis=1)
    cosine, sine_rows = rope_tables(positions)
    input_rows = tokens_in.astype(jnp.float32)
    normed_one, pull_one = jax.vjp(rms_scale, input_rows, full_gains[0].astype(jnp.float32))
    hidden_one = normed_one.astype(jnp.bfloat16)
    query_raw = jnp.dot(hidden_one, full_query, preferred_element_type=jnp.float32)
    keyval_raw = jnp.dot(hidden_one, full_keyval, preferred_element_type=jnp.float32)
    queries = rotate(query_raw.reshape(tok_rows, heads_local, HEAD_DIM), cosine, sine_rows).astype(
        jnp.bfloat16
    )
    key_local = rotate(keyval_raw[:, None, :HEAD_DIM], cosine, sine_rows)[:, 0].astype(jnp.bfloat16)
    keyval_local = jnp.concatenate(
        [key_local, keyval_raw[:, HEAD_DIM:].astype(jnp.bfloat16)], axis=1
    )
    earlier_pairs = []
    for offset in range(KV_BLOCKS, 0, -1):
        earlier_pairs.append(shifted(keyval_local, ("shard", "dp"), offset))
    keyval_window = jnp.concatenate(earlier_pairs + [keyval_local], axis=0)
    key_rows = keyval_window[:, :HEAD_DIM]
    value_rows = keyval_window[:, HEAD_DIM:]
    scores = (
        jnp.einsum("thd,kd->htk", queries, key_rows, preferred_element_type=jnp.float32)
        * score_scale
    )
    scores = jnp.where(allowed[None], scores, -jnp.inf)
    row_max = jnp.max(scores, axis=2, keepdims=True)
    row_total = jnp.sum(jnp.exp(scores - row_max), axis=2, keepdims=True)
    log_total = row_max + jnp.log(row_total)
    probs_low = jnp.exp(scores - log_total).astype(jnp.bfloat16)
    mixed = jnp.einsum("htk,kd->thd", probs_low, value_rows, preferred_element_type=jnp.float32)
    mixed_low = mixed.reshape(tok_rows, heads_local * HEAD_DIM).astype(jnp.bfloat16)
    attn_part = jnp.dot(mixed_low, full_outproj, preferred_element_type=jnp.float32)
    residual = input_rows + lax.psum(attn_part.astype(jnp.bfloat16), "mp").astype(jnp.float32)
    normed_two, pull_two = jax.vjp(rms_scale, residual, full_gains[1].astype(jnp.float32))
    hidden_two = normed_two.astype(jnp.bfloat16)
    gateup_flat = full_gateup.reshape(model_width, 2 * ff_local)
    gateup_pre = jnp.dot(hidden_two, gateup_flat, preferred_element_type=jnp.float32)
    gate_pre = gateup_pre[:, :ff_local]
    up_pre = gateup_pre[:, ff_local:]
    gelu_val, gelu_pull = jax.vjp(partial(jax.nn.gelu, approximate=True), gate_pre)
    act_low = (gelu_val * up_pre).astype(jnp.bfloat16)
    ffn_part = jnp.dot(act_low, full_down, preferred_element_type=jnp.float32)
    block_out = (
        residual + lax.psum(ffn_part.astype(jnp.bfloat16), "mp").astype(jnp.float32)
    ).astype(jnp.bfloat16)
    cotangent = block_cotangent.astype(jnp.float32)
    down_grad = rows_product(act_low, block_cotangent)
    act_grad = cols_product(block_cotangent, full_down)
    gate_grad = gelu_pull(act_grad * up_pre)[0]
    up_grad = act_grad * gelu_val
    gateup_low = jnp.concatenate([gate_grad, up_grad], axis=1).astype(jnp.bfloat16)
    gateup_grad = rows_product(hidden_two, gateup_low).reshape(model_width, 2, ff_local)
    own_gateup, own_down = (
        lax.psum_scatter(gateup_grad, ("shard", "dp"), scatter_dimension=0, tiled=True),
        lax.psum_scatter(down_grad, ("shard", "dp"), scatter_dimension=1, tiled=True),
    )
    hidden_two_grad = lax.psum(
        cols_product(gateup_low, gateup_flat).astype(jnp.bfloat16), "mp"
    ).astype(jnp.float32)
    residual_from, gain_two_grad = pull_two(hidden_two_grad)
    residual_grad = cotangent + residual_from
    attn_low = residual_grad.astype(jnp.bfloat16)
    outproj_grad = rows_product(mixed_low, attn_low)
    mixed_grad = (
        cols_product(attn_low, full_outproj)
        .astype(jnp.bfloat16)
        .reshape(tok_rows, heads_local, HEAD_DIM)
    )
    scores_again = (
        jnp.einsum("thd,kd->htk", queries, key_rows, preferred_element_type=jnp.float32)
        * score_scale
    )
    scores_again = jnp.where(allowed[None], scores_again, -jnp.inf)
    probs_again = jnp.exp(scores_again - log_total)
    probs_again_low = probs_again.astype(jnp.bfloat16)
    probs_grad = jnp.einsum(
        "thd,kd->htk", mixed_grad, value_rows, preferred_element_type=jnp.float32
    )
    value_grad = jnp.einsum(
        "htk,thd->kd", probs_again_low, mixed_grad, preferred_element_type=jnp.float32
    )
    inner_sum = jnp.sum(probs_again * probs_grad, axis=2, keepdims=True)
    scores_low = (probs_again * (probs_grad - inner_sum) * score_scale).astype(jnp.bfloat16)
    query_rot_grad = jnp.einsum(
        "htk,kd->thd", scores_low, key_rows, preferred_element_type=jnp.float32
    )
    key_rot_grad = jnp.einsum(
        "htk,thd->kd", scores_low, queries, preferred_element_type=jnp.float32
    )
    window_grad = jnp.concatenate([key_rot_grad, value_grad], axis=1)
    keyval_sum = window_grad[KV_BLOCKS * tok_rows :]
    for offset in range(1, KV_BLOCKS + 1):
        start_row = (KV_BLOCKS - offset) * tok_rows
        keyval_sum = keyval_sum + shifted(
            window_grad[start_row : start_row + tok_rows].astype(jnp.bfloat16),
            ("shard", "dp"),
            -offset,
        ).astype(jnp.float32)
    query_low = (
        unrotate(query_rot_grad, cosine, sine_rows)
        .reshape(tok_rows, heads_local * HEAD_DIM)
        .astype(jnp.bfloat16)
    )
    query_part = cols_product(query_low, full_query)
    hidden_part, keyval_total = (
        lax.psum(query_part.astype(jnp.bfloat16), "mp").astype(jnp.float32),
        lax.psum(keyval_sum.astype(jnp.bfloat16), "mp").astype(jnp.float32),
    )
    key_raw_grad = unrotate(keyval_total[:, None, :HEAD_DIM], cosine, sine_rows)[:, 0]
    keyval_low = jnp.concatenate([key_raw_grad, keyval_total[:, HEAD_DIM:]], axis=1).astype(
        jnp.bfloat16
    )
    hidden_one_grad = hidden_part + cols_product(keyval_low, full_keyval)
    query_grad = rows_product(hidden_one, query_low)
    keyval_grad = rows_product(hidden_one, keyval_low)
    input_from, gain_one_grad = pull_one(hidden_one_grad)
    input_grad = residual_grad + input_from
    gains_grad = jnp.stack([gain_one_grad, gain_two_grad], axis=0)
    own_query, own_keyval, own_outproj, own_gains = (
        lax.psum_scatter(query_grad, ("shard", "dp"), scatter_dimension=0, tiled=True),
        lax.psum_scatter(keyval_grad, ("shard", "dp"), scatter_dimension=0, tiled=True),
        lax.psum_scatter(outproj_grad, ("shard", "dp"), scatter_dimension=1, tiled=True),
        lax.psum_scatter(gains_grad, ("shard", "dp"), scatter_dimension=1, tiled=True),
    )
    step_value = step_count[0].astype(jnp.float32)
    bias_first = 1.0 - jnp.power(BETA_ONE, step_value)
    bias_second = 1.0 - jnp.power(BETA_TWO, step_value)
    query_new = adam_update(
        own_query, query_weight, query_first, query_second, bias_first, bias_second, DECAY_RATE
    )
    keyval_new = adam_update(
        own_keyval, keyval_weight, keyval_first, keyval_second, bias_first, bias_second, DECAY_RATE
    )
    outproj_new = adam_update(
        own_outproj,
        outproj_weight,
        outproj_first,
        outproj_second,
        bias_first,
        bias_second,
        DECAY_RATE,
    )
    gateup_new = adam_update(
        own_gateup, gateup_weight, gateup_first, gateup_second, bias_first, bias_second, DECAY_RATE
    )
    down_new = adam_update(
        own_down, down_weight, down_first, down_second, bias_first, bias_second, DECAY_RATE
    )
    gains_new = adam_update(
        own_gains, norm_gains, gains_first, gains_second, bias_first, bias_second, 0.0
    )
    return (
        block_out,
        input_grad,
        own_query,
        own_keyval,
        own_outproj,
        own_gateup,
        own_down,
        own_gains,
        query_new[0],
        keyval_new[0],
        outproj_new[0],
        gateup_new[0],
        down_new[0],
        gains_new[0],
        query_new[1],
        keyval_new[1],
        outproj_new[1],
        gateup_new[1],
        down_new[1],
        gains_new[1],
        query_new[2],
        keyval_new[2],
        outproj_new[2],
        gateup_new[2],
        down_new[2],
        gains_new[2],
    )


def solution(mesh):
    in_specs = (
        P(("shard", "dp"), None),
        P(("shard", "dp")),
        P(("shard", "dp"), None),
        P(("shard", "dp"), "mp"),
        P(("shard", "dp"), None),
        P("mp", ("shard", "dp")),
        P(("shard", "dp"), None, "mp"),
        P("mp", ("shard", "dp")),
        P(None, ("shard", "dp")),
        P(("shard", "dp"), "mp"),
        P(("shard", "dp"), None),
        P("mp", ("shard", "dp")),
        P(("shard", "dp"), None, "mp"),
        P("mp", ("shard", "dp")),
        P(None, ("shard", "dp")),
        P(("shard", "dp"), "mp"),
        P(("shard", "dp"), None),
        P("mp", ("shard", "dp")),
        P(("shard", "dp"), None, "mp"),
        P("mp", ("shard", "dp")),
        P(None, ("shard", "dp")),
        P(),
    )
    out_specs = (
        P(("shard", "dp"), None),
        P(("shard", "dp"), None),
        P(("shard", "dp"), "mp"),
        P(("shard", "dp"), None),
        P("mp", ("shard", "dp")),
        P(("shard", "dp"), None, "mp"),
        P("mp", ("shard", "dp")),
        P(None, ("shard", "dp")),
        P(("shard", "dp"), "mp"),
        P(("shard", "dp"), None),
        P("mp", ("shard", "dp")),
        P(("shard", "dp"), None, "mp"),
        P("mp", ("shard", "dp")),
        P(None, ("shard", "dp")),
        P(("shard", "dp"), "mp"),
        P(("shard", "dp"), None),
        P("mp", ("shard", "dp")),
        P(("shard", "dp"), None, "mp"),
        P("mp", ("shard", "dp")),
        P(None, ("shard", "dp")),
        P(("shard", "dp"), "mp"),
        P(("shard", "dp"), None),
        P("mp", ("shard", "dp")),
        P(("shard", "dp"), None, "mp"),
        P("mp", ("shard", "dp")),
        P(None, ("shard", "dp")),
    )
    return jax.shard_map(shards, mesh=mesh, in_specs=in_specs, out_specs=out_specs, check_vma=False)
```

profile of v0, /device:TPU:14, one launch (start us, length us, event | category | flops | bytes accessed | tf_op | source)
XLA Modules:
  0.0 4453.6 jit_solution(12682853102505052794)
XLA Ops:
  22.3 29.0 all-gather
  89.2 12.2 collective-permute-done.8
  117.1 10.1 collective-permute-done.13
  127.2 9.0 collective-permute-done.14
  140.9 47.3 %all-gather.9.cloned.1.call-done = bf16[2560,1280]{1,0:T(8,128)(2,1)} async-done(((bf16[160,1280]{1,0:T(8,128)(2,1)}), bf16[2560,1280]{1,0:T(8,128)(2,1)}) %all-gather.9.cloned.1.call-update) | async-done | bytes 6553616 | tf_op jit(solution)/shard_map/all_gather | solution.py:113
  198.5 87.4 %all-gather.11.cloned.1.call-done = bf16[1280,2560]{0,1:T(8,128)(2,1)} async-done(((bf16[1280,160]{0,1:T(8,128)(2,1)}), bf16[1280,2560]{0,1:T(8,128)(2,1)}) %all-gather.11.cloned.1.call-update) | async-done | bytes 6553616 | tf_op jit(solution)/shard_map/all_gather | solution.py:115
  293.6 17.5 all-reduce.7.cloned.1.call-done
  312.5 405.2 %all-gather.13.cloned.1.call-done = bf16[2560,2,3840]{2,1,0:T(2,128)(2,1)} async-done(((bf16[160,2,3840]{2,1,0:T(2,128)(2,1)}), bf16[2560,2,3840]{2,1,0:T(2,128)(2,1)}) %all-gather.13.cloned.1.call-update) | async-done | bytes 39321616 | tf_op jit(solution)/shard_map/all_gather | solution.py:116
  717.7 27.0 copy.116
  744.7 17.2 fusion.97
  762.0 175.9 %all-gather.15.cloned.1.call-done = bf16[3840,2560]{0,1:T(8,128)(2,1)} async-done(((bf16[3840,160]{0,1:T(8,128)(2,1)}), bf16[3840,2560]{0,1:T(8,128)(2,1)}) %all-gather.15.cloned.1.call-update) | async-done | bytes 19660816 | tf_op jit(solution)/shard_map/all_gather | solution.py:117
  937.8 12.9 fusion.18
  950.8 19.6 convolution_convert_fusion.3
  970.6 13.8 convolution_convert_fusion
  984.4 6.3 all-reduce.9.cloned.1.call-done
  1001.1 7.0 fusion.42
  1008.1 6.7 convolution_bitcast_fusion.2
  1030.5 7.7 collective-permute-start.17
  1043.5 6.1 convolution_convert_fusion.1
  1057.7 19.6 all-reduce.13.cloned.1.call-done
  1087.6 6.7 fusion.99
  1095.5 7.0 fusion.51
  1102.5 16.6 fusion.116
  1119.4 28.9 fusion.45
  1148.3 86.3 %reshape.283 = f32[2560,2,3840]{2,1,0:T(2,128)} reshape(f32[2560,7680]{1,0:T(8,128)} %fusion.45) | data formatting | bytes 157286400 | tf_op jit(solution)/shard_map/reshape | solution.py:187
  1242.2 36.1 reduce-scatter.10.cloned.1.call-done
  1280.6 277.1 %reduce-scatter.8.cloned.1.call-done = f32[160,1280]{1,0:T(8,128)} async-done(((f32[2560,1280]{1,0:T(8,128)}), f32[160,1280]{1,0:T(8,128)}) %reduce-scatter.8.cloned.1.call-update) | async-done | bytes 819216 | tf_op jit(solution)/shard_map/reduce_scatter | solution.py:255
  1560.6 277.4 %reduce-scatter.12.cloned.1.call-done = f32[1280,160]{0,1:T(8,128)} async-done(((f32[1280,2560]{0,1:T(8,128)}), f32[1280,160]{0,1:T(8,128)}) %reduce-scatter.12.cloned.1.call-update) | async-done | bytes 819216 | tf_op jit(solution)/shard_map/reduce_scatter | solution.py:257
  1841.2 574.2 %reduce-scatter.14.cloned.1.call-done = f32[3840,160]{0,1:T(8,128)} async-done(((f32[3840,2560]{0,1:T(8,128)}), f32[3840,160]{0,1:T(8,128)}) %reduce-scatter.14.cloned.1.call-update) | async-done | bytes 2457616 | tf_op jit(solution)/shard_map/reduce_scatter | solution.py:190
  2415.4 7.7 add_multiply_fusion.1
  2423.1 1999.8 %all-reduce.11.cloned.1.call-done = f32[2560,2,3840]{2,1,0:T(2,128)} async-done(((f32[2560,2,3840]{2,1,0:T(2,128)}), f32[2560,2,3840]{2,1,0:T(2,128)}) %all-reduce.11.cloned.1.call-update) | async-done | bytes 78643216
  4422.9 23.6 add_multiply_fusion
  (222 shorter events, 158.0 us)
Async XLA Ops:
  7.2 68.3 %all-gather.7.cloned.1.call-start = ((), (), s32[]{:S(2)}) async-start(), calls=%async_computation.5 | async-start | bytes 2785280 | tf_op jit(solution)/shard_map/all_gather | solution.py:114
  7.9 180.3 %all-gather.9.cloned.1.call-start = ((), (), s32[]{:S(2)}) async-start(), calls=%async_computation.6 | async-start | bytes 6963200 | tf_op jit(solution)/shard_map/all_gather | solution.py:113
  8.7 277.2 %all-gather.11.cloned.1.call-start = ((), (), s32[]{:S(2)}) async-start(), calls=%async_computation.7 | async-start | bytes 6963200 | tf_op jit(solution)/shard_map/all_gather | solution.py:115
  9.4 301.7 %all-reduce.7.cloned.1.call-start = ((), (), s32[]{:S(2)}) async-start(), calls=%async_computation.8 | async-start | bytes 1310720 | tf_op jit(solution)/shard_map/psum | solution.py:168
  10.1 43.2 collective-permute-start
  14.6 42.2 collective-permute-start.1
  16.6 46.3 %collective-permute-start.2 = (s32[128]{0:T(128)S(1)}, s32[128]{0:T(128)S(1)}, u32[]{:S(2)}, u32[]{:S(2)}) collective-permute-start(s32[128]{0:T(128)S(1)} %broadcast_add_fusion), channel_id=1, source_target_pairs={{0,12},{2,14},{4,16},{6,18},{8,20},{10,22},{12,24},{14,26},{16,28}... | collective-permute-start | bytes 1544 | tf_op jit(solution)/shard_map/ppermute | solution.py:24
  18.5 49.5 %collective-permute-start.3 = (s32[128]{0:T(128)S(1)}, s32[128]{0:T(128)S(1)}, u32[]{:S(2)}, u32[]{:S(2)}) collective-permute-start(s32[128]{0:T(128)S(1)} %broadcast_add_fusion), channel_id=1, source_target_pairs={{0,10},{2,12},{4,14},{6,16},{8,18},{10,20},{12,22},{14,24},{16,26}... | collective-permute-start | bytes 1544 | tf_op jit(solution)/shard_map/ppermute | solution.py:24
  20.4 47.6 %collective-permute-start.4 = (s32[128]{0:T(128)S(1)}, s32[128]{0:T(128)S(1)}, u32[]{:S(2)}, u32[]{:S(2)}) collective-permute-start(s32[128]{0:T(128)S(1)} %broadcast_add_fusion), channel_id=1, source_target_pairs={{0,8},{2,10},{4,12},{6,14},{8,16},{10,18},{12,20},{14,22},{16,24},... | collective-permute-start | bytes 1544 | tf_op jit(solution)/shard_map/ppermute | solution.py:24
  78.2 23.3 collective-permute-start.8
  80.9 26.1 collective-permute-start.9
  83.5 26.5 collective-permute-start.10
  85.4 27.3 collective-permute-start.11
  87.3 29.8 collective-permute-start.12
  101.5 25.7 collective-permute-start.13
  107.1 29.1 collective-permute-start.14
  109.9 30.9 collective-permute-start.15
  291.9 425.8 %all-gather.13.cloned.1.call-start = ((), (), s32[]{:S(2)}) async-start(), calls=%async_computation.9 | async-start | bytes 41779200 | tf_op jit(solution)/shard_map/all_gather | solution.py:116
  292.5 645.4 %all-gather.15.cloned.1.call-start = ((), (), s32[]{:S(2)}) async-start(), calls=%async_computation.10 | async-start | bytes 20889600 | tf_op jit(solution)/shard_map/all_gather | solution.py:117
  293.0 697.7 %all-reduce.9.cloned.1.call-start = ((), (), s32[]{:S(2)}) async-start(), calls=%async_computation.11 | async-start | bytes 1310720 | tf_op jit(solution)/shard_map/psum | solution.py:192
  970.4 107.0 %all-reduce.13.cloned.1.call-start = ((), (), s32[]{:S(2)}) async-start(), calls=%async_computation.18 | async-start | bytes 2883584 | tf_op jit(solution)/shard_map/psum | solution.py:179
  1020.7 17.5 collective-permute-start.21
  1024.7 24.9 collective-permute-start.20
  1026.6 22.9 collective-permute-start.19
  1028.6 21.0 collective-permute-start.18
  1030.5 19.9 collective-permute-start.17
  1057.5 183.0 %reduce-scatter.16.cloned.1.call-start = ((), (), s32[]{:S(2)}) async-start(), calls=%async_computation.16 | async-start | bytes 1392640
  1084.2 194.1 %reduce-scatter.10.cloned.1.call-start = ((), (), s32[]{:S(2)}) async-start(), calls=%async_computation.13 | async-start | bytes 5570560 | tf_op jit(solution)/shard_map/reduce_scatter | solution.py:256
  1087.5 470.1 %reduce-scatter.8.cloned.1.call-start = ((), (), s32[]{:S(2)}) async-start(), calls=%async_computation.12 | async-start | bytes 13926400 | tf_op jit(solution)/shard_map/reduce_scatter | solution.py:255
  1094.3 743.7 %reduce-scatter.12.cloned.1.call-start = ((), (), s32[]{:S(2)}) async-start(), calls=%async_computation.14 | async-start | bytes 13926400 | tf_op jit(solution)/shard_map/reduce_scatter | solution.py:257
  1102.5 1312.9 %reduce-scatter.14.cloned.1.call-start = ((), (), s32[]{:S(2)}) async-start(), calls=%async_computation.15 | async-start | bytes 41779200 | tf_op jit(solution)/shard_map/reduce_scatter | solution.py:190
  1119.1 3303.8 %all-reduce.11.cloned.1.call-start = ((), (), s32[]{:S(2)}) async-start(), calls=%async_computation.17 | async-start | bytes 157286400
  (41 other events, 5840.9 us)
Sparse Core Ops, SparseCore 0:
  10.7 64.7 all-gather.6
  78.2 109.9 all-gather.8
  190.9 94.9 all-gather.10
  292.0 19.0 all-reduce.6
  314.1 403.4 all-gather.12
  720.7 217.0 all-gather.14
  970.5 20.1 all-reduce.8
  1057.6 19.7 all-reduce.12
  1084.3 65.1 reduce-scatter.15
  1152.3 125.9 reduce-scatter.9
  1281.3 276.2 reduce-scatter.7
  1560.5 277.4 reduce-scatter.11
  1845.7 569.6 reduce-scatter.13
  2422.8 2000.0 all-reduce.10
where the time goes:
time: 4470 us; the launch traced here: 4450 us
  waiting for transfers between devices  3980 us (89%)
  matrix products  174 us (4%)
  local copies, waits for them, and re-layouts  122 us (3%)
  starting transfers between devices  68.9 us (2%)
  other arithmetic  57.6 us (1%)
    unnamed x16, waiting for transfers between devices  2000 us
    reduce_scatter x1, waiting for transfers between devices, shards(): lax.psum_scatter(down_grad, ('shard', 'dp'), scatter_dimension=1, tiled=T...  574 us
    all_gather x1, waiting for transfers between devices, shards(): lax.all_gather(gateup_weight, ('shard', 'dp'), axis=0, tiled=True)  405 us
    reduce_scatter x1, waiting for transfers between devices, shards(): lax.psum_scatter(outproj_grad, ('shard', 'dp'), scatter_dimension=1, tile...  277 us
    reduce_scatter x1, waiting for transfers between devices, shards(): lax.psum_scatter(query_grad, ('shard', 'dp'), scatter_dimension=0, tiled=...  277 us
    all_gather x1, waiting for transfers between devices, shards(): lax.all_gather(down_weight, ('shard', 'dp'), axis=1, tiled=True)  176 us
  transfers between devices with their start and end apart: 38, of which 24 were waited for; matrix products, arithmetic and copies ran while one was open for 6% of the time, Pallas kernels for 0%

commit v1 on v0

v1 whole, which is shorter than its diff:
```python
from functools import partial

import jax
import jax.numpy as jnp
from jax import lax
from jax.experimental import pallas as pl
from jax.experimental.pallas import tpu as pltpu
from jax.sharding import PartitionSpec as P

HEAD_DIM = 256
KV_BLOCKS = 8

EPS_NORM = 1e-06
BETA_ONE = 0.9
BETA_TWO = 0.95
ADAM_EPS = 1e-08
LEARN_RATE = 0.01
DECAY_RATE = 0.1
ROPE_BASE = 10000.0

MESH = pl.DeviceIdType.MESH
TOK = ("shard", "dp")
VMEM_LIMIT = 56 << 20
F32 = jnp.float32
BF16 = jnp.bfloat16


def when(cond, fn):
    if cond is True:
        fn()
    else:
        pl.when(cond)(fn)


def planes(s, ns, far_first=False):
    steps = [(s, 0, 0, True)]
    for t in range(1, ns):
        steps.append((s - t, t, 1, s - t >= 0))
        steps.append((s + t, t, -1, s + t < ns))
    return steps[::-1] if far_first else steps


def greet(ns, nd, use_z, use_plane, use_core, z_all=False):
    s, d, m = (lax.axis_index(a) for a in ("shard", "dp", "mp"))
    bar = pltpu.get_barrier_semaphore()

    def hello(dev):
        pl.semaphore_signal(bar, 1, device_id=dev, device_id_type=MESH)

    count = 0
    if use_z and z_all:
        for k in range(1, ns):
            hello({"shard": lax.rem(s + k, ns)})
        count += ns - 1
    elif use_z:
        when(s < ns - 1, lambda: hello({"shard": s + 1}))
        when(s > 0, lambda: hello({"shard": s - 1}))
        count = (s < ns - 1).astype(jnp.int32) + (s > 0).astype(jnp.int32)
    if use_plane:
        for k in range(1, nd):
            hello({"dp": lax.rem(d + k, nd)})
        count += nd - 1
    if use_core:
        hello({"mp": 1 - m})
        count += 1
    pl.semaphore_wait(bar, count)


def square(d):
    low = lax.rem(d, 2)
    x = d + 1 - 2 * low
    y = lax.rem(d + 2, 4)
    return x, y, lax.rem(x + 2, 4)


def gather_kernel(ns, nd, modes, *refs):
    n = len(modes)
    ins, outs, sems = refs[:n], refs[n : 2 * n], refs[2 * n :]
    s, d, m = (lax.axis_index(a) for a in ("shard", "dp", "mp"))
    use_z = any(k in ("z", "all") for k in modes)
    use_plane = any(k in ("plane", "all", "swap") for k in modes)
    greet(ns, nd, use_z, use_plane, "all" in modes)
    peers = [lax.rem(d + k, nd) for k in range(1, nd)]
    relay = [
        nd == 4 and modes[i] in ("all", "plane") and ins[i].shape[0] % 32 == 0 for i in range(n)]
    if nd == 4:
        x, y, across = square(d)

    def place(i, b, e, core):
        if modes[i] == "z":
            return outs[i].at[b]
        if modes[i] in ("plane", "swap"):
            return outs[i].at[e]
        return outs[i].at[b, e, core]

    def part(i, ref, k):
        if k is None:
            return ref
        rows = ins[i].shape[0] // 2
        return ref.at[pl.ds(k * rows, rows)]

    def zcopy(i, b, way, first):
        src = ins[i] if first else place(i, b, d, m)
        return pltpu.make_async_remote_copy(
            src, place(i, b, d, m), sems[7 * i].at[(way + 1) // 2, b], sems[7 * i + 1].at[b],
            device_id={"shard": s + way}, device_id_type=MESH)

    def pcopy(i, b, to, slot, first, e=None, k=None):
        e = d if e is None else e
        src = (ins[i].at[to] if modes[i] == "swap" else ins[i]) if first else place(i, b, e, m)
        return pltpu.make_async_remote_copy(
            part(i, src, k), part(i, place(i, b, e, m), k),
            sems[7 * i + 2].at[b, slot], sems[7 * i + 3].at[b, e, k or 0],
            device_id={"dp": to}, device_id_type=MESH)

    def precv(i, b, e, k=None):
        ref = place(i, b, e, m)
        return pltpu.make_async_remote_copy(
            part(i, ref, k), part(i, ref, k), sems[7 * i + 2].at[b, 0], sems[7 * i + 3].at[b, e, k or 0],
            device_id={"dp": peers[0]}, device_id_type=MESH)

    def own_copies(i, b, first):
        if relay[i]:
            return [pcopy(i, b, x, 0, first, k=0), pcopy(i, b, y, 1, first, k=1),
                    pcopy(i, b, x, 2, first, k=1), pcopy(i, b, y, 3, first, k=0)]
        return [pcopy(i, b, e, j, first) for j, e in enumerate(peers)]

    def pass_copies(i, b):
        return [(precv(i, b, x, 0), pcopy(i, b, y, 4, False, x, 0)),
                (precv(i, b, y, 1), pcopy(i, b, x, 5, False, y, 1))]

    def ccopy(i, b, e, first):
        src = ins[i] if first else place(i, b, e, m)
        return pltpu.make_async_remote_copy(
            src, place(i, b, e, m), sems[7 * i + 4].at[b, e], sems[7 * i + 5].at[b, e],
            device_id={"mp": 1 - m}, device_id_type=MESH)

    def crecv(i, b, e):
        ref = place(i, b, e, 1 - m)
        return pltpu.make_async_remote_copy(
            ref, ref, sems[7 * i + 4].at[b, e], sems[7 * i + 5].at[b, e],
            device_id={"mp": 1 - m}, device_id_type=MESH)

    def lcopy(i):
        src = ins[i].at[d] if modes[i] == "swap" else ins[i]
        return pltpu.make_async_copy(src, place(i, s, d, m), sems[7 * i + 6])

    def in_z(i):
        return modes[i] in ("z", "all")

    def in_plane(i, t):
        return modes[i] == "all" or (modes[i] in ("plane", "swap") and t == 0)

    def onward(i, b, t, way):
        first = t == 0
        if in_z(i):
            if way >= 0:
                when(s < ns - 1, lambda: zcopy(i, b, 1, first).start())
            if way <= 0:
                when(s > 0, lambda: zcopy(i, b, -1, first).start())
        if in_plane(i, t):
            for c in own_copies(i, b, first):
                c.start()
        if modes[i] == "all":
            ccopy(i, b, d, first).start()
        if first:
            lcopy(i).start()

    def arrive(i, b, t, way):
        zcopy(i, b, -way, False).wait_recv()
        onward(i, b, t, way)

    def pass_on(i, b):
        for got, on in pass_copies(i, b):
            got.wait_recv()
            on.start()

    def settle(i, b):
        if relay[i]:
            waits = [(x, [precv(i, b, x, 1)]), (y, [precv(i, b, y, 0)]),
                     (across, [precv(i, b, across, 0), precv(i, b, across, 1)])]
        else:
            waits = [(e, [precv(i, b, e)]) for e in peers]
        for e, got in waits:
            for w in got:
                w.wait_recv()
            if modes[i] == "all":
                ccopy(i, b, e, False).start()

    def finish(i, b, t, way):
        first = t == 0
        if in_z(i):
            if way >= 0:
                when(s < ns - 1, lambda: zcopy(i, b, 1, first).wait_send())
            if way <= 0:
                when(s > 0, lambda: zcopy(i, b, -1, first).wait_send())
        if in_plane(i, t):
            for c in own_copies(i, b, first):
                c.wait_send()
            if relay[i]:
                for _, on in pass_copies(i, b):
                    on.wait_send()
        if modes[i] == "all":
            for e in [d] + peers:
                crecv(i, b, e).wait_recv()
                ccopy(i, b, e, False).wait_send()
        if first:
            lcopy(i).wait()

    def each(steps, chosen, fn):
        for b, t, way, ok in steps:
            for i in range(n):
                if chosen(i, t):
                    when(ok, partial(fn, i, b, t, way))

    steps = planes(s, ns)
    levels = [[q for q in steps if q[1] == t] for t in range(ns)]
    each(levels[0], lambda i, t: True, onward)
    for t in range(1, ns + 1):
        if t < ns:
            each(levels[t], lambda i, t: in_z(i), arrive)
        each(levels[t - 1], lambda i, t: relay[i] and in_plane(i, t), lambda i, b, t, way: pass_on(i, b))
    each(steps, in_plane, lambda i, b, t, way: settle(i, b))
    each(steps, lambda i, t: t == 0 or in_z(i), finish)


def gather(collective, mesh_shape, items):
    ns, nd = mesh_shape["shard"], mesh_shape["dp"]
    modes = tuple(mode for _, mode in items)
    lead = {"z": (ns,), "plane": (nd,), "all": (ns, nd, 2), "swap": ()}
    shapes = [jax.ShapeDtypeStruct(lead[mode] + a.shape, a.dtype) for a, mode in items]
    sems = []
    dma = pltpu.SemaphoreType.DMA
    for _ in items:
        sems += [dma((2, ns)), dma((ns,)), dma((ns, max(nd, 6))), dma((ns, nd, 2)), dma((ns, nd)), dma((ns, nd)),
                 dma(())]
    return pl.pallas_call(
        partial(gather_kernel, ns, nd, modes),
        out_shape=shapes,
        in_specs=[pl.BlockSpec(memory_space=pl.ANY)] * len(items),
        out_specs=[pl.BlockSpec(memory_space=pl.ANY)] * len(items),
        scratch_shapes=sems,
        compiler_params=pltpu.CompilerParams(
            collective_id=collective, has_side_effects=True, vmem_limit_bytes=VMEM_LIMIT),
        cost_estimate=pl.CostEstimate(flops=0, bytes_accessed=1 << 20, transcendentals=0),
    )(*[a for a, _ in items])


def reduce_kernel(ns, nd, share, p, out, own, sib, got, mid, zgot, fin,
                  lsem, ss, sr, ps, pr, zs, zr, fs, fr, ls2):
    s, d, m = (lax.axis_index(a) for a in ("shard", "dp", "mp"))
    h, c = fin.shape
    tile = 16
    greet(ns, nd, True, True, True, z_all=True)
    peers = [lax.rem(d + k, nd) for k in range(1, nd)]
    relay = nd == 4 and h % 32 == 0
    if relay:
        x, y, across = square(d)
        peers = [across, x, y]
    order = [lax.rem(s + k, ns) for k in sorted(range(1, ns), key=lambda k: abs(k - ns // 2))] + [s]

    def score(b):
        return pltpu.make_async_remote_copy(
            p.at[b, :, 1 - m], sib.at[b], ss.at[b], sr.at[b], device_id={"mp": 1 - m}, device_id_type=MESH)

    def load(b):
        return pltpu.make_async_copy(p.at[b, :, m], own.at[b], lsem.at[b])

    def pcopy(b, src, slot, to):
        return pltpu.make_async_remote_copy(
            src, slot[0], ps.at[b, slot[1]], pr.at[b, slot[1]], device_id={"dp": to}, device_id_type=MESH)

    def sends(b):
        if not relay:
            return [pltpu.make_async_remote_copy(
                own.at[b, e], got.at[b, d], ps.at[b, e], pr.at[b, d], device_id={"dp": e}, device_id_type=MESH)
                for e in peers]
        half = h // 2
        first, last = pl.ds(0, half), pl.ds(half, half)
        return [
            pcopy(b, own.at[b, across, first], (got.at[b, 0, first], 0), x),
            pcopy(b, own.at[b, across, last], (got.at[b, 0, last], 1), y),
            pcopy(b, own.at[b, x], (got.at[b, 1], 2), x),
            pcopy(b, own.at[b, y], (got.at[b, 2], 3), y),
        ]

    def zcopy(b, to):
        return pltpu.make_async_remote_copy(
            mid.at[b], zgot.at[to], zs.at[b], zr.at[to], device_id={"shard": b}, device_id_type=MESH)

    def rows(r):
        return pl.ds(pl.multiple_of(r * tile, tile), tile)

    def sum_rows(lo, hi, terms, store):
        @pl.loop(lo // tile, hi // tile)
        def _(r):
            at = rows(r)
            v = terms[0](at).astype(F32)
            for f in terms[1:]:
                v = v + f(at).astype(F32)
            store(at, v)

    def to_own(b, e):
        def store(at, v):
            own[b, e, at] = v.astype(BF16)
        return store

    def one(b):
        score(b).wait_recv()
        load(b).wait()
        out_now = sends(b)
        for j, e in enumerate(peers + [d]):
            sum_rows(0, h, [lambda at, e=e: own[b, e, at], lambda at, e=e: sib[b, e, at]], to_own(b, e))
            if relay and j == 0:
                out_now[0].start()
                out_now[1].start()
            elif not relay and j < len(peers):
                out_now[j].start()

    def two(b):
        if not relay:
            return
        half = h // 2
        c0, c1, c2, c3 = sends(b)
        c0.wait_recv()
        sum_rows(0, half, [lambda at: own[b, y, at], lambda at: got[b, 0, at]], to_own(b, y))
        c3.start()
        c1.wait_recv()
        sum_rows(half, h, [lambda at: own[b, x, at], lambda at: got[b, 0, at]], to_own(b, x))
        c2.start()

    def plane_terms(b):
        slots = [1, 2] if relay else peers
        return [lambda at: own[b, d, at]] + [lambda at, e=e: got[b, e, at] for e in slots]

    def three(b, last):
        if relay:
            for w in sends(b)[2:]:
                w.wait_recv()
        else:
            for e in peers:
                pltpu.make_async_remote_copy(
                    own.at[b, e], got.at[b, e], ps.at[b, e], pr.at[b, e],
                    device_id={"dp": e}, device_id_type=MESH).wait_recv()
        if not last:
            def store(at, v):
                mid[b, at] = v.astype(BF16)
            sum_rows(0, h, plane_terms(b), store)
            zcopy(b, s).start()

    for b in order:
        score(b).start()
        load(b).start()
    for k in range(ns + 2):
        if k < ns:
            one(order[k])
        if 0 <= k - 1 < ns:
            two(order[k - 1])
        if 0 <= k - 2 < ns:
            three(order[k - 2], k - 2 == ns - 1)
    others = order[:-1]
    for b in others:
        zcopy(b, b).wait_recv()

    def store(at, v):
        fin[at] = v.astype(fin.dtype)

    sum_rows(0, h, plane_terms(s) + [lambda at, b=b: zgot[b, at] for b in others], store)
    if share:
        give = pltpu.make_async_remote_copy(
            fin, out.at[m], fs, fr, device_id={"mp": 1 - m}, device_id_type=MESH)
        take = pltpu.make_async_remote_copy(
            fin, out.at[1 - m], fs, fr, device_id={"mp": 1 - m}, device_id_type=MESH)
        give.start()
        keep = pltpu.make_async_copy(fin, out.at[m], ls2)
        keep.start()
        take.wait_recv()
        give.wait_send()
        keep.wait()
    else:
        keep = pltpu.make_async_copy(fin, out, ls2)
        keep.start()
        keep.wait()
    for b in order:
        score(b).wait_send()
        for w in sends(b):
            w.wait_send()
    for b in others:
        zcopy(b, s).wait_send()


def reduce_scatter(collective, mesh_shape, p, share):
    ns, nd = mesh_shape["shard"], mesh_shape["dp"]
    h, c = p.shape[3:]
    if 3 * (p.size // 2) * 2 > (40 << 20):
        total = lax.psum_scatter(p.reshape(ns * nd, 2, h, c), TOK, scatter_dimension=0, tiled=True)[0]
        total = lax.psum(total, "mp")
        return total if share else lax.dynamic_index_in_dim(total, lax.axis_index("mp"), 0, False)
    dma = pltpu.SemaphoreType.DMA
    return pl.pallas_call(
        partial(reduce_kernel, ns, nd, share),
        out_shape=jax.ShapeDtypeStruct((2, h, c) if share else (h, c), BF16),
        in_specs=[pl.BlockSpec(memory_space=pl.ANY)],
        out_specs=pl.BlockSpec(memory_space=pl.ANY),
        scratch_shapes=[
            pltpu.VMEM((ns, nd, h, c), BF16),
            pltpu.VMEM((ns, nd, h, c), BF16),
            pltpu.VMEM((ns, nd, h, c), BF16),
            pltpu.VMEM((ns, h, c), BF16),
            pltpu.VMEM((ns, h, c), BF16),
            pltpu.VMEM((h, c), BF16),
            dma((ns,)), dma((ns,)), dma((ns,)),
            dma((ns, nd)), dma((ns, nd)),
            dma((ns,)), dma((ns,)), dma(()), dma(()), dma(()),
        ],
        compiler_params=pltpu.CompilerParams(
            collective_id=collective, has_side_effects=True, vmem_limit_bytes=VMEM_LIMIT),
        cost_estimate=pl.CostEstimate(flops=0, bytes_accessed=1 << 20, transcendentals=0),
    )(p)


def rope_tables(positions):
    half_dim = HEAD_DIM // 2
    exponent = jnp.arange(half_dim, dtype=F32) * (-2.0 / HEAD_DIM)
    angles = positions.astype(F32)[:, None] * jnp.power(ROPE_BASE, exponent)[None, :]
    return (jnp.cos(angles), jnp.sin(angles))


def rotate(values, cosine, sine_rows):
    half_dim = values.shape[-1] // 2
    front_half = values[..., :half_dim]
    back_half = values[..., half_dim:]
    return jnp.concatenate(
        [front_half * cosine - back_half * sine_rows, back_half * cosine + front_half * sine_rows], axis=-1)


def rows_product(left_side, right_side):
    return lax.dot_general(
        left_side, right_side, (((0,), (0,)), ((), ())), preferred_element_type=F32)


def cols_product(left_side, right_side):
    return lax.dot_general(
        left_side, right_side, (((1,), (1,)), ((), ())), preferred_element_type=F32)


def product(left_side, right_side):
    return jnp.dot(left_side, right_side, preferred_element_type=F32)


def adam_update(grad_own, weight, first_old, second_old, bias_first, bias_second, decay):
    first_new = BETA_ONE * first_old + (1.0 - BETA_ONE) * grad_own
    second_new = BETA_TWO * second_old + (1.0 - BETA_TWO) * grad_own * grad_own
    direction = first_new / bias_first / (jnp.sqrt(second_new / bias_second) + ADAM_EPS)
    return (first_new, second_new, -LEARN_RATE * (direction + decay * weight.astype(F32)))


def swap_add(value):
    other = lax.ppermute(value, "mp", [(0, 1), (1, 0)])
    return value.astype(F32) + other.astype(F32)


def shards(
    mesh_shape,
    tokens_in,
    segment_ids,
    block_cotangent,
    query_weight,
    keyval_weight,
    outproj_weight,
    gateup_weight,
    down_weight,
    norm_gains,
    query_first,
    keyval_first,
    outproj_first,
    gateup_first,
    down_first,
    gains_first,
    query_second,
    keyval_second,
    outproj_second,
    gateup_second,
    down_second,
    gains_second,
    step_count,
):
    ns, nd = mesh_shape["shard"], mesh_shape["dp"]
    n = ns * nd
    s, d, m = (lax.axis_index(a) for a in ("shard", "dp", "mp"))
    me = s * nd + d
    tok, width = tokens_in.shape
    own_d = query_weight.shape[0]
    q_cols = query_weight.shape[1]
    heads_local = q_cols // HEAD_DIM
    ff_local = gateup_weight.shape[2]
    units = -(-(-(-ff_local // n)) // 128) * 128
    ff_pad = units * n - ff_local
    half = tok // 2
    plane_tok = nd * tok
    plane_d = ns * own_d

    gateup_cut = jnp.pad(gateup_weight, ((0, 0), (0, 0), (0, ff_pad)))
    gateup_cut = gateup_cut.reshape(own_d, 2, n, units).transpose(2, 0, 1, 3).reshape(n, own_d, 2 * units)
    down_cut = jnp.pad(down_weight, ((0, ff_pad), (0, 0))).reshape(n, units, own_d)
    gateup_mine = lax.all_to_all(gateup_cut, TOK, 0, 0, tiled=True).reshape(width, 2 * units)
    down_mine = lax.all_to_all(down_cut, TOK, 0, 0, tiled=True)
    down_mine = down_mine.transpose(1, 0, 2).reshape(units, width)

    input_rows = tokens_in.astype(F32)
    inverse_one = lax.rsqrt(jnp.mean(input_rows * input_rows, axis=1) + EPS_NORM)
    lanes = max(256, -(-max(own_d, tok) // 128) * 128)

    def line(v):
        return jnp.pad(v, ((0, 0), (0, lanes - v.shape[1])))

    small = jnp.concatenate(
        [line(norm_gains.astype(F32)), line(segment_ids.astype(F32)[None]), line(inverse_one[None]),
         jnp.zeros((4, lanes), F32)], axis=0)
    qkv_weight = jnp.concatenate(
        [query_weight, lax.dynamic_slice_in_dim(keyval_weight, m * HEAD_DIM, HEAD_DIM, 1)], axis=1)

    def plane_cut(value):
        return value.reshape(tok, ns, nd, own_d).transpose(2, 0, 1, 3).reshape(nd, tok, plane_d)

    tokens_plane, qkv_plane, small_all, cot_all = gather(
        0, mesh_shape,
        [(plane_cut(tokens_in), "swap"), (qkv_weight, "z"), (small, "all"),
         (lax.dynamic_slice_in_dim(block_cotangent, m * half, half, 0), "all")])
    tokens_plane = tokens_plane.reshape(plane_tok, plane_d)
    qkv_plane = qkv_plane.reshape(plane_d, q_cols + HEAD_DIM)
    cot_all = cot_all.reshape(n * tok, width)
    small_all = small_all[:, :, 0]
    gains_by = small_all[:, :, :2, :own_d]
    full_gains = gains_by.transpose(2, 0, 1, 3).reshape(2, width)
    tags = small_all[:, :, 2, :tok].reshape(n * tok)
    plane_scale = lax.dynamic_index_in_dim(small_all[:, :, 3, :tok], s, 0, False).reshape(plane_tok, 1)
    plane_gain = lax.dynamic_index_in_dim(gains_by[:, :, 0], d, 1, False).reshape(1, plane_d)

    def to_plane(value):
        return lax.all_to_all(plane_cut(value), "dp", 0, 0, tiled=True).reshape(plane_tok, plane_d)

    def from_plane(value):
        got = lax.all_to_all(value.reshape(nd, tok, plane_d), "dp", 0, 0, tiled=True)
        return got.reshape(nd, tok, ns, own_d).transpose(1, 2, 0, 3).reshape(tok, width)

    def plane_sum(value):
        got = lax.all_to_all(value.reshape(nd, tok, -1), "dp", 0, 0, tiled=True)
        return jnp.sum(got.astype(F32), axis=0)

    hidden_plane = (tokens_plane.astype(F32) * plane_scale * plane_gain).astype(BF16)
    qkv_raw = plane_sum(product(hidden_plane, qkv_plane).astype(BF16))

    pad = KV_BLOCKS * tok
    key_span = pad + tok
    start = me * tok
    tag_pad = jnp.concatenate([jnp.full((pad,), -1.0, F32), tags])
    key_tags = lax.dynamic_slice_in_dim(tag_pad, start, key_span, 0)
    own_tags = segment_ids.astype(F32)
    query_index = jnp.arange(tok, dtype=jnp.int32) + pad
    key_index = jnp.arange(key_span, dtype=jnp.int32)
    same_segment = key_tags[None, :] == own_tags[:, None]
    allowed = same_segment & (key_index[None, :] <= query_index[:, None])
    positions = jnp.sum(
        (same_segment & (key_index[None, :] < query_index[:, None])).astype(jnp.int32), axis=1)
    cosine, sine_rows = rope_tables(positions)
    cos_h, sin_h = cosine[:, None, :], sine_rows[:, None, :]
    score_scale = HEAD_DIM ** (-0.5)
    queries = rotate(qkv_raw[:, :q_cols].reshape(tok, heads_local, HEAD_DIM), cos_h, sin_h).astype(BF16)
    kv_raw = qkv_raw[:, q_cols:]
    kv_mine = jnp.where(m == 0, rotate(kv_raw, cosine, sine_rows), kv_raw).astype(BF16)
    (kv_all,) = gather(1, mesh_shape, [(kv_mine, "all")])
    kv_all = kv_all.reshape(n, 2, tok, HEAD_DIM)
    kv_pad = jnp.concatenate([jnp.zeros((KV_BLOCKS, 2, tok, HEAD_DIM), BF16), kv_all], axis=0)
    kv_window = lax.dynamic_slice_in_dim(kv_pad, me, KV_BLOCKS + 1, 0)
    key_rows = kv_window[:, 0].reshape(key_span, HEAD_DIM)
    value_rows = kv_window[:, 1].reshape(key_span, HEAD_DIM)
    scores = jnp.einsum("thd,kd->htk", queries, key_rows, preferred_element_type=F32) * score_scale
    scores = jnp.where(allowed[None], scores, -jnp.inf)
    row_max = jnp.max(scores, axis=2, keepdims=True)
    raw = jnp.exp(scores - row_max)
    probs = raw / jnp.sum(raw, axis=2, keepdims=True)
    probs_low = probs.astype(BF16)
    mixed = jnp.einsum("htk,kd->thd", probs_low, value_rows, preferred_element_type=F32)
    mixed_low = mixed.reshape(tok, q_cols).astype(BF16)
    mixed_plane, outproj_z = gather(
        2, mesh_shape, [(mixed_low, "plane"), (outproj_weight, "z")])
    mixed_plane = mixed_plane.reshape(plane_tok, q_cols)
    outproj_plane = outproj_z.transpose(1, 0, 2).reshape(q_cols, plane_d)
    attn_part = from_plane(product(mixed_plane, outproj_plane).astype(BF16))
    residual = input_rows + swap_add(attn_part)
    gain_two = full_gains[1]
    inverse_two = lax.rsqrt(jnp.mean(residual * residual, axis=1, keepdims=True) + EPS_NORM)
    hidden_two = (residual * inverse_two * gain_two).astype(BF16)
    (hidden_all,) = gather(
        3, mesh_shape, [(lax.dynamic_slice_in_dim(hidden_two, m * half, half, 0), "all")])
    hidden_all = hidden_all.reshape(n * tok, width)

    gateup_pre = product(hidden_all, gateup_mine)
    gate_pre, up_pre = gateup_pre[:, :units], gateup_pre[:, units:]
    gelu_val, gelu_pull = jax.vjp(partial(jax.nn.gelu, approximate=True), gate_pre)
    act_low = (gelu_val * up_pre).astype(BF16)
    act_grad = cols_product(cot_all, down_mine)
    gateup_low = jnp.concatenate(
        [gelu_pull(act_grad * up_pre)[0], act_grad * gelu_val], axis=1).astype(BF16)
    hidden_two_part = cols_product(gateup_low, gateup_mine).astype(BF16)
    hidden_two_grad = reduce_scatter(
        4, mesh_shape, hidden_two_part.reshape(ns, nd, 2, half, width), True).reshape(tok, width).astype(F32)
    gateup_grad = rows_product(hidden_all, gateup_low).astype(BF16).reshape(n, own_d, 2 * units)
    down_grad = rows_product(act_low, cot_all).astype(BF16)
    down_grad = down_grad.reshape(units, n, own_d).transpose(1, 0, 2)
    own_gateup = lax.all_to_all(gateup_grad, TOK, 0, 0, tiled=True).reshape(n, own_d, 2, units)
    own_gateup = own_gateup.transpose(1, 2, 0, 3).reshape(own_d, 2, n * units)[:, :, :ff_local].astype(F32)
    own_down = lax.all_to_all(down_grad, TOK, 0, 0, tiled=True).reshape(n * units, own_d)[:ff_local].astype(F32)
    ffn_part = product(act_low, down_mine).astype(BF16)
    ffn_sum = reduce_scatter(
        5, mesh_shape, ffn_part.reshape(ns, nd, 2, half, width), True).reshape(tok, width).astype(F32)
    block_out = (residual + ffn_sum).astype(BF16)

    def norm_back(rows, inverse, gain_row, grad):
        normed = rows * inverse
        scaled = grad * gain_row
        inner = jnp.mean(normed * scaled, axis=1, keepdims=True)
        return inverse * (scaled - normed * inner), jnp.sum(grad * normed, axis=0)

    residual_from, gain_two_grad = norm_back(residual, inverse_two, gain_two, hidden_two_grad)
    residual_grad = block_cotangent.astype(F32) + residual_from
    attn_low = to_plane(residual_grad.astype(BF16))
    mixed_grad = plane_sum(cols_product(attn_low, outproj_plane).astype(BF16))
    mixed_grad = mixed_grad.astype(BF16).reshape(tok, heads_local, HEAD_DIM)

    def z_sum(value):
        got = lax.all_to_all(value, "shard", 0, 0, tiled=True)
        return jnp.sum(got.astype(F32), axis=0)

    outproj_grad = rows_product(mixed_plane, attn_low).astype(BF16)
    own_outproj = z_sum(outproj_grad.reshape(q_cols, ns, own_d).transpose(1, 0, 2))

    probs_grad = jnp.einsum("thd,kd->htk", mixed_grad, value_rows, preferred_element_type=F32)
    value_grad = jnp.einsum("htk,thd->kd", probs_low, mixed_grad, preferred_element_type=F32)
    inner_sum = jnp.sum(probs * probs_grad, axis=2, keepdims=True)
    scores_low = (probs * (probs_grad - inner_sum) * score_scale).astype(BF16)
    query_rot_grad = jnp.einsum("htk,kd->thd", scores_low, key_rows, preferred_element_type=F32)
    key_rot_grad = jnp.einsum("htk,thd->kd", scores_low, queries, preferred_element_type=F32)
    window_grad = jnp.stack(
        [key_rot_grad.reshape(KV_BLOCKS + 1, tok, HEAD_DIM), value_grad.reshape(KV_BLOCKS + 1, tok, HEAD_DIM)],
        axis=1).astype(BF16)
    kv_grad_pad = lax.dynamic_update_slice_in_dim(
        jnp.zeros((KV_BLOCKS + n, 2, tok, HEAD_DIM), BF16), window_grad, me, 0)
    kv_grad = reduce_scatter(
        6, mesh_shape, kv_grad_pad[KV_BLOCKS:].reshape(ns, nd, 2, tok, HEAD_DIM), False).astype(F32)
    kv_low = jnp.where(m == 0, rotate(kv_grad, cosine, -sine_rows), kv_grad)
    query_low = rotate(query_rot_grad, cos_h, -sin_h).reshape(tok, q_cols)
    qkv_low = jnp.concatenate([query_low, kv_low], axis=1).astype(BF16)
    (qkv_low_plane,) = gather(7, mesh_shape, [(qkv_low, "plane")])
    qkv_low_plane = qkv_low_plane.reshape(plane_tok, q_cols + HEAD_DIM)
    hidden_part = from_plane(cols_product(qkv_low_plane, qkv_plane).astype(BF16))
    hidden_one_grad = swap_add(hidden_part)
    qkv_grad = rows_product(hidden_plane, qkv_low_plane).astype(BF16)
    own_qkv = z_sum(qkv_grad.reshape(ns, own_d, q_cols + HEAD_DIM))
    own_query = own_qkv[:, :q_cols]
    kv_own = own_qkv[:, q_cols:]
    kv_other = lax.ppermute(kv_own, "mp", [(0, 1), (1, 0)])
    own_keyval = jnp.where(
        m == 0, jnp.concatenate([kv_own, kv_other], axis=1), jnp.concatenate([kv_other, kv_own], axis=1))

    inverse_col = inverse_one[:, None]
    input_from, gain_one_grad = norm_back(input_rows, inverse_col, full_gains[0], hidden_one_grad)
    input_grad = residual_grad + input_from
    gains_cut = jnp.stack([gain_one_grad, gain_two_grad], axis=0).reshape(2, n, own_d).transpose(1, 0, 2)
    own_gains = jnp.sum(lax.all_to_all(gains_cut, TOK, 0, 0, tiled=True), axis=0)

    step_value = step_count[0].astype(F32)
    bias_first = 1.0 - jnp.power(BETA_ONE, step_value)
    bias_second = 1.0 - jnp.power(BETA_TWO, step_value)
    grads = (own_query, own_keyval, own_outproj, own_gateup, own_down, own_gains)
    weights = (query_weight, keyval_weight, outproj_weight, gateup_weight, down_weight, norm_gains)
    firsts = (query_first, keyval_first, outproj_first, gateup_first, down_first, gains_first)
    seconds = (query_second, keyval_second, outproj_second, gateup_second, down_second, gains_second)
    decays = (DECAY_RATE,) * 5 + (0.0,)
    news = [
        adam_update(g, w, a, b, bias_first, bias_second, c)
        for g, w, a, b, c in zip(grads, weights, firsts, seconds, decays)
    ]
    return (
        (block_out, input_grad)
        + grads
        + tuple(x[0] for x in news)
        + tuple(x[1] for x in news)
        + tuple(x[2] for x in news)
    )


def solution(mesh):
    rows, split_q, split_o = P(TOK, None), P(TOK, "mp"), P("mp", TOK)
    params = (split_q, rows, split_o, P(TOK, None, "mp"), split_o, P(None, TOK))
    in_specs = (rows, P(TOK), rows) + params * 3 + (P(),)
    out_specs = (rows, rows) + params * 4
    return jax.shard_map(
        partial(shards, dict(mesh.shape)), mesh=mesh, in_specs=in_specs, out_specs=out_specs, check_vma=False)
```

time: 4470 us -> 867 us (0.19)
  waiting for transfers between devices: 3980 us -> 171 us
  Pallas kernels: 0 us -> 374 us
  matrix products: 174 us -> 103 us
  local copies, waits for them, and re-layouts: 122 us -> 54.5 us
    unnamed x16 -> x0, waiting for transfers between devices: 2000 us -> none
    reduce_scatter x4 -> x0, waiting for transfers between devices: 1160 us -> none  [the longest x1 574 us: shards(): lax.psum_scatter(down_grad, ('shard', 'dp'), scatter_dimension=1, tiled=T...]
    all_gather x5 -> x0, waiting for transfers between devices: 720 us -> none  [the longest x1 405 us: shards(): lax.all_gather(gateup_weight, ('shard', 'dp'), axis=0, tiled=True)]
    pallas_call x0 -> x8, Pallas kernels: none -> 374 us  [the longest x5 231 us: gather(): pl.pallas_call(partial(gather_kernel, ns, nd, modes), out_shape=shapes, i...]
    all_to_all x0 -> x11, waiting for transfers between devices: none -> 169 us  [the longest x1 52.7 us: shards(): lax.all_to_all(gateup_cut, TOK, 0, 0, tiled=True).reshape(width, 2 * units)]
    all_to_all x0 -> x11, starting transfers between devices: none -> 68.6 us  [the longest x2 13.5 us: z_sum(): got = lax.all_to_all(value, 'shard', 0, 0, tiled=True)]
    ppermute x24 -> x3, starting transfers between devices: 67.2 us -> 0.29 us  [the longest x1 0.15 us: shards(): kv_other = lax.ppermute(kv_own, 'mp', [(0, 1), (1, 0)])]
    reshape x3 -> x12, local copies, waits for them, and re-layouts: 86.3 us -> 24.3 us  [the longest x2 7.86 us: shards(): lax.all_to_all(gateup_grad, TOK, 0, 0, tiled=True)]
  transfers between devices with their start and end apart: 38 -> 14, of which waited for: 24 -> 8; matrix products, arithmetic and copies ran while one was open for 6% -> 11% of each run, Pallas kernels for 0% -> 15%
where the time goes in v1:
time: 867 us; the launch traced here: 856 us
  Pallas kernels  374 us (43%)
  waiting for transfers between devices  171 us (20%)
  matrix products  103 us (12%)
  other arithmetic  69.9 us (8%)
  starting transfers between devices  68.9 us (8%)
  local copies, waits for them, and re-layouts  54.5 us (6%)
  blocking collectives  12.8 us (1%)
    pallas_call x5, Pallas kernels, gather(): pl.pallas_call(partial(gather_kernel, ns, nd, modes), out_shape=shapes, i...  231 us
    pallas_call x3, Pallas kernels, reduce_scatter(): pl.pallas_call(partial(reduce_kernel, ns, nd, share), out_shape=jax.Shape...  143 us
    all_to_all x1, waiting for transfers between devices, shards(): lax.all_to_all(gateup_cut, TOK, 0, 0, tiled=True).reshape(width, 2 * units)  52.7 us
    all_to_all x1, waiting for transfers between devices, shards(): lax.all_to_all(gateup_grad, TOK, 0, 0, tiled=True)  39 us
    mul x6, other arithmetic, adam_update(): -LEARN_RATE * (direction + decay * weight.astype(F32))  33.2 us
    all_to_all x2, waiting for transfers between devices, z_sum(): got = lax.all_to_all(value, 'shard', 0, 0, tiled=True)  28.5 us
    dot_general x4, matrix products, cols_product(): lax.dot_general(left_side, right_side, (((1,), (1,)), ((), ())), preferre...  28.4 us
    dot_general x4, matrix products, rows_product(): lax.dot_general(left_side, right_side, (((0,), (0,)), ((), ())), preferre...  27.4 us
  transfers between devices with their start and end apart: 14, of which 8 were waited for; matrix products, arithmetic and copies ran while one was open for 11% of the time, Pallas kernels for 15%

profile of v1, /device:TPU:14, one launch (start us, length us, event | category | flops | bytes accessed | tf_op | source)
XLA Modules:
  0.0 856.5 jit_solution(7750710299487845729)
XLA Ops:
  8.9 62.2 %shard_map.413 = (bf16[4,128,640]{2,1,0:T(8,128)(2,1)}, bf16[4,160,1536]{2,1,0:T(8,128)(2,1)}, f32[4,4,2,8,256]{4,3,2,1,0:T(8,128)}, bf16[4,4,2,64,2560]{4,3,2,1,0:T(8,128)(2,1)}) custom-call(bf16[4,128,640]{2,1,0:T(8,128)(2,1)} %copy.142.refs_0_, bf16[160,1536]{1,0:T(8,128)(2,1)} %pad_maximum_fusion.4.refs_1_, f32[8,256]{1,0:T(8,128)} %fusion.75.refs_2_, ...), custom_call_target="tpu_custom_call" | custom-call | bytes 1048576 | tf_op jit(solution)/shard_map/pallas_call | solution.py:237
  85.6 15.9 %all-to-all-done = bf16[4,128,1536]{2,1,0:T(8,128)(2,1)S(1)} async-done(((bf16[4,128,1536]{2,1,0:T(8,128)(2,1)}), bf16[4,128,1536]{2,1,0:T(8,128)(2,1)S(1)}, u32[]{:S(2)}, u32[]{:S(2)}) %all-to-all-start) | async-done | bytes 1572896 | tf_op jit(solution)/shard_map/all_to_all | solution.py:548
  103.4 32.1 %shard_map.414 = bf16[4,4,2,128,256]{4,3,2,1,0:T(8,128)(2,1)} custom-call(bf16[128,256]{1,0:T(8,128)(2,1)} %fusion.62.refs_0_), custom_call_target="tpu_custom_call" | custom-call | bytes 1048576 | tf_op jit(solution)/shard_map/pallas_call | solution.py:237
  140.3 52.3 %shard_map.415 = (bf16[4,128,1280]{2,1,0:T(8,128)(2,1)}, bf16[4,1280,160]{2,1,0:T(8,128)(2,1)}) custom-call(bf16[128,1280]{1,0:T(8,128)(2,1)} %copy.149.refs_0_, bf16[1280,160]{1,0:T(8,128)(2,1)} %copy.150.refs_1_), custom_call_target="tpu_custom_call" | custom-call | bytes 1048576 | tf_op jit(solution)/shard_map/pallas_call | solution.py:237
  200.2 5.2 all-to-all-start.1
  214.1 7.7 all-to-all-start.2
  226.5 52.7 %all-to-all-done.2 = bf16[16,160,512]{2,1,0:T(8,128)(2,1)} async-done(((bf16[16,160,512]{2,1,0:T(8,128)(2,1)}), bf16[16,160,512]{2,1,0:T(8,128)(2,1)}, u32[]{:S(2)}, u32[]{:S(2)}) %all-to-all-start.2) | async-done | bytes 2621472 | tf_op jit(solution)/shard_map/all_to_all | solution.py:506
  285.2 67.4 %shard_map.416 = bf16[4,4,2,64,2560]{4,3,2,1,0:T(8,128)(2,1)} custom-call(bf16[64,2560]{1,0:T(8,128)(2,1)} %fusion.59.refs_0_), custom_call_target="tpu_custom_call" | custom-call | bytes 1048576 | tf_op jit(solution)/shard_map/pallas_call | solution.py:237
  352.6 11.0 %fusion.103 = f32[2048,512]{0,1:T(8,128)} fusion(bf16[2048,2560]{1,0:T(8,128)(2,1)} %bitcast.202, bf16[2560,512]{1,0:T(8,128)(2,1)} %bitcast.30), kind=kOutput, calls=%fused_computation.192 | convolution fusion | flops 5368709120 | bytes 17301504 | tf_op jit(solution)/shard_map/dot_general | solution.py:448
  363.6 10.9 %fusion.22 = (bf16[2048,256]{0,1:T(8,128)(2,1)S(1)}, bf16[2048,256]{0,1:T(8,128)(2,1)S(1)}, bf16[2048,256]{0,1:T(8,128)(2,1)}) fusion(f32[2048,512]{0,1:T(8,128)} %fusion.103, bf16[2048,2560]{1,0:T(8,128)(2,1)} %bitcast.247, bf16[256,2560]{0,1:T(8,128)(2,1)} %bitcast.32), kind=kOutput, calls=%fused_computation.54 | convolution fusion | flops 2697986048 | bytes 19136512 | tf_op jit(solution)/shard_map/dot_general | solution.py:443
  374.5 10.8 %convolution_convert_fusion = bf16[2048,2560]{1,0:T(8,128)(2,1)} fusion(bf16[2560,512]{1,0:T(8,128)(2,1)} %bitcast.30, bf16[2048,256]{0,1:T(8,128)(2,1)S(1)} %get-tuple-element.66, bf16[2048,256]{0,1:T(8,128)(2,1)S(1)} %get-tuple-element.65), kind=kOutput, calls=%fused_computation.1 | convolution fusion | flops 5378146304 | bytes 15204352 | tf_op jit(solution)/shard_map/dot_general | solution.py:443
  385.3 59.3 %shard_map.418 = bf16[2,64,2560]{2,1,0:T(8,128)(2,1)} custom-call(bf16[4,4,2,64,2560]{4,3,2,1,0:T(8,128)(2,1)} %bitcast.204), custom_call_target="tpu_custom_call" | custom-call | bytes 1048576 | tf_op jit(solution)/shard_map/pallas_call | solution.py:400
  450.5 12.8 %all_to_all.60 = bf16[4,128,640]{1,2,0:T(8,128)(2,1)S(1)} all-to-all(bf16[4,128,640]{1,2,0:T(8,128)(2,1)S(1)} %bitcast.225), channel_id=1, replica_groups=mesh['shard'=4,'dp'=4,'mp'=2] {'dp'}, dimensions={0} | all-to-all | bytes 1310720 | tf_op jit(solution)/shard_map/all_to_all | solution.py:541
  468.2 6.4 all-to-all-start.5
  478.5 10.7 %all-to-all-done.5 = bf16[4,128,1280]{2,1,0:T(8,128)(2,1)} async-done(((bf16[4,128,1280]{2,1,0:T(8,128)(2,1)}), bf16[4,128,1280]{2,1,0:T(8,128)(2,1)}, u32[]{:S(2)}, u32[]{:S(2)}) %all-to-all-start.5) | async-done | bytes 1310752 | tf_op jit(solution)/shard_map/all_to_all | solution.py:548
  494.9 7.6 fusion.49
  502.6 7.2 fusion.12
  517.2 19.1 %shard_map.419 = bf16[128,256]{1,0:T(8,128)(2,1)} custom-call(bf16[4,4,2,128,256]{4,3,2,1,0:T(8,128)(2,1)} %bitcast.210), custom_call_target="tpu_custom_call" | custom-call | bytes 1048576 | tf_op jit(solution)/shard_map/pallas_call | solution.py:400
  539.1 16.8 %shard_map.420 = bf16[4,128,1536]{2,1,0:T(8,128)(2,1)} custom-call(bf16[128,1536]{1,0:T(8,128)(2,1)} %pad_maximum_fusion.5.refs_0_), custom_call_target="tpu_custom_call" | custom-call | bytes 1048576 | tf_op jit(solution)/shard_map/pallas_call | solution.py:237
  565.0 8.2 convolution_convert_fusion.3
  575.6 6.8 all-to-all-start.10
  589.3 21.6 %all-to-all-done.10 = bf16[16,256,160]{1,2,0:T(8,128)(2,1)} async-done(((bf16[16,256,160]{1,2,0:T(8,128)(2,1)}), bf16[16,256,160]{1,2,0:T(8,128)(2,1)}, u32[]{:S(2)}, u32[]{:S(2)}) %all-to-all-start.10) | async-done | bytes 1310752 | tf_op jit(solution)/shard_map/all_to_all | solution.py:614
  610.9 5.6 all-to-all-start.11
  620.9 5.7 all-to-all-start.8
  630.7 28.5 %all-to-all-done.8 = bf16[4,1280,160]{1,2,0:T(8,128)(2,1)} async-done(((bf16[4,1280,160]{1,2,0:T(8,128)(2,1)}), bf16[4,1280,160]{1,2,0:T(8,128)(2,1)}, u32[]{:S(2)}, u32[]{:S(2)}) %all-to-all-start.8) | async-done | bytes 1638432 | tf_op jit(solution)/shard_map/all_to_all | solution.py:633
  659.2 7.8 all-to-all-start.7
  667.7 8.5 convolution_convert_fusion.1
  676.2 64.5 %shard_map.417 = bf16[2,64,2560]{2,1,0:T(8,128)(2,1)} custom-call(bf16[4,4,2,64,2560]{4,3,2,1,0:T(8,128)(2,1)} %bitcast.201), custom_call_target="tpu_custom_call" | custom-call | bytes 1048576 | tf_op jit(solution)/shard_map/pallas_call | solution.py:400
  740.8 11.4 %convolution_convert_fusion.2 = bf16[2560,512]{1,0:T(8,128)(2,1)} fusion(bf16[2048,2560]{1,0:T(8,128)(2,1)} %bitcast.203, bf16[2048,256]{0,1:T(8,128)(2,1)S(1)} %copy-done.64, bf16[2048,256]{0,1:T(8,128)(2,1)S(1)} %copy-done.62), kind=kOutput, calls=%fused_computation.7 | convolution fusion | flops 5374214144 | bytes 15204352 | tf_op jit(solution)/shard_map/dot_general | solution.py:438
  752.1 7.9 all-to-all-start.9
  782.3 39.0 %all-to-all-done.9 = bf16[16,160,512]{2,1,0:T(8,128)(2,1)} async-done(((bf16[16,160,512]{2,1,0:T(8,128)(2,1)}), bf16[16,160,512]{2,1,0:T(8,128)(2,1)}, u32[]{:S(2)}, u32[]{:S(2)}) %all-to-all-start.9) | async-done | bytes 2621472 | tf_op jit(solution)/shard_map/all_to_all | solution.py:612
  832.7 23.5 %add_multiply_fusion = (f32[160,2,3840]{2,1,0:T(2,128)}, f32[160,2,3840]{2,1,0:T(2,128)}, f32[160,2,3840]{2,1,0:T(2,128)}, f32[160,2,3840]{2,1,0:T(2,128)}) fusion(bf16[160,2,3840]{2,1,0:T(2,128)(2,1)} %param.28, f32[]{:T(128)} %bitcast.75, f32[]{:T(128)} %bitcast.74, f32[160,2,3840]{2,1,0:T(2,128)} %param.40, f32[160,2,3840]{2,1,0:T(2,128)} %param.34, ...), kind=kLoop, calls=%fused_computation.5 | loop fusion | flops 19660800 | bytes 34406408 | tf_op jit(solution)/shard_map/mul | solution.py:455
  (255 shorter events, 146.5 us)
Async XLA Ops:
  77.8 23.7 %all-to-all-start = ((bf16[4,128,1536]{2,1,0:T(8,128)(2,1)}), bf16[4,128,1536]{2,1,0:T(8,128)(2,1)S(1)}, u32[]{:S(2)}, u32[]{:S(2)}) async-start(bf16[4,128,1536]{2,1,0:T(8,128)(2,1)} %bitcast.9), calls=%async_computation | async-start | bytes 3145728 | tf_op jit(solution)/shard_map/all_to_all | solution.py:548
  84.4 18.0 %copy-start.48 = (f32[128]{0:T(128)}, f32[128]{0:T(128)S(1)}, u32[]{:S(2)}) copy-start(f32[128]{0:T(128)S(1)} %convert_element_type.185) | copy-start | bytes 1540
  84.4 18.0 %copy-start.50 = (f32[128]{0:T(128)}, f32[128]{0:T(128)S(1)}, u32[]{:S(2)}) copy-start(f32[128]{0:T(128)S(1)} %multiply_power_fusion) | copy-start | bytes 1540
  85.4 51.6 %copy-start.30 = (f32[128,128]{1,0:T(8,128)}, f32[128,128]{1,0:T(8,128)S(1)}, u32[]{:S(2)}) copy-start(f32[128,128]{1,0:T(8,128)S(1)} %get-tuple-element.86) | copy-start | bytes 196612
  85.6 52.8 %copy-start.28 = (pred[128,1152]{0,1:T(8,128)(4,1)}, pred[128,1152]{0,1:T(8,128)(4,1)S(1)}, u32[]{:S(2)}) copy-start(pred[128,1152]{0,1:T(8,128)(4,1)S(1)} %compare_and_fusion) | copy-start | bytes 442372
  200.2 13.9 %all-to-all-start.1 = ((bf16[4,128,640]{1,2,0:T(8,128)(2,1)}), bf16[4,128,640]{1,2,0:T(8,128)(2,1)S(1)}, u32[]{:S(2)}, u32[]{:S(2)}) async-start(bf16[4,128,640]{1,2,0:T(8,128)(2,1)} %copy.152), calls=%async_computation.1 | async-start | bytes 1310720 | tf_op jit(solution)/shard_map/all_to_all | solution.py:544
  214.1 65.1 %all-to-all-start.2 = ((bf16[16,160,512]{2,1,0:T(8,128)(2,1)}), bf16[16,160,512]{2,1,0:T(8,128)(2,1)}, u32[]{:S(2)}, u32[]{:S(2)}) async-start(bf16[16,160,512]{2,1,0:T(8,128)(2,1)} %reshape.418), calls=%async_computation.2 | async-start | bytes 5242880 | tf_op jit(solution)/shard_map/all_to_all | solution.py:506
  222.1 3.5 collective-permute-start
  226.0 220.6 %copy-start.52 = (f32[128]{0:T(128)}, f32[128]{0:T(128)S(1)}, u32[]{:S(2)}) copy-start(f32[128]{0:T(128)S(1)} %add_rsqrt_fusion) | copy-start | bytes 1540
  279.2 84.4 %all-to-all-start.3 = ((bf16[16,256,160]{1,2,0:T(8,128)(2,1)}), bf16[16,256,160]{1,2,0:T(8,128)(2,1)}, u32[]{:S(2)}, u32[]{:S(2)}) async-start(bf16[16,256,160]{1,2,0:T(8,128)(2,1)} %bitcast.213), calls=%async_computation.3 | async-start | bytes 2621440 | tf_op jit(solution)/shard_map/all_to_all | solution.py:507
  374.5 10.8 %copy-start.61 = (bf16[2048,256]{0,1:T(8,128)(2,1)}, bf16[2048,256]{0,1:T(8,128)(2,1)S(1)}, u32[]{:S(2)}) copy-start(bf16[2048,256]{0,1:T(8,128)(2,1)S(1)} %get-tuple-element.65) | copy-start | bytes 3145732
  374.5 10.8 %copy-start.63 = (bf16[2048,256]{0,1:T(8,128)(2,1)}, bf16[2048,256]{0,1:T(8,128)(2,1)S(1)}, u32[]{:S(2)}) copy-start(bf16[2048,256]{0,1:T(8,128)(2,1)S(1)} %get-tuple-element.66) | copy-start | bytes 3145732
  385.3 61.3 %copy-start.9 = (bf16[128,2560]{1,0:T(8,128)(2,1)S(1)}, bf16[128,2560]{1,0:T(8,128)(2,1)}, u32[]{:S(2)}) copy-start(bf16[128,2560]{1,0:T(8,128)(2,1)} %param.24) | copy-start | bytes 1966084
  468.2 20.9 %all-to-all-start.5 = ((bf16[4,128,1280]{2,1,0:T(8,128)(2,1)}), bf16[4,128,1280]{2,1,0:T(8,128)(2,1)}, u32[]{:S(2)}, u32[]{:S(2)}) async-start(bf16[4,128,1280]{2,1,0:T(8,128)(2,1)} %bitcast.235), calls=%async_computation.5 | async-start | bytes 2621440 | tf_op jit(solution)/shard_map/all_to_all | solution.py:548
  474.9 17.8 %copy-start.17 = (bf16[9,1,128,256]{3,2,0,1:T(8,128)(2,1)S(1)}, bf16[9,1,128,256]{3,2,0,1:T(8,128)(2,1)}, u32[]{:S(2)}) copy-start(bf16[9,1,128,256]{3,2,0,1:T(8,128)(2,1)} %copy-done.16) | copy-start | bytes 1769476
  494.9 7.6 copy-start.46
  515.7 21.4 %copy-start.49 = (f32[128]{0:T(128)S(1)}, f32[128]{0:T(128)}, u32[]{:S(2)}) copy-start(f32[128]{0:T(128)} %copy-done.48) | copy-start | bytes 1540
  515.7 21.4 %copy-start.51 = (f32[128]{0:T(128)S(1)}, f32[128]{0:T(128)}, u32[]{:S(2)}) copy-start(f32[128]{0:T(128)} %copy-done.50) | copy-start | bytes 1540
  517.2 38.7 %copy-start.60 = (bf16[4,160,1536]{2,1,0:T(8,128)(2,1)S(1)}, bf16[4,160,1536]{2,1,0:T(8,128)(2,1)}, u32[]{:S(2)}) copy-start(bf16[4,160,1536]{2,1,0:T(8,128)(2,1)} %get-tuple-element.34) | copy-start | bytes 5898244
  559.8 15.8 %all-to-all-start.6 = ((bf16[4,128,640]{1,2,0:T(8,128)(2,1)}), bf16[4,128,640]{1,2,0:T(8,128)(2,1)S(1)}, u32[]{:S(2)}, u32[]{:S(2)}) async-start(bf16[4,128,640]{1,2,0:T(8,128)(2,1)} %copy.170), calls=%async_computation.6 | async-start | bytes 1310720 | tf_op jit(solution)/shard_map/all_to_all | solution.py:544
  575.6 9.1 %copy-start.42 = (f32[4,4,160]{2,1,0:T(4,128)S(1)}, f32[4,4,160]{2,1,0:T(4,128)}, u32[]{:S(2)}) copy-start(f32[4,4,160]{2,1,0:T(4,128)} %get-tuple-element.42) | copy-start | bytes 30724
  575.6 9.2 %copy-start.43 = (f32[2560]{0:T(1024)S(1)}, f32[2560]{0:T(1024)}, u32[]{:S(2)}) copy-start(f32[2560]{0:T(1024)} %get-tuple-element.40) | copy-start | bytes 30724
  575.6 11.3 %copy-start.55 = (f32[128]{0:T(128)S(1)}, f32[128]{0:T(128)}, u32[]{:S(2)}) copy-start(f32[128]{0:T(128)} %get-tuple-element.87) | copy-start | bytes 1540
  575.6 35.3 %all-to-all-start.10 = ((bf16[16,256,160]{1,2,0:T(8,128)(2,1)}), bf16[16,256,160]{1,2,0:T(8,128)(2,1)}, u32[]{:S(2)}, u32[]{:S(2)}) async-start(bf16[16,256,160]{1,2,0:T(8,128)(2,1)} %bitcast.212), calls=%async_computation.10 | async-start | bytes 2621440 | tf_op jit(solution)/shard_map/all_to_all | solution.py:614
  584.6 2.3 collective-permute-start.1
  610.9 10.0 %all-to-all-start.11 = ((f32[16,2,160]{2,1,0:T(2,128)}), f32[16,2,160]{2,1,0:T(2,128)S(1)}, u32[]{:S(2)}, u32[]{:S(2)}) async-start(f32[16,2,160]{2,1,0:T(2,128)} %maximum_bitcast_fusion), calls=%async_computation.11 | async-start | bytes 65536 | tf_op jit(solution)/shard_map/all_to_all | solution.py:671
  620.9 38.4 %all-to-all-start.8 = ((bf16[4,1280,160]{1,2,0:T(8,128)(2,1)}), bf16[4,1280,160]{1,2,0:T(8,128)(2,1)}, u32[]{:S(2)}, u32[]{:S(2)}) async-start(bf16[4,1280,160]{1,2,0:T(8,128)(2,1)} %bitcast.231), calls=%async_computation.8 | async-start | bytes 3276800 | tf_op jit(solution)/shard_map/all_to_all | solution.py:633
  659.2 92.9 %all-to-all-start.7 = ((bf16[4,160,1536]{2,1,0:T(8,128)(2,1)}), bf16[4,160,1536]{2,1,0:T(8,128)(2,1)}, u32[]{:S(2)}, u32[]{:S(2)}) async-start(bf16[4,160,1536]{2,1,0:T(8,128)(2,1)} %bitcast.230), calls=%async_computation.7 | async-start | bytes 3932160 | tf_op jit(solution)/shard_map/all_to_all | solution.py:633
  676.2 64.6 %copy-start.62 = (bf16[2048,256]{0,1:T(8,128)(2,1)S(1)}, bf16[2048,256]{0,1:T(8,128)(2,1)}, u32[]{:S(2)}) copy-start(bf16[2048,256]{0,1:T(8,128)(2,1)} %copy-done.61) | copy-start | bytes 3145732
  676.2 64.6 %copy-start.64 = (bf16[2048,256]{0,1:T(8,128)(2,1)S(1)}, bf16[2048,256]{0,1:T(8,128)(2,1)}, u32[]{:S(2)}) copy-start(bf16[2048,256]{0,1:T(8,128)(2,1)} %copy-done.63) | copy-start | bytes 3145732
  752.1 69.2 %all-to-all-start.9 = ((bf16[16,160,512]{2,1,0:T(8,128)(2,1)}), bf16[16,160,512]{2,1,0:T(8,128)(2,1)}, u32[]{:S(2)}, u32[]{:S(2)}) async-start(bf16[16,160,512]{2,1,0:T(8,128)(2,1)} %bitcast.217), calls=%async_computation.9 | async-start | bytes 5242880 | tf_op jit(solution)/shard_map/all_to_all | solution.py:612
  779.1 2.0 collective-permute-start.2
  (47 other events, 170.7 us)

commit v2 on v1

--- a/solution.py
+++ b/solution.py
@@ -40,7 +40,7 @@
     return steps[::-1] if far_first else steps
 
 
-def greet(ns, nd, use_z, use_plane, use_core, z_all=False):
+def greet(ns, nd, use_z, use_plane, use_core, z_all=False, everyone=False):
     s, d, m = (lax.axis_index(a) for a in ("shard", "dp", "mp"))
     bar = pltpu.get_barrier_semaphore()
 
@@ -56,6 +56,10 @@
         when(s < ns - 1, lambda: hello({"shard": s + 1}))
         when(s > 0, lambda: hello({"shard": s - 1}))
         count = (s < ns - 1).astype(jnp.int32) + (s > 0).astype(jnp.int32)
+    if everyone:
+        for b, e in others(ns, nd):
+            hello({"shard": b, "dp": e})
+        count += ns * nd - 1
     if use_plane:
         for k in range(1, nd):
             hello({"dp": lax.rem(d + k, nd)})
@@ -66,6 +70,13 @@
     pl.semaphore_wait(bar, count)
 
 
+def others(ns, nd):
+    me = lax.axis_index("shard") * nd + lax.axis_index("dp")
+    for k in range(1, ns * nd):
+        p = lax.rem(me + k, ns * nd)
+        yield p // nd, lax.rem(p, nd)
+
+
 def square(d):
     low = lax.rem(d, 2)
     x = d + 1 - 2 * low
@@ -79,7 +90,7 @@
     s, d, m = (lax.axis_index(a) for a in ("shard", "dp", "mp"))
     use_z = any(k in ("z", "all") for k in modes)
     use_plane = any(k in ("plane", "all", "swap") for k in modes)
-    greet(ns, nd, use_z, use_plane, "all" in modes)
+    greet(ns, nd, use_z, use_plane, "all" in modes, everyone="spread" in modes)
     peers = [lax.rem(d + k, nd) for k in range(1, nd)]
     relay = [
         nd == 4 and modes[i] in ("all", "plane") and ins[i].shape[0] % 32 == 0 for i in range(n)]
@@ -89,6 +100,8 @@
     def place(i, b, e, core):
         if modes[i] == "z":
             return outs[i].at[b]
+        if modes[i] == "spread":
+            return outs[i].at[b * nd + e]
         if modes[i] in ("plane", "swap"):
             return outs[i].at[e]
         return outs[i].at[b, e, core]
@@ -141,8 +154,18 @@
             ref, ref, sems[7 * i + 4].at[b, e], sems[7 * i + 5].at[b, e],
             device_id={"mp": 1 - m}, device_id_type=MESH)
 
+    def spread_copies(i, arriving):
+        copies = []
+        for b, e in others(ns, nd):
+            to = outs[i].at[b * nd + e] if arriving else outs[i].at[s * nd + d]
+            slot = (b, e, 0) if arriving else (s, d, 0)
+            copies.append(pltpu.make_async_remote_copy(
+                ins[i].at[b * nd + e], to, sems[7 * i + 2].at[b, e], sems[7 * i + 3].at[slot],
+                device_id={"shard": b, "dp": e}, device_id_type=MESH))
+        return copies
+
     def lcopy(i):
-        src = ins[i].at[d] if modes[i] == "swap" else ins[i]
+        src = ins[i].at[d] if modes[i] == "swap" else ins[i].at[s * nd + d] if modes[i] == "spread" else ins[i]
         return pltpu.make_async_copy(src, place(i, s, d, m), sems[7 * i + 6])
 
     def in_z(i):
@@ -163,6 +186,9 @@
                 c.start()
         if modes[i] == "all":
             ccopy(i, b, d, first).start()
+        if modes[i] == "spread":
+            for c in spread_copies(i, False):
+                c.start()
         if first:
             lcopy(i).start()
 
@@ -200,6 +226,11 @@
             if relay[i]:
                 for _, on in pass_copies(i, b):
                     on.wait_send()
+        if modes[i] == "spread":
+            for c in spread_copies(i, False):
+                c.wait_send()
+            for c in spread_copies(i, True):
+                c.wait_recv()
         if modes[i] == "all":
             for e in [d] + peers:
                 crecv(i, b, e).wait_recv()
@@ -227,7 +258,7 @@
 def gather(collective, mesh_shape, items):
     ns, nd = mesh_shape["shard"], mesh_shape["dp"]
     modes = tuple(mode for _, mode in items)
-    lead = {"z": (ns,), "plane": (nd,), "all": (ns, nd, 2), "swap": ()}
+    lead = {"z": (ns,), "plane": (nd,), "all": (ns, nd, 2), "swap": (), "spread": ()}
     shapes = [jax.ShapeDtypeStruct(lead[mode] + a.shape, a.dtype) for a, mode in items]
     sems = []
     dma = pltpu.SemaphoreType.DMA
@@ -246,10 +277,13 @@
     )(*[a for a, _ in items])
 
 
-def reduce_kernel(ns, nd, share, p, out, own, sib, got, mid, zgot, fin,
-                  lsem, ss, sr, ps, pr, zs, zr, fs, fr, ls2):
+def reduce_kernel(ns, nd, share, spans, *refs):
+    count = len(spans) if spans else 1
+    n_in = count + 1 if spans else 1
+    ins, outs, scratch = refs[:n_in], refs[n_in : n_in + count], refs[n_in + count :]
+    own, sib, give, got, mid, zgot, fin, lsem, ss, sr, ps, pr, zs, zr, fs, fr, ks = scratch
     s, d, m = (lax.axis_index(a) for a in ("shard", "dp", "mp"))
-    h, c = fin.shape
+    h, c = fin.shape[1:]
     tile = 16
     greet(ns, nd, True, True, True, z_all=True)
     peers = [lax.rem(d + k, nd) for k in range(1, nd)]
@@ -258,161 +292,282 @@
         x, y, across = square(d)
         peers = [across, x, y]
     order = [lax.rem(s + k, ns) for k in sorted(range(1, ns), key=lambda k: abs(k - ns // 2))] + [s]
-
-    def score(b):
-        return pltpu.make_async_remote_copy(
-            p.at[b, :, 1 - m], sib.at[b], ss.at[b], sr.at[b], device_id={"mp": 1 - m}, device_id_type=MESH)
-
-    def load(b):
-        return pltpu.make_async_copy(p.at[b, :, m], own.at[b], lsem.at[b])
-
-    def pcopy(b, src, slot, to):
-        return pltpu.make_async_remote_copy(
-            src, slot[0], ps.at[b, slot[1]], pr.at[b, slot[1]], device_id={"dp": to}, device_id_type=MESH)
-
-    def sends(b):
+    items = [(a, k, order[k]) for k in range(ns) for a in range(count)]
+
+    def score(a, k, b):
+        src = give.at[a, k % 2] if spans else ins[0].at[b, :, 1 - m]
+        return pltpu.make_async_remote_copy(
+            src, sib.at[a, b], ss.at[a, b], sr.at[a, b], device_id={"mp": 1 - m}, device_id_type=MESH)
+
+    def load(a, b):
+        return pltpu.make_async_copy(ins[0].at[b, :, m], own.at[a, b], lsem.at[a, b])
+
+    def multiply(a, b, core, store):
+        lo, hi = spans[a]
+        step = 512 if c % 512 == 0 else 128
+        left = ins[a][b, :, core].reshape(nd * h, hi - lo)
+
+        @pl.loop(0, c // step)
+        def _(j):
+            cols = pl.ds(pl.multiple_of(j * step, step), step)
+            term = cols_product(left, ins[count][cols, lo:hi])
+            store(cols, term.astype(BF16).reshape(nd, h, step))
+
+    def zero(a, k, b):
+        if not spans:
+            score(a, k, b).start()
+            load(a, b).start()
+            return
+        if k >= 2:
+            score(a, k - 2, order[k - 2]).wait_send()
+
+        def to_give(cols, v):
+            give[a, k % 2, :, :, cols] = v
+
+        def to_own(cols, v):
+            own[a, b, :, :, cols] = v
+
+        multiply(a, b, 1 - m, to_give)
+        score(a, k, b).start()
+        multiply(a, b, m, to_own)
+
+    def pcopy(a, b, src, dst, slot, to):
+        return pltpu.make_async_remote_copy(
+            src, dst, ps.at[a, b, slot], pr.at[a, b, slot], device_id={"dp": to}, device_id_type=MESH)
+
+    def sends(a, b):
         if not relay:
             return [pltpu.make_async_remote_copy(
-                own.at[b, e], got.at[b, d], ps.at[b, e], pr.at[b, d], device_id={"dp": e}, device_id_type=MESH)
-                for e in peers]
+                own.at[a, b, e], got.at[a, b, d], ps.at[a, b, e], pr.at[a, b, d],
+                device_id={"dp": e}, device_id_type=MESH) for e in peers]
         half = h // 2
         first, last = pl.ds(0, half), pl.ds(half, half)
         return [
-            pcopy(b, own.at[b, across, first], (got.at[b, 0, first], 0), x),
-            pcopy(b, own.at[b, across, last], (got.at[b, 0, last], 1), y),
-            pcopy(b, own.at[b, x], (got.at[b, 1], 2), x),
-            pcopy(b, own.at[b, y], (got.at[b, 2], 3), y),
+            pcopy(a, b, own.at[a, b, across, first], got.at[a, b, 0, first], 0, x),
+            pcopy(a, b, own.at[a, b, across, last], got.at[a, b, 0, last], 1, y),
+            pcopy(a, b, own.at[a, b, x], got.at[a, b, 1], 2, x),
+            pcopy(a, b, own.at[a, b, y], got.at[a, b, 2], 3, y),
         ]
 
-    def zcopy(b, to):
-        return pltpu.make_async_remote_copy(
-            mid.at[b], zgot.at[to], zs.at[b], zr.at[to], device_id={"shard": b}, device_id_type=MESH)
-
-    def rows(r):
-        return pl.ds(pl.multiple_of(r * tile, tile), tile)
+    def zcopy(a, b, to):
+        return pltpu.make_async_remote_copy(
+            mid.at[a, b], zgot.at[a, to], zs.at[a, b], zr.at[a, to], device_id={"shard": b}, device_id_type=MESH)
 
     def sum_rows(lo, hi, terms, store):
         @pl.loop(lo // tile, hi // tile)
         def _(r):
-            at = rows(r)
+            at = pl.ds(pl.multiple_of(r * tile, tile), tile)
             v = terms[0](at).astype(F32)
             for f in terms[1:]:
                 v = v + f(at).astype(F32)
-            store(at, v)
-
-    def to_own(b, e):
+            store(at, v.astype(BF16))
+
+    def to_own(a, b, e):
         def store(at, v):
-            own[b, e, at] = v.astype(BF16)
+            own[a, b, e, at] = v
         return store
 
-    def one(b):
-        score(b).wait_recv()
-        load(b).wait()
-        out_now = sends(b)
+    def one(a, k, b):
+        score(a, k, b).wait_recv()
+        if not spans:
+            load(a, b).wait()
+        out_now = sends(a, b)
         for j, e in enumerate(peers + [d]):
-            sum_rows(0, h, [lambda at, e=e: own[b, e, at], lambda at, e=e: sib[b, e, at]], to_own(b, e))
+            sum_rows(0, h, [lambda at, e=e: own[a, b, e, at], lambda at, e=e: sib[a, b, e, at]], to_own(a, b, e))
             if relay and j == 0:
                 out_now[0].start()
                 out_now[1].start()
             elif not relay and j < len(peers):
                 out_now[j].start()
 
-    def two(b):
+    def two(a, k, b):
         if not relay:
             return
         half = h // 2
-        c0, c1, c2, c3 = sends(b)
+        c0, c1, c2, c3 = sends(a, b)
         c0.wait_recv()
-        sum_rows(0, half, [lambda at: own[b, y, at], lambda at: got[b, 0, at]], to_own(b, y))
+        sum_rows(0, half, [lambda at: own[a, b, y, at], lambda at: got[a, b, 0, at]], to_own(a, b, y))
         c3.start()
         c1.wait_recv()
-        sum_rows(half, h, [lambda at: own[b, x, at], lambda at: got[b, 0, at]], to_own(b, x))
+        sum_rows(half, h, [lambda at: own[a, b, x, at], lambda at: got[a, b, 0, at]], to_own(a, b, x))
         c2.start()
 
-    def plane_terms(b):
+    def plane_terms(a, b):
         slots = [1, 2] if relay else peers
-        return [lambda at: own[b, d, at]] + [lambda at, e=e: got[b, e, at] for e in slots]
-
-    def three(b, last):
+        return [lambda at: own[a, b, d, at]] + [lambda at, e=e: got[a, b, e, at] for e in slots]
+
+    def three(a, k, b):
         if relay:
-            for w in sends(b)[2:]:
+            for w in sends(a, b)[2:]:
                 w.wait_recv()
         else:
             for e in peers:
                 pltpu.make_async_remote_copy(
-                    own.at[b, e], got.at[b, e], ps.at[b, e], pr.at[b, e],
+                    own.at[a, b, e], got.at[a, b, e], ps.at[a, b, e], pr.at[a, b, e],
                     device_id={"dp": e}, device_id_type=MESH).wait_recv()
-        if not last:
+        if k < ns - 1:
             def store(at, v):
-                mid[b, at] = v.astype(BF16)
-            sum_rows(0, h, plane_terms(b), store)
-            zcopy(b, s).start()
-
-    for b in order:
-        score(b).start()
-        load(b).start()
-    for k in range(ns + 2):
-        if k < ns:
-            one(order[k])
-        if 0 <= k - 1 < ns:
-            two(order[k - 1])
-        if 0 <= k - 2 < ns:
-            three(order[k - 2], k - 2 == ns - 1)
+                mid[a, b, at] = v
+            sum_rows(0, h, plane_terms(a, b), store)
+            zcopy(a, b, s).start()
+
+    stages = [zero, one, two, three]
+    if not spans:
+        for item in items:
+            zero(*item)
+        stages = stages[1:]
+    for t in range(len(items) + len(stages) - 1):
+        for j, stage in enumerate(stages):
+            if 0 <= t - j < len(items):
+                stage(*items[t - j])
+
+    def give_out(a, core):
+        return pltpu.make_async_remote_copy(
+            fin.at[a], outs[a].at[core], fs.at[a], fr.at[a], device_id={"mp": 1 - m}, device_id_type=MESH)
+
+    def keep(a):
+        return pltpu.make_async_copy(fin.at[a], outs[a].at[m] if share else outs[a], ks.at[a])
+
     others = order[:-1]
-    for b in others:
-        zcopy(b, b).wait_recv()
-
-    def store(at, v):
-        fin[at] = v.astype(fin.dtype)
-
-    sum_rows(0, h, plane_terms(s) + [lambda at, b=b: zgot[b, at] for b in others], store)
-    if share:
-        give = pltpu.make_async_remote_copy(
-            fin, out.at[m], fs, fr, device_id={"mp": 1 - m}, device_id_type=MESH)
-        take = pltpu.make_async_remote_copy(
-            fin, out.at[1 - m], fs, fr, device_id={"mp": 1 - m}, device_id_type=MESH)
-        give.start()
-        keep = pltpu.make_async_copy(fin, out.at[m], ls2)
-        keep.start()
-        take.wait_recv()
-        give.wait_send()
-        keep.wait()
+    for a in range(count):
+        for b in others:
+            zcopy(a, b, b).wait_recv()
+
+        def store(at, v, a=a):
+            fin[a, at] = v
+
+        sum_rows(0, h, plane_terms(a, s) + [lambda at, b=b: zgot[a, b, at] for b in others], store)
+        if share:
+            give_out(a, m).start()
+        keep(a).start()
+    for a in range(count):
+        if share:
+            give_out(a, 1 - m).wait_recv()
+            give_out(a, m).wait_send()
+        keep(a).wait()
+        for k, b in enumerate(order):
+            if not spans or k >= ns - 2:
+                score(a, k, b).wait_send()
+            for w in sends(a, b):
+                w.wait_send()
+        for b in others:
+            zcopy(a, b, s).wait_send()
+
+
+def reduce_scatter(collective, mesh_shape, share, blocks, terms=None, factors=None, weight=None):
+    ns, nd = mesh_shape["shard"], mesh_shape["dp"]
+    rows, c = blocks
+    h = rows // 2
+    count = len(factors) if factors else 1
+    size = ns * nd * h * c * 2
+    if size * count * 3 > (40 << 20):
+        whole = [terms] if factors is None else [
+            cols_product(x, weight[:, lo:hi]).astype(BF16) for x, lo, hi in factors]
+        sums = []
+        for p in whole:
+            total = lax.psum_scatter(p.reshape(ns * nd, 2, h, c), TOK, scatter_dimension=0, tiled=True)[0]
+            total = lax.psum(total, "mp")
+            sums.append(total if share else lax.dynamic_index_in_dim(total, lax.axis_index("mp"), 0, False))
+        return sums
+    if factors is None:
+        spans = None
+        args = [terms.reshape(ns, nd, 2, h, c)]
+        in_specs = [pl.BlockSpec(memory_space=pl.ANY)]
+        give = (1, 1, 1, 16, 128)
     else:
-        keep = pltpu.make_async_copy(fin, out, ls2)
-        keep.start()
-        keep.wait()
-    for b in order:
-        score(b).wait_send()
-        for w in sends(b):
-            w.wait_send()
-    for b in others:
-        zcopy(b, s).wait_send()
-
-
-def reduce_scatter(collective, mesh_shape, p, share):
-    ns, nd = mesh_shape["shard"], mesh_shape["dp"]
-    h, c = p.shape[3:]
-    if 3 * (p.size // 2) * 2 > (40 << 20):
-        total = lax.psum_scatter(p.reshape(ns * nd, 2, h, c), TOK, scatter_dimension=0, tiled=True)[0]
-        total = lax.psum(total, "mp")
-        return total if share else lax.dynamic_index_in_dim(total, lax.axis_index("mp"), 0, False)
+        spans = tuple((lo, hi) for _, lo, hi in factors)
+        args = [x.reshape(ns, nd, 2, h, hi - lo) for x, lo, hi in factors] + [weight]
+        in_specs = [pl.BlockSpec(memory_space=pltpu.VMEM)] * (count + 1)
+        give = (count, 2, nd, h, c)
+    slots = 3 if nd == 4 and h % 32 == 0 else nd
     dma = pltpu.SemaphoreType.DMA
     return pl.pallas_call(
-        partial(reduce_kernel, ns, nd, share),
-        out_shape=jax.ShapeDtypeStruct((2, h, c) if share else (h, c), BF16),
+        partial(reduce_kernel, ns, nd, share, spans),
+        out_shape=[jax.ShapeDtypeStruct((2, h, c) if share else (h, c), BF16)] * count,
+        in_specs=in_specs,
+        out_specs=[pl.BlockSpec(memory_space=pl.ANY)] * count,
+        scratch_shapes=[
+            pltpu.VMEM((count, ns, nd, h, c), BF16),
+            pltpu.VMEM((count, ns, nd, h, c), BF16),
+            pltpu.VMEM(give, BF16),
+            pltpu.VMEM((count, ns, slots, h, c), BF16),
+            pltpu.VMEM((count, ns, h, c), BF16),
+            pltpu.VMEM((count, ns, h, c), BF16),
+            pltpu.VMEM((count, h, c), BF16),
+            dma((count, ns)), dma((count, ns)), dma((count, ns)),
+            dma((count, ns, max(nd, 4))), dma((count, ns, max(nd, 4))),
+            dma((count, ns)), dma((count, ns)), dma((count,)), dma((count,)), dma((count,)),
+        ],
+        compiler_params=pltpu.CompilerParams(
+            collective_id=collective, has_side_effects=True, vmem_limit_bytes=VMEM_LIMIT),
+        cost_estimate=pl.CostEstimate(flops=0, bytes_accessed=1 << 20, transcendentals=0),
+    )(*args)
+
+
+def plane_kernel(ns, nd, p, out, own, sib, ls, ss, sr, ps, pr, fs, fr, ks):
+    d, m = lax.axis_index("dp"), lax.axis_index("mp")
+    h, c = own.shape[1:]
+    tile = 16
+    greet(ns, nd, False, True, True)
+    peers = [lax.rem(d + k, nd) for k in range(1, nd)]
+    order = ([square(d)[2], square(d)[0], square(d)[1]] if nd == 4 else peers) + [d]
+    other = {"mp": 1 - m}
+
+    def score(e):
+        return pltpu.make_async_remote_copy(
+            p.at[e, 1 - m], sib.at[e], ss.at[e], sr.at[e], device_id=other, device_id_type=MESH)
+
+    def load(e):
+        return pltpu.make_async_copy(p.at[e, m], own.at[e], ls.at[e])
+
+    def send(e, block):
+        return pltpu.make_async_remote_copy(
+            own.at[e], out.at[block, m], ps.at[e], pr.at[block], device_id={"dp": e}, device_id_type=MESH)
+
+    def share(e, core):
+        src = own.at[d] if e is d else out.at[e, m]
+        return pltpu.make_async_remote_copy(
+            src, out.at[e, core], fs.at[e], fr.at[e], device_id=other, device_id_type=MESH)
+
+    for e in order:
+        score(e).start()
+        load(e).start()
+    for e in order:
+        score(e).wait_recv()
+        load(e).wait()
+
+        @pl.loop(0, h // tile)
+        def _(r, e=e):
+            at = pl.ds(pl.multiple_of(r * tile, tile), tile)
+            own[e, at] = (own[e, at].astype(F32) + sib[e, at].astype(F32)).astype(BF16)
+
+        if e is not d:
+            send(e, d).start()
+    keep = pltpu.make_async_copy(own.at[d], out.at[d, m], ks)
+    keep.start()
+    share(d, m).start()
+    for e in order[:-1]:
+        send(e, e).wait_recv()
+        share(e, m).start()
+    keep.wait()
+    for e in order:
+        share(e, 1 - m).wait_recv()
+        share(e, m).wait_send()
+        score(e).wait_send()
+        if e is not d:
+            send(e, d).wait_send()
+
+
+def plane_reduce(collective, mesh_shape, p):
+    ns, nd = mesh_shape["shard"], mesh_shape["dp"]
+    h, c = p.shape[2:]
+    dma = pltpu.SemaphoreType.DMA
+    return pl.pallas_call(
+        partial(plane_kernel, ns, nd),
+        out_shape=jax.ShapeDtypeStruct(p.shape, BF16),
         in_specs=[pl.BlockSpec(memory_space=pl.ANY)],
         out_specs=pl.BlockSpec(memory_space=pl.ANY),
-        scratch_shapes=[
-            pltpu.VMEM((ns, nd, h, c), BF16),
-            pltpu.VMEM((ns, nd, h, c), BF16),
-            pltpu.VMEM((ns, nd, h, c), BF16),
-            pltpu.VMEM((ns, h, c), BF16),
-            pltpu.VMEM((ns, h, c), BF16),
-            pltpu.VMEM((h, c), BF16),
-            dma((ns,)), dma((ns,)), dma((ns,)),
-            dma((ns, nd)), dma((ns, nd)),
-            dma((ns,)), dma((ns,)), dma(()), dma(()), dma(()),
-        ],
+        scratch_shapes=[pltpu.VMEM((nd, h, c), BF16)] * 2 + [dma((nd,))] * 7 + [dma(())],
         compiler_params=pltpu.CompilerParams(
             collective_id=collective, has_side_effects=True, vmem_limit_bytes=VMEM_LIMIT),
         cost_estimate=pl.CostEstimate(flops=0, bytes_accessed=1 << 20, transcendentals=0),
@@ -448,16 +603,72 @@
     return jnp.dot(left_side, right_side, preferred_element_type=F32)
 
 
-def adam_update(grad_own, weight, first_old, second_old, bias_first, bias_second, decay):
-    first_new = BETA_ONE * first_old + (1.0 - BETA_ONE) * grad_own
-    second_new = BETA_TWO * second_old + (1.0 - BETA_TWO) * grad_own * grad_own
-    direction = first_new / bias_first / (jnp.sqrt(second_new / bias_second) + ADAM_EPS)
-    return (first_new, second_new, -LEARN_RATE * (direction + decay * weight.astype(F32)))
-
-
-def swap_add(value):
-    other = lax.ppermute(value, "mp", [(0, 1), (1, 0)])
-    return value.astype(F32) + other.astype(F32)
+def pack_kernel(full, gateup, down, out):
+    units = down.shape[1]
+    here = pl.program_id(0) < full
+
+    def keep(v):
+        return jnp.where(here, v, jnp.zeros_like(v)).astype(BF16)
+
+    out[0, :, :units] = keep(gateup[:, 0, :].astype(F32))
+    out[0, :, units : 2 * units] = keep(gateup[:, 1, :].astype(F32))
+    out[0, :, 2 * units :] = keep(down[...].astype(F32))
+
+
+def pack(n, units, gateup_weight, down_cols):
+    own_d, _, ff_local = gateup_weight.shape
+    full = ff_local // units
+    return pl.pallas_call(
+        partial(pack_kernel, full),
+        out_shape=jax.ShapeDtypeStruct((n, own_d, 3 * units), BF16),
+        grid=(n,),
+        in_specs=[
+            pl.BlockSpec((own_d, 2, units), lambda j: (0, 0, jnp.minimum(j, full - 1))),
+            pl.BlockSpec((own_d, units), lambda j: (0, jnp.minimum(j, full - 1))),
+        ],
+        out_specs=pl.BlockSpec((1, own_d, 3 * units), lambda j: (j, 0, 0)),
+        compiler_params=pltpu.CompilerParams(vmem_limit_bytes=VMEM_LIMIT),
+    )(gateup_weight, down_cols)
+
+
+def adam_step(rates, grad, weight, first, second, decay):
+    first_new = BETA_ONE * first + (1.0 - BETA_ONE) * grad
+    second_new = BETA_TWO * second + (1.0 - BETA_TWO) * grad * grad
+    direction = first_new * rates[0] / (jnp.sqrt(second_new * rates[1]) + ADAM_EPS)
+    return first_new, second_new, -LEARN_RATE * (direction + decay * weight.astype(F32))
+
+
+def unpack_kernel(rates, got, gw, gf, gs, dw, df, ds, gg, gfn, gsn, gu, dg, dfn, dsn, du):
+    units = dw.shape[1]
+    pair = (rates[0], rates[1])
+    for k in range(2):
+        grad = got[0, :, k * units : (k + 1) * units].astype(F32)
+        gg[:, k, :] = grad
+        gfn[:, k, :], gsn[:, k, :], gu[:, k, :] = adam_step(
+            pair, grad, gw[:, k, :], gf[:, k, :], gs[:, k, :], DECAY_RATE)
+    grad = got[0, :, 2 * units :].astype(F32)
+    dg[...] = grad
+    dfn[...], dsn[...], du[...] = adam_step(pair, grad, dw[...], df[...], ds[...], DECAY_RATE)
+
+
+def unpack_adam(units, rates, got, gateup, down):
+    own_d, _, ff_local = gateup[0].shape
+    three = pl.BlockSpec((own_d, 2, units), lambda j: (0, 0, j))
+    two = pl.BlockSpec((own_d, units), lambda j: (0, j))
+    shape3 = jax.ShapeDtypeStruct(gateup[0].shape, F32)
+    shape2 = jax.ShapeDtypeStruct(down[0].shape, F32)
+    out = pl.pallas_call(
+        unpack_kernel,
+        out_shape=[shape3] * 4 + [shape2] * 4,
+        grid=(ff_local // units,),
+        in_specs=[
+            pl.BlockSpec(memory_space=pltpu.SMEM),
+            pl.BlockSpec((1, own_d, 3 * units), lambda j: (j, 0, 0)),
+        ] + [three] * 3 + [two] * 3,
+        out_specs=[three] * 4 + [two] * 4,
+        compiler_params=pltpu.CompilerParams(vmem_limit_bytes=VMEM_LIMIT),
+    )(rates, got, *gateup, *down)
+    return out[:4], out[4:]
 
 
 def shards(
@@ -500,12 +711,7 @@
     plane_tok = nd * tok
     plane_d = ns * own_d
 
-    gateup_cut = jnp.pad(gateup_weight, ((0, 0), (0, 0), (0, ff_pad)))
-    gateup_cut = gateup_cut.reshape(own_d, 2, n, units).transpose(2, 0, 1, 3).reshape(n, own_d, 2 * units)
-    down_cut = jnp.pad(down_weight, ((0, ff_pad), (0, 0))).reshape(n, units, own_d)
-    gateup_mine = lax.all_to_all(gateup_cut, TOK, 0, 0, tiled=True).reshape(width, 2 * units)
-    down_mine = lax.all_to_all(down_cut, TOK, 0, 0, tiled=True)
-    down_mine = down_mine.transpose(1, 0, 2).reshape(units, width)
+    three = pack(n, units, gateup_weight, down_weight.T)
 
     input_rows = tokens_in.astype(F32)
     inverse_one = lax.rsqrt(jnp.mean(input_rows * input_rows, axis=1) + EPS_NORM)
@@ -523,11 +729,14 @@
     def plane_cut(value):
         return value.reshape(tok, ns, nd, own_d).transpose(2, 0, 1, 3).reshape(nd, tok, plane_d)
 
-    tokens_plane, qkv_plane, small_all, cot_all = gather(
+    small_all, tokens_plane, cot_all, qkv_plane = gather(
         0, mesh_shape,
-        [(plane_cut(tokens_in), "swap"), (qkv_weight, "z"), (small, "all"),
-         (lax.dynamic_slice_in_dim(block_cotangent, m * half, half, 0), "all")])
+        [(small, "all"), (plane_cut(tokens_in), "swap"),
+         (lax.dynamic_slice_in_dim(block_cotangent, m * half, half, 0), "all"), (qkv_weight, "z")])
     tokens_plane = tokens_plane.reshape(plane_tok, plane_d)
+    three, tokens_plane = lax.optimization_barrier((three, tokens_plane))
+    three = lax.all_to_all(three, TOK, 0, 0, tiled=True).reshape(width, 3 * units)
+    gateup_mine, down_mine = three[:, : 2 * units], three[:, 2 * units :]
     qkv_plane = qkv_plane.reshape(plane_d, q_cols + HEAD_DIM)
     cot_all = cot_all.reshape(n * tok, width)
     small_all = small_all[:, :, 0]
@@ -537,19 +746,20 @@
     plane_scale = lax.dynamic_index_in_dim(small_all[:, :, 3, :tok], s, 0, False).reshape(plane_tok, 1)
     plane_gain = lax.dynamic_index_in_dim(gains_by[:, :, 0], d, 1, False).reshape(1, plane_d)
 
-    def to_plane(value):
-        return lax.all_to_all(plane_cut(value), "dp", 0, 0, tiled=True).reshape(plane_tok, plane_d)
-
-    def from_plane(value):
-        got = lax.all_to_all(value.reshape(nd, tok, plane_d), "dp", 0, 0, tiled=True)
-        return got.reshape(nd, tok, ns, own_d).transpose(1, 2, 0, 3).reshape(tok, width)
-
-    def plane_sum(value):
-        got = lax.all_to_all(value.reshape(nd, tok, -1), "dp", 0, 0, tiled=True)
+    def to_plane(collective, value):
+        (got,) = gather(collective, mesh_shape, [(plane_cut(value), "swap")])
+        return got.reshape(plane_tok, plane_d)
+
+    def from_plane(collective, value):
+        got = plane_reduce(collective, mesh_shape, value.reshape(nd, 2, half, plane_d))
+        return got.reshape(nd, tok, ns, own_d).transpose(1, 2, 0, 3).reshape(tok, width).astype(F32)
+
+    def plane_sum(collective, value):
+        (got,) = gather(collective, mesh_shape, [(value.reshape(nd, tok, -1), "swap")])
         return jnp.sum(got.astype(F32), axis=0)
 
     hidden_plane = (tokens_plane.astype(F32) * plane_scale * plane_gain).astype(BF16)
-    qkv_raw = plane_sum(product(hidden_plane, qkv_plane).astype(BF16))
+    qkv_raw = plane_sum(8, product(hidden_plane, qkv_plane).astype(BF16))
 
     pad = KV_BLOCKS * tok
     key_span = pad + tok
@@ -584,11 +794,10 @@
     mixed = jnp.einsum("htk,kd->thd", probs_low, value_rows, preferred_element_type=F32)
     mixed_low = mixed.reshape(tok, q_cols).astype(BF16)
     mixed_plane, outproj_z = gather(
-        2, mesh_shape, [(mixed_low, "plane"), (outproj_weight, "z")])
+        2, mesh_shape, [(mixed_low, "plane"), (outproj_weight.T, "z")])
     mixed_plane = mixed_plane.reshape(plane_tok, q_cols)
-    outproj_plane = outproj_z.transpose(1, 0, 2).reshape(q_cols, plane_d)
-    attn_part = from_plane(product(mixed_plane, outproj_plane).astype(BF16))
-    residual = input_rows + swap_add(attn_part)
+    outproj_plane = outproj_z.reshape(plane_d, q_cols)
+    residual = input_rows + from_plane(9, cols_product(mixed_plane, outproj_plane).astype(BF16))
     gain_two = full_gains[1]
     inverse_two = lax.rsqrt(jnp.mean(residual * residual, axis=1, keepdims=True) + EPS_NORM)
     hidden_two = (residual * inverse_two * gain_two).astype(BF16)
@@ -600,21 +809,18 @@
     gate_pre, up_pre = gateup_pre[:, :units], gateup_pre[:, units:]
     gelu_val, gelu_pull = jax.vjp(partial(jax.nn.gelu, approximate=True), gate_pre)
     act_low = (gelu_val * up_pre).astype(BF16)
-    act_grad = cols_product(cot_all, down_mine)
+    act_grad = product(cot_all, down_mine)
     gateup_low = jnp.concatenate(
         [gelu_pull(act_grad * up_pre)[0], act_grad * gelu_val], axis=1).astype(BF16)
-    hidden_two_part = cols_product(gateup_low, gateup_mine).astype(BF16)
-    hidden_two_grad = reduce_scatter(
-        4, mesh_shape, hidden_two_part.reshape(ns, nd, 2, half, width), True).reshape(tok, width).astype(F32)
-    gateup_grad = rows_product(hidden_all, gateup_low).astype(BF16).reshape(n, own_d, 2 * units)
-    down_grad = rows_product(act_low, cot_all).astype(BF16)
-    down_grad = down_grad.reshape(units, n, own_d).transpose(1, 0, 2)
-    own_gateup = lax.all_to_all(gateup_grad, TOK, 0, 0, tiled=True).reshape(n, own_d, 2, units)
-    own_gateup = own_gateup.transpose(1, 2, 0, 3).reshape(own_d, 2, n * units)[:, :, :ff_local].astype(F32)
-    own_down = lax.all_to_all(down_grad, TOK, 0, 0, tiled=True).reshape(n * units, own_d)[:ff_local].astype(F32)
-    ffn_part = product(act_low, down_mine).astype(BF16)
-    ffn_sum = reduce_scatter(
-        5, mesh_shape, ffn_part.reshape(ns, nd, 2, half, width), True).reshape(tok, width).astype(F32)
+    three_grad = jnp.concatenate(
+        [rows_product(hidden_all, gateup_low).astype(BF16), rows_product(cot_all, act_low).astype(BF16)], axis=1)
+    three_grad, act_low, gateup_low = lax.optimization_barrier((three_grad, act_low, gateup_low))
+    three_grad = lax.all_to_all(three_grad.reshape(n, own_d, 3 * units), TOK, 0, 0, tiled=True)
+    hidden_two_grad, ffn_sum = reduce_scatter(
+        4, mesh_shape, True, (tok, width),
+        factors=[(gateup_low, 0, 2 * units), (act_low, 2 * units, 3 * units)], weight=three)
+    hidden_two_grad = hidden_two_grad.reshape(tok, width).astype(F32)
+    ffn_sum = ffn_sum.reshape(tok, width).astype(F32)
     block_out = (residual + ffn_sum).astype(BF16)
 
     def norm_back(rows, inverse, gain_row, grad):
@@ -625,16 +831,17 @@
 
     residual_from, gain_two_grad = norm_back(residual, inverse_two, gain_two, hidden_two_grad)
     residual_grad = block_cotangent.astype(F32) + residual_from
-    attn_low = to_plane(residual_grad.astype(BF16))
-    mixed_grad = plane_sum(cols_product(attn_low, outproj_plane).astype(BF16))
+    attn_low = to_plane(10, residual_grad.astype(BF16))
+    mixed_grad = plane_sum(11, product(attn_low, outproj_plane).astype(BF16))
     mixed_grad = mixed_grad.astype(BF16).reshape(tok, heads_local, HEAD_DIM)
 
     def z_sum(value):
         got = lax.all_to_all(value, "shard", 0, 0, tiled=True)
         return jnp.sum(got.astype(F32), axis=0)
 
-    outproj_grad = rows_product(mixed_plane, attn_low).astype(BF16)
-    own_outproj = z_sum(outproj_grad.reshape(q_cols, ns, own_d).transpose(1, 0, 2))
+    outproj_grad = rows_product(attn_low, mixed_plane).astype(BF16)
+    outproj_grad, three_grad = lax.optimization_barrier((outproj_grad, three_grad))
+    own_outproj = z_sum(outproj_grad.reshape(ns, own_d, q_cols))
 
     probs_grad = jnp.einsum("thd,kd->htk", mixed_grad, value_rows, preferred_element_type=F32)
     value_grad = jnp.einsum("htk,thd->kd", probs_low, mixed_grad, preferred_element_type=F32)
@@ -647,15 +854,14 @@
         axis=1).astype(BF16)
     kv_grad_pad = lax.dynamic_update_slice_in_dim(
         jnp.zeros((KV_BLOCKS + n, 2, tok, HEAD_DIM), BF16), window_grad, me, 0)
-    kv_grad = reduce_scatter(
-        6, mesh_shape, kv_grad_pad[KV_BLOCKS:].reshape(ns, nd, 2, tok, HEAD_DIM), False).astype(F32)
+    (kv_grad,) = reduce_scatter(6, mesh_shape, False, (2 * tok, HEAD_DIM), terms=kv_grad_pad[KV_BLOCKS:])
+    kv_grad = kv_grad.astype(F32)
     kv_low = jnp.where(m == 0, rotate(kv_grad, cosine, -sine_rows), kv_grad)
     query_low = rotate(query_rot_grad, cos_h, -sin_h).reshape(tok, q_cols)
     qkv_low = jnp.concatenate([query_low, kv_low], axis=1).astype(BF16)
     (qkv_low_plane,) = gather(7, mesh_shape, [(qkv_low, "plane")])
     qkv_low_plane = qkv_low_plane.reshape(plane_tok, q_cols + HEAD_DIM)
-    hidden_part = from_plane(cols_product(qkv_low_plane, qkv_plane).astype(BF16))
-    hidden_one_grad = swap_add(hidden_part)
+    hidden_one_grad = from_plane(12, cols_product(qkv_low_plane, qkv_plane).astype(BF16))
     qkv_grad = rows_product(hidden_plane, qkv_low_plane).astype(BF16)
     own_qkv = z_sum(qkv_grad.reshape(ns, own_d, q_cols + HEAD_DIM))
     own_query = own_qkv[:, :q_cols]
@@ -668,27 +874,31 @@
     input_from, gain_one_grad = norm_back(input_rows, inverse_col, full_gains[0], hidden_one_grad)
     input_grad = residual_grad + input_from
     gains_cut = jnp.stack([gain_one_grad, gain_two_grad], axis=0).reshape(2, n, own_d).transpose(1, 0, 2)
-    own_gains = jnp.sum(lax.all_to_all(gains_cut, TOK, 0, 0, tiled=True), axis=0)
+    gains_cut = jnp.pad(gains_cut, ((0, 0), (0, 6), (0, lanes - own_d)))
+    (gains_got,) = gather(13, mesh_shape, [(gains_cut, "spread")])
+    own_gains = jnp.sum(gains_got[:, :2, :own_d], axis=0)
 
     step_value = step_count[0].astype(F32)
     bias_first = 1.0 - jnp.power(BETA_ONE, step_value)
     bias_second = 1.0 - jnp.power(BETA_TWO, step_value)
-    grads = (own_query, own_keyval, own_outproj, own_gateup, own_down, own_gains)
-    weights = (query_weight, keyval_weight, outproj_weight, gateup_weight, down_weight, norm_gains)
-    firsts = (query_first, keyval_first, outproj_first, gateup_first, down_first, gains_first)
-    seconds = (query_second, keyval_second, outproj_second, gateup_second, down_second, gains_second)
-    decays = (DECAY_RATE,) * 5 + (0.0,)
+    rates = jnp.stack([1.0 / bias_first, 1.0 / bias_second])
+    gateup_news, down_news = unpack_adam(
+        units, rates, three_grad, (gateup_weight, gateup_first, gateup_second),
+        (down_weight.T, down_first.T, down_second.T))
+    down_news = [x.T for x in down_news]
+
+    def adam(grad, weight, first, second, decay):
+        return (grad,) + adam_step(rates, grad, weight, first, second, decay)
+
     news = [
-        adam_update(g, w, a, b, bias_first, bias_second, c)
-        for g, w, a, b, c in zip(grads, weights, firsts, seconds, decays)
+        adam(own_query, query_weight, query_first, query_second, DECAY_RATE),
+        adam(own_keyval, keyval_weight, keyval_first, keyval_second, DECAY_RATE),
+        tuple(v.T for v in adam(own_outproj, outproj_weight.T, outproj_first.T, outproj_second.T, DECAY_RATE)),
+        gateup_news,
+        down_news,
+        adam(own_gains, norm_gains, gains_first, gains_second, 0.0),
     ]
-    return (
-        (block_out, input_grad)
-        + grads
-        + tuple(x[0] for x in news)
-        + tuple(x[1] for x in news)
-        + tuple(x[2] for x in news)
-    )
+    return (block_out, input_grad) + tuple(x[k] for k in range(4) for x in news)
 
 
 def solution(mesh):

time: 867 us -> 762 us (0.88)
  waiting for transfers between devices: 171 us -> 0.01 us
  Pallas kernels: 374 us -> 527 us
  matrix products: 103 us -> 77 us
  other arithmetic: 69.9 us -> 44.9 us
  starting transfers between devices: 68.9 us -> 47.9 us
  blocking collectives: 12.8 us -> 0 us
    all_to_all x9 -> x2, waiting for transfers between devices: 141 us -> 0.01 us  [the longest x1 0.01 us: shards(): lax.all_to_all(three, TOK, 0, 0, tiled=True).reshape(width, 3 * units)]
    pallas_call x5 -> x9, Pallas kernels: 231 us -> 311 us  [gather(): pl.pallas_call(partial(gather_kernel, ns, nd, modes), out_shape=shapes, i...]
    pallas_call x3 -> x6, Pallas kernels: 143 us -> 217 us  [the longest x2 155 us: reduce_scatter(): pl.pallas_call(partial(reduce_kernel, ns, nd, share, spans), out_shape=[j...]
    all_to_all x2, waiting for transfers between devices: 28.5 us -> 0.01 us  [z_sum(): got = lax.all_to_all(value, 'shard', 0, 0, tiled=True)]
    mul x6 -> x4, other arithmetic: 33.2 us -> 5.47 us  [adam_step(): -LEARN_RATE * (direction + decay * weight.astype(F32))]
    reshape x10 -> x0, local copies, waits for them, and re-layouts: 22.1 us -> none  [the longest x2 7.86 us: shards(): lax.all_to_all(gateup_grad, TOK, 0, 0, tiled=True)]
    dot_general x4 -> x2, matrix products: 28.4 us -> 8.16 us  [cols_product(): lax.dot_general(left_side, right_side, (((1,), (1,)), ((), ())), preferre...]
    all_to_all x9 -> x2, starting transfers between devices: 55.1 us -> 35.7 us  [the longest x1 18.8 us: shards(): lax.all_to_all(three_grad.reshape(n, own_d, 3 * units), TOK, 0, 0, tiled=...]
  transfers between devices with their start and end apart: 14 -> 5, of which waited for: 8 -> 0; matrix products, arithmetic and copies ran while one was open for 11% -> 16% of each run, Pallas kernels for 15% -> 61%
where the time goes in v2:
time: 762 us; the launch traced here: 750 us
  Pallas kernels  527 us (69%)
  matrix products  77 us (10%)
  local copies, waits for them, and re-layouts  50.1 us (7%)
  starting transfers between devices  47.9 us (6%)
  other arithmetic  44.9 us (6%)
    pallas_call x9, Pallas kernels, gather(): pl.pallas_call(partial(gather_kernel, ns, nd, modes), out_shape=shapes, i...  311 us
    pallas_call x2, Pallas kernels, reduce_scatter(): pl.pallas_call(partial(reduce_kernel, ns, nd, share, spans), out_shape=[j...  155 us
    pallas_call x1, Pallas kernels, unpack_adam(): pl.pallas_call(unpack_kernel, out_shape=[shape3] * 4 + [shape2] * 4, grid...  26.2 us
    dot_general x4, matrix products, product(): return jnp.dot(left_side, right_side, preferred_element_type=F32)  25.9 us
    pallas_call x2, Pallas kernels, plane_reduce(): pl.pallas_call(partial(plane_kernel, ns, nd), out_shape=jax.ShapeDtypeStr...  21.6 us
    dot_general x4, matrix products, rows_product(): lax.dot_general(left_side, right_side, (((0,), (0,)), ((), ())), preferre...  19.8 us
    all_to_all x1, starting transfers between devices, shards(): lax.all_to_all(three_grad.reshape(n, own_d, 3 * units), TOK, 0, 0, tiled=...  18.8 us
    all_to_all x1, starting transfers between devices, shards(): lax.all_to_all(three, TOK, 0, 0, tiled=True).reshape(width, 3 * units)  16.9 us
  transfers between devices with their start and end apart: 5, of which 0 were waited for; matrix products, arithmetic and copies ran while one was open for 16% of the time, Pallas kernels for 61%

profile of v2, /device:TPU:14, one launch (start us, length us, event | category | flops | bytes accessed | tf_op | source)
XLA Modules:
  0.0 750.3 jit_solution(6082134448541735303)
XLA Ops:
  8.2 14.0 %shard_map.413 = bf16[16,160,768]{2,1,0:T(8,128)(2,1)} custom-call(bf16[160,2,3840]{2,1,0:T(2,128)(2,1)} %gw.1, bf16[160,3840]{1,0:T(8,128)(2,1)} %bitcast.184), custom_call_target="tpu_custom_call" | custom-call | tf_op jit(solution)/shard_map/pallas_call | solution.py:621
  22.8 59.2 %shard_map.414 = (f32[4,4,2,8,256]{4,3,2,1,0:T(8,128)}, bf16[4,128,640]{2,1,0:T(8,128)(2,1)}, bf16[4,4,2,64,2560]{4,3,2,1,0:T(8,128)(2,1)}, bf16[4,160,1536]{2,1,0:T(8,128)(2,1)}) custom-call(f32[8,256]{1,0:T(8,128)} %fusion.76.refs_0_, bf16[4,128,640]{2,1,0:T(8,128)(2,1)} %copy.101.refs_1_, bf16[64,2560]{1,0:T(8,128)(2,1)} %constant_dynamic-slice_fusion.2.refs_2_, ...), custom_call_target="tpu_custom_call" | custom-call | bytes 1048576 | tf_op jit(solution)/shard_map/pallas_call | solution.py:268
  82.0 16.9 %all-to-all-start = ((bf16[16,160,768]{2,1,0:T(8,128)(2,1)}), bf16[16,160,768]{2,1,0:T(8,128)(2,1)}, u32[]{:S(2)}, u32[]{:S(2)}) async-start(bf16[16,160,768]{2,1,0:T(8,128)(2,1)} %shard_map.413), calls=%async_computation | async-start | bytes 7864320 | tf_op jit(solution)/shard_map/all_to_all | solution.py:738
  99.2 4.1 convolution_convert_fusion.4
  103.4 36.0 %shard_map.415 = bf16[4,128,1536]{2,1,0:T(8,128)(2,1)} custom-call(bf16[4,128,1536]{2,1,0:T(8,128)(2,1)} %bitcast.202), custom_call_target="tpu_custom_call" | custom-call | bytes 1048576 | tf_op jit(solution)/shard_map/pallas_call | solution.py:268
  143.1 60.2 %shard_map.416 = bf16[4,4,2,128,256]{4,3,2,1,0:T(8,128)(2,1)} custom-call(bf16[128,256]{1,0:T(8,128)(2,1)} %fusion.63.refs_0_), custom_call_target="tpu_custom_call" | custom-call | bytes 1048576 | tf_op jit(solution)/shard_map/pallas_call | solution.py:268
  210.0 37.0 %shard_map.417 = (bf16[4,128,1280]{2,1,0:T(8,128)(2,1)}, bf16[4,160,1280]{2,1,0:T(8,128)(2,1)}) custom-call(bf16[128,1280]{1,0:T(8,128)(2,1)} %copy.108.refs_0_, bf16[160,1280]{1,0:T(8,128)(2,1)} %bitcast.200), custom_call_target="tpu_custom_call" | custom-call | bytes 1048576 | tf_op jit(solution)/shard_map/pallas_call | solution.py:268
  247.1 3.9 convolution_convert_fusion.6
  250.9 11.0 %shard_map.418 = bf16[4,2,64,640]{3,2,1,0:T(8,128)(2,1)} custom-call(bf16[4,2,64,640]{3,2,1,0:T(8,128)(2,1)} %bitcast.209), custom_call_target="tpu_custom_call" | custom-call | bytes 1048576 | tf_op jit(solution)/shard_map/pallas_call | solution.py:565
  268.4 51.2 %shard_map.419 = bf16[4,4,2,64,2560]{4,3,2,1,0:T(8,128)(2,1)} custom-call(bf16[64,2560]{1,0:T(8,128)(2,1)} %fusion.60.refs_0_), custom_call_target="tpu_custom_call" | custom-call | bytes 1048576 | tf_op jit(solution)/shard_map/pallas_call | solution.py:268
  319.6 9.2 %fusion.11 = f32[2048,512]{0,1:T(8,128)S(1)} fusion(bf16[2048,2560]{1,0:T(8,128)(2,1)} %bitcast.175, bf16[2560,768]{1,0:T(8,128)(2,1)} %bitcast.30.refs_2_), kind=kOutput, calls=%fused_computation.32 | convolution fusion | flops 5368709120 | bytes 17301504 | tf_op jit(solution)/shard_map/dot_general | solution.py:603
  328.8 8.7 %fusion.22 = (bf16[2048,256]{0,1:T(8,128)(2,1)S(1)}, bf16[2048,256]{0,1:T(8,128)(2,1)S(1)}, bf16[2048,256]{0,1:T(8,128)(2,1)S(1)}) fusion(f32[2048,512]{0,1:T(8,128)S(1)} %fusion.11, bf16[2048,2560]{1,0:T(8,128)(2,1)} %bitcast.217, bf16[2560,768]{1,0:T(8,128)(2,1)} %bitcast.30.refs_2_), kind=kOutput, calls=%fused_computation.43 | convolution fusion | flops 2697986048 | bytes 19136512 | tf_op jit(solution)/shard_map/dot_general | solution.py:603
  339.1 9.2 %convolution_convert_fusion = bf16[2560,512]{0,1:T(8,128)(2,1)S(1)} fusion(bf16[2048,2560]{1,0:T(8,128)(2,1)} %bitcast.176, bf16[2048,256]{0,1:T(8,128)(2,1)S(1)} %get-tuple-element.93, bf16[2048,256]{0,1:T(8,128)(2,1)S(1)} %get-tuple-element.92), kind=kOutput, calls=%fused_computation.1 | convolution fusion | flops 5374214144 | bytes 15204352 | tf_op jit(solution)/shard_map/dot_general | solution.py:593
  353.4 6.3 copy.128
  359.7 18.8 %all-to-all-start.2 = ((bf16[16,160,768]{2,1,0:T(8,128)(2,1)}), bf16[16,160,768]{2,1,0:T(8,128)(2,1)}, u32[]{:S(2)}, u32[]{:S(2)}) async-start(bf16[16,160,768]{2,1,0:T(8,128)(2,1)} %bitcast.174), calls=%async_computation.2 | async-start | bytes 7864320 | tf_op jit(solution)/shard_map/all_to_all | solution.py:818
  382.3 3.9 copy.111
  388.4 136.4 %shard_map.420 = (bf16[2,64,2560]{2,1,0:T(8,128)(2,1)}, bf16[2,64,2560]{2,1,0:T(8,128)(2,1)}) custom-call(bf16[4,4,2,64,512]{4,3,2,1,0:T(8,128)(2,1)} %bitcast.177, bf16[4,4,2,64,256]{4,3,2,1,0:T(8,128)(2,1)} %bitcast.188, bf16[2560,768]{1,0:T(8,128)(2,1)} %bitcast.30.refs_2_), custom_call_target="tpu_custom_call" | custom-call | bytes 1048576 | tf_op jit(solution)/shard_map/pallas_call | solution.py:484
  534.0 13.4 %shard_map.421 = bf16[4,128,640]{2,1,0:T(8,128)(2,1)} custom-call(bf16[4,128,640]{2,1,0:T(8,128)(2,1)} %copy.115.refs_0_), custom_call_target="tpu_custom_call" | custom-call | bytes 1048576 | tf_op jit(solution)/shard_map/pallas_call | solution.py:268
  547.3 3.9 convolution_convert_fusion.3
  551.2 18.3 %shard_map.422 = bf16[4,128,1280]{2,1,0:T(8,128)(2,1)} custom-call(bf16[4,128,1280]{2,1,0:T(8,128)(2,1)} %bitcast.205), custom_call_target="tpu_custom_call" | custom-call | bytes 1048576 | tf_op jit(solution)/shard_map/pallas_call | solution.py:268
  577.1 7.7 %fusion.51 = f32[128,5,256]{2,0,1:T(8,128)} fusion(bf16[1152,256,1]{1,0,2:T(8,128)(2,1)} %bitcast.212, f32[5,128,1152]{1,2,0:T(8,128)} %convolution_bitcast_fusion.1, f32[1152,128,5]{1,0,2:T(8,128)} %copy-done.1, f32[5,128]{1,0:T(8,128)S(1)} %copy-done.34, f32[5,128]{1,0:T(8,128)S(1)} %copy-done.32, pred[128,1152]{0,1:T(8,128)(4,1)S(1)} %compare_and_fusion), kind=kOutput, calls=%fused_computation.83 | convolution fusion | flops 385599232 | bytes 7296000 | tf_op jit(solution)/shard_map/htk,kd->thd/dot_general | solution.py:850
  593.4 7.5 fusion.13
  603.7 18.6 %shard_map.423 = bf16[128,256]{1,0:T(8,128)(2,1)} custom-call(bf16[4,4,2,128,256]{4,3,2,1,0:T(8,128)(2,1)} %bitcast.179), custom_call_target="tpu_custom_call" | custom-call | bytes 1048576 | tf_op jit(solution)/shard_map/pallas_call | solution.py:484
  625.3 15.5 %shard_map.424 = bf16[4,128,1536]{2,1,0:T(8,128)(2,1)} custom-call(bf16[128,1536]{1,0:T(8,128)(2,1)} %pad_maximum_fusion.4.refs_0_), custom_call_target="tpu_custom_call" | custom-call | bytes 1048576 | tf_op jit(solution)/shard_map/pallas_call | solution.py:268
  640.8 4.0 convolution_convert_fusion.2
  644.9 6.5 all-to-all-start.1
  652.8 4.3 convolution_convert_fusion.5
  657.1 10.6 %shard_map.425 = bf16[4,2,64,640]{3,2,1,0:T(8,128)(2,1)} custom-call(bf16[4,2,64,640]{3,2,1,0:T(8,128)(2,1)} %bitcast.208), custom_call_target="tpu_custom_call" | custom-call | bytes 1048576 | tf_op jit(solution)/shard_map/pallas_call | solution.py:565
  679.6 19.9 %shard_map.427 = f32[16,8,256]{2,1,0:T(8,128)} custom-call(f32[16,8,256]{2,1,0:T(8,128)} %pad.20.refs_0_), custom_call_target="tpu_custom_call" | custom-call | bytes 1048576 | tf_op jit(solution)/shard_map/pallas_call | solution.py:268
  703.3 5.6 all-to-all-start.3
  710.5 4.1 fusion.45
  719.9 26.2 %shard_map.426 = (f32[160,2,3840]{2,1,0:T(2,128)}, f32[160,2,3840]{2,1,0:T(2,128)}, f32[160,2,3840]{2,1,0:T(2,128)}, f32[160,2,3840]{2,1,0:T(2,128)}, f32[160,38...) custom-call(f32[2]{0:T(128)} %pad_maximum_fusion.9.rates, ...), custom_call_target="tpu_custom_call" | custom-call | tf_op jit(solution)/shard_map/pallas_call | solution.py:660
  (221 shorter events, 95.4 us)
Async XLA Ops:
  4.2 202.3 %copy-start.35 = (f32[128]{0:T(128)}, f32[128]{0:T(128)S(1)}, u32[]{:S(2)}) copy-start(f32[128]{0:T(128)S(1)} %get-tuple-element.116) | copy-start | bytes 1540
  4.2 202.3 %copy-start.37 = (s32[128]{0:T(128)}, s32[128]{0:T(128)S(1)}, u32[]{:S(2)}) copy-start(s32[128]{0:T(128)S(1)} %get-tuple-element.120) | copy-start | bytes 1540
  82.0 17.0 %copy-start.30 = (f32[4,4,2,8,256]{4,3,2,1,0:T(8,128)S(1)}, f32[4,4,2,8,256]{4,3,2,1,0:T(8,128)}, u32[]{:S(2)}) copy-start(f32[4,4,2,8,256]{4,3,2,1,0:T(8,128)} %get-tuple-element.51) | copy-start | bytes 786436
  82.0 17.2 %copy-start.54 = (bf16[4,128,640]{2,1,0:T(8,128)(2,1)S(1)}, bf16[4,128,640]{2,1,0:T(8,128)(2,1)}, u32[]{:S(2)}) copy-start(bf16[4,128,640]{2,1,0:T(8,128)(2,1)} %get-tuple-element.49) | copy-start | bytes 1966084
  82.0 237.6 %all-to-all-start = ((bf16[16,160,768]{2,1,0:T(8,128)(2,1)}), bf16[16,160,768]{2,1,0:T(8,128)(2,1)}, u32[]{:S(2)}, u32[]{:S(2)}) async-start(bf16[16,160,768]{2,1,0:T(8,128)(2,1)} %shard_map.413), calls=%async_computation | async-start | bytes 7864320 | tf_op jit(solution)/shard_map/all_to_all | solution.py:738
  141.8 64.7 %copy-start.28 = (f32[1152]{0:T(1024)}, f32[1152]{0:T(1024)S(1)}, u32[]{:S(2)}) copy-start(f32[1152]{0:T(1024)S(1)} %pad_dynamic-slice_fusion.2) | copy-start | bytes 13828
  142.1 62.2 %copy-start.40 = (f32[128]{0:T(128)}, f32[128]{0:T(128)S(1)}, u32[]{:S(2)}) copy-start(f32[128]{0:T(128)S(1)} %convert_element_type.168) | copy-start | bytes 1540
  142.1 62.1 %copy-start.42 = (f32[128]{0:T(128)}, f32[128]{0:T(128)S(1)}, u32[]{:S(2)}) copy-start(f32[128]{0:T(128)S(1)} %multiply_power_fusion) | copy-start | bytes 1540
  267.4 259.0 %copy-start.44 = (f32[128]{0:T(128)}, f32[128]{0:T(128)S(1)}, u32[]{:S(2)}) copy-start(f32[128]{0:T(128)S(1)} %add_rsqrt_fusion) | copy-start | bytes 1540
  337.6 10.7 %copy-start.12 = (bf16[2048,256]{0,1:T(8,128)(2,1)}, bf16[2048,256]{0,1:T(8,128)(2,1)S(1)}, u32[]{:S(2)}) copy-start(bf16[2048,256]{0,1:T(8,128)(2,1)S(1)} %get-tuple-element.58) | copy-start | bytes 3145732
  337.6 10.7 %slice-start = ((s8[10485760]{0:T(1024)(128)(4,1)}), s8[4194304]{0:T(1024)(128)(4,1)S(1)}, s32[]{:S(2)}) async-start(s8[10485760]{0:T(1024)(128)(4,1)} %bitcast.218), calls=%async_computation.4 | async-start | bytes 8388608
  339.0 9.2 %slice-start.1 = ((s8[10485760]{0:T(1024)(128)(4,1)}), s8[4194304]{0:T(1024)(128)(4,1)S(1)}, s32[]{:S(2)}) async-start(s8[10485760]{0:T(1024)(128)(4,1)} %bitcast.218), calls=%async_computation.5 | async-start | bytes 8388608
  339.1 9.2 %slice-start.2 = ((s8[10485760]{0:T(1024)(128)(4,1)}), s8[2097152]{0:T(1024)(128)(4,1)S(1)}, s32[]{:S(2)}) async-start(s8[10485760]{0:T(1024)(128)(4,1)} %bitcast.218), calls=%async_computation.6 | async-start | bytes 4194304
  359.6 18.8 %copy-start.29 = (f32[1152]{0:T(1024)S(1)}, f32[1152]{0:T(1024)}, u32[]{:S(2)}) copy-start(f32[1152]{0:T(1024)} %copy-done.28) | copy-start | bytes 13828
  359.6 18.8 %copy-start.36 = (f32[128]{0:T(128)S(1)}, f32[128]{0:T(128)}, u32[]{:S(2)}) copy-start(f32[128]{0:T(128)} %copy-done.35) | copy-start | bytes 1540
  359.6 18.8 %copy-start.38 = (s32[128]{0:T(128)S(1)}, s32[128]{0:T(128)}, u32[]{:S(2)}) copy-start(s32[128]{0:T(128)} %copy-done.37) | copy-start | bytes 1540
  359.6 19.0 %copy-start.32 = (f32[5,128]{1,0:T(8,128)S(1)}, f32[5,128]{1,0:T(8,128)}, u32[]{:S(2)}) copy-start(f32[5,128]{1,0:T(8,128)} %copy-done.31) | copy-start | bytes 7684
  359.6 19.0 %copy-start.34 = (f32[5,128]{1,0:T(8,128)S(1)}, f32[5,128]{1,0:T(8,128)}, u32[]{:S(2)}) copy-start(f32[5,128]{1,0:T(8,128)} %copy-done.33) | copy-start | bytes 7684
  359.7 285.2 %all-to-all-start.2 = ((bf16[16,160,768]{2,1,0:T(8,128)(2,1)}), bf16[16,160,768]{2,1,0:T(8,128)(2,1)}, u32[]{:S(2)}, u32[]{:S(2)}) async-start(bf16[16,160,768]{2,1,0:T(8,128)(2,1)} %bitcast.174), calls=%async_computation.2 | async-start | bytes 7864320 | tf_op jit(solution)/shard_map/all_to_all | solution.py:818
  577.1 7.7 %copy-start.19 = (f32[128,128]{1,0:T(8,128)S(1)}, f32[128,128]{1,0:T(8,128)}, u32[]{:S(2)}) copy-start(f32[128,128]{1,0:T(8,128)} %copy-done.18) | copy-start | bytes 196612
  603.7 19.6 %copy-start.41 = (f32[128]{0:T(128)S(1)}, f32[128]{0:T(128)}, u32[]{:S(2)}) copy-start(f32[128]{0:T(128)} %copy-done.40) | copy-start | bytes 1540
  603.7 19.6 %copy-start.43 = (f32[128]{0:T(128)S(1)}, f32[128]{0:T(128)}, u32[]{:S(2)}) copy-start(f32[128]{0:T(128)} %copy-done.42) | copy-start | bytes 1540
  603.7 20.8 %copy-start.11 = (bf16[128,1280]{1,0:T(8,128)(2,1)S(1)}, bf16[128,1280]{1,0:T(8,128)(2,1)}, u32[]{:S(2)}) copy-start(bf16[128,1280]{1,0:T(8,128)(2,1)} %copy.124) | copy-start | bytes 983044
  622.3 18.5 %copy-start.48 = (f32[640]{0:T(1024)S(1)}, f32[640]{0:T(1024)}, u32[]{:S(2)}) copy-start(f32[640]{0:T(1024)} %copy-done.47) | copy-start | bytes 7684
  622.3 18.5 %copy-start.53 = (f32[1,4,1,128]{3,2,1,0:T(1,128)S(1)}, f32[1,4,1,128]{3,2,1,0:T(1,128)}, u32[]{:S(2)}) copy-start(f32[1,4,1,128]{3,2,1,0:T(1,128)} %copy-done.52) | copy-start | bytes 6148
  622.3 18.5 %copy-start.55 = (bf16[4,128,640]{2,1,0:T(8,128)(2,1)S(1)}, bf16[4,128,640]{2,1,0:T(8,128)(2,1)}, u32[]{:S(2)}) copy-start(bf16[4,128,640]{2,1,0:T(8,128)(2,1)} %get-tuple-element.49) | copy-start | bytes 1966084
  644.9 58.4 %all-to-all-start.1 = ((bf16[4,160,1536]{2,1,0:T(8,128)(2,1)}), bf16[4,160,1536]{2,1,0:T(8,128)(2,1)}, u32[]{:S(2)}, u32[]{:S(2)}) async-start(bf16[4,160,1536]{2,1,0:T(8,128)(2,1)} %bitcast.199), calls=%async_computation.1 | async-start | bytes 3932160 | tf_op jit(solution)/shard_map/all_to_all | solution.py:839
  703.2 6.6 copy-start.50
  703.2 6.6 copy-start.51
  703.2 7.2 copy-start.45
  703.3 42.8 %all-to-all-start.3 = ((bf16[4,160,1280]{2,1,0:T(8,128)(2,1)}), bf16[4,160,1280]{2,1,0:T(8,128)(2,1)}, u32[]{:S(2)}, u32[]{:S(2)}) async-start(bf16[4,160,1280]{2,1,0:T(8,128)(2,1)} %bitcast.201), calls=%async_computation.3 | async-start | bytes 3276800 | tf_op jit(solution)/shard_map/all_to_all | solution.py:839
  716.7 2.0 collective-permute-start
  (32 other events, 82.0 us)

commit v3 on v2

--- a/solution.py
+++ b/solution.py
@@ -40,7 +40,7 @@
     return steps[::-1] if far_first else steps
 
 
-def greet(ns, nd, use_z, use_plane, use_core, z_all=False, everyone=False):
+def greet(ns, nd, use_z, use_plane, use_core, z_all=False):
     s, d, m = (lax.axis_index(a) for a in ("shard", "dp", "mp"))
     bar = pltpu.get_barrier_semaphore()
 
@@ -56,10 +56,6 @@
         when(s < ns - 1, lambda: hello({"shard": s + 1}))
         when(s > 0, lambda: hello({"shard": s - 1}))
         count = (s < ns - 1).astype(jnp.int32) + (s > 0).astype(jnp.int32)
-    if everyone:
-        for b, e in others(ns, nd):
-            hello({"shard": b, "dp": e})
-        count += ns * nd - 1
     if use_plane:
         for k in range(1, nd):
             hello({"dp": lax.rem(d + k, nd)})
@@ -70,13 +66,6 @@
     pl.semaphore_wait(bar, count)
 
 
-def others(ns, nd):
-    me = lax.axis_index("shard") * nd + lax.axis_index("dp")
-    for k in range(1, ns * nd):
-        p = lax.rem(me + k, ns * nd)
-        yield p // nd, lax.rem(p, nd)
-
-
 def square(d):
     low = lax.rem(d, 2)
     x = d + 1 - 2 * low
@@ -84,29 +73,31 @@
     return x, y, lax.rem(x + 2, 4)
 
 
-def gather_kernel(ns, nd, modes, *refs):
+def gather_kernel(ns, nd, modes, work, n_work, *refs):
     n = len(modes)
-    ins, outs, sems = refs[:n], refs[n : 2 * n], refs[2 * n :]
+    ins, more_in = refs[:n], refs[n : n + n_work]
+    outs, more_out = refs[n + n_work : 2 * n + n_work], refs[2 * n + n_work : 2 * n + 2 * n_work - (n_work > 0)]
+    sems = refs[-7 * n :]
     s, d, m = (lax.axis_index(a) for a in ("shard", "dp", "mp"))
     use_z = any(k in ("z", "all") for k in modes)
     use_plane = any(k in ("plane", "all", "swap") for k in modes)
-    greet(ns, nd, use_z, use_plane, "all" in modes, everyone="spread" in modes)
+    direct = [modes[i] == "all" and ins[i].size * ins[i].dtype.itemsize < 128 << 10 for i in range(n)]
+    late = [modes[i] == "z" and any(k == "all" and not q for k, q in zip(modes, direct)) for i in range(n)]
+    greet(ns, nd, use_z, use_plane, "all" in modes, z_all=any(direct))
     peers = [lax.rem(d + k, nd) for k in range(1, nd)]
     relay = [
-        nd == 4 and modes[i] in ("all", "plane") and ins[i].shape[0] % 32 == 0 for i in range(n)]
+        nd == 4 and modes[i] in ("all", "plane") and ins[i].shape[0] % 32 == 0 and not direct[i] for i in range(n)]
     if nd == 4:
         x, y, across = square(d)
 
     def place(i, b, e, core):
         if modes[i] == "z":
             return outs[i].at[b]
-        if modes[i] == "spread":
-            return outs[i].at[b * nd + e]
         if modes[i] in ("plane", "swap"):
             return outs[i].at[e]
         return outs[i].at[b, e, core]
 
-    def part(i, ref, k):
+    def half_of(i, ref, k):
         if k is None:
             return ref
         rows = ins[i].shape[0] // 2
@@ -122,14 +113,14 @@
         e = d if e is None else e
         src = (ins[i].at[to] if modes[i] == "swap" else ins[i]) if first else place(i, b, e, m)
         return pltpu.make_async_remote_copy(
-            part(i, src, k), part(i, place(i, b, e, m), k),
+            half_of(i, src, k), half_of(i, place(i, b, e, m), k),
             sems[7 * i + 2].at[b, slot], sems[7 * i + 3].at[b, e, k or 0],
             device_id={"dp": to}, device_id_type=MESH)
 
     def precv(i, b, e, k=None):
         ref = place(i, b, e, m)
         return pltpu.make_async_remote_copy(
-            part(i, ref, k), part(i, ref, k), sems[7 * i + 2].at[b, 0], sems[7 * i + 3].at[b, e, k or 0],
+            half_of(i, ref, k), half_of(i, ref, k), sems[7 * i + 2].at[b, 0], sems[7 * i + 3].at[b, e, k or 0],
             device_id={"dp": peers[0]}, device_id_type=MESH)
 
     def own_copies(i, b, first):
@@ -154,22 +145,19 @@
             ref, ref, sems[7 * i + 4].at[b, e], sems[7 * i + 5].at[b, e],
             device_id={"mp": 1 - m}, device_id_type=MESH)
 
-    def spread_copies(i, arriving):
-        copies = []
-        for b, e in others(ns, nd):
-            to = outs[i].at[b * nd + e] if arriving else outs[i].at[s * nd + d]
-            slot = (b, e, 0) if arriving else (s, d, 0)
-            copies.append(pltpu.make_async_remote_copy(
-                ins[i].at[b * nd + e], to, sems[7 * i + 2].at[b, e], sems[7 * i + 3].at[slot],
-                device_id={"shard": b, "dp": e}, device_id_type=MESH))
-        return copies
+    def dcopy(i, to, block):
+        return pltpu.make_async_remote_copy(
+            ins[i], place(i, block, d, m), sems[7 * i].at[0, to], sems[7 * i + 1].at[block],
+            device_id={"shard": to}, device_id_type=MESH)
+
+    planes_off = [lax.rem(s + k, ns) for k in range(1, ns)]
 
     def lcopy(i):
-        src = ins[i].at[d] if modes[i] == "swap" else ins[i].at[s * nd + d] if modes[i] == "spread" else ins[i]
+        src = ins[i].at[d] if modes[i] == "swap" else ins[i]
         return pltpu.make_async_copy(src, place(i, s, d, m), sems[7 * i + 6])
 
     def in_z(i):
-        return modes[i] in ("z", "all")
+        return modes[i] in ("z", "all") and not direct[i]
 
     def in_plane(i, t):
         return modes[i] == "all" or (modes[i] in ("plane", "swap") and t == 0)
@@ -186,9 +174,9 @@
                 c.start()
         if modes[i] == "all":
             ccopy(i, b, d, first).start()
-        if modes[i] == "spread":
-            for c in spread_copies(i, False):
-                c.start()
+        if first and direct[i]:
+            for p in planes_off:
+                dcopy(i, p, s).start()
         if first:
             lcopy(i).start()
 
@@ -226,11 +214,9 @@
             if relay[i]:
                 for _, on in pass_copies(i, b):
                     on.wait_send()
-        if modes[i] == "spread":
-            for c in spread_copies(i, False):
-                c.wait_send()
-            for c in spread_copies(i, True):
-                c.wait_recv()
+        if direct[i] and first:
+            for p in planes_off:
+                dcopy(i, p, s).wait_send()
         if modes[i] == "all":
             for e in [d] + peers:
                 crecv(i, b, e).wait_recv()
@@ -246,19 +232,40 @@
 
     steps = planes(s, ns)
     levels = [[q for q in steps if q[1] == t] for t in range(ns)]
-    each(levels[0], lambda i, t: True, onward)
-    for t in range(1, ns + 1):
+    straight = [(b, 1, 0, True) for b in planes_off]
+    lag = max(ns - 2, 1)
+    each(levels[0], lambda i, t: not late[i], onward)
+
+    def arrive_straight(i, b, t, way):
+        dcopy(i, b, b).wait_recv()
+        onward(i, b, t, way)
+
+    def part(t):
+        if work is not None and t < ns:
+            work(t, ns, more_in, more_out)
+
+    part(0)
+    each(straight, lambda i, t: direct[i], arrive_straight)
+    for t in range(1, ns + lag):
         if t < ns:
-            each(levels[t], lambda i, t: in_z(i), arrive)
-        each(levels[t - 1], lambda i, t: relay[i] and in_plane(i, t), lambda i, b, t, way: pass_on(i, b))
-    each(steps, in_plane, lambda i, b, t, way: settle(i, b))
-    each(steps, lambda i, t: t == 0 or in_z(i), finish)
-
-
-def gather(collective, mesh_shape, items):
+            each(levels[t], lambda i, t: in_z(i) and not late[i], arrive)
+        if t == lag:
+            each(levels[0], lambda i, t: late[i], onward)
+        part(t)
+        if t <= ns:
+            each(levels[t - 1], lambda i, t: relay[i] and in_plane(i, t), lambda i, b, t, way: pass_on(i, b))
+        if 1 <= t - lag:
+            each(levels[t - lag], lambda i, t: late[i], arrive)
+    each(steps, lambda i, t: in_plane(i, t) and not direct[i], lambda i, b, t, way: settle(i, b))
+    each(levels[0] + straight, lambda i, t: direct[i], lambda i, b, t, way: settle(i, b))
+    each(steps, lambda i, t: (t == 0 or in_z(i)) and not direct[i], finish)
+    each(levels[0] + straight, lambda i, t: direct[i], finish)
+
+
+def gather(collective, mesh_shape, items, work=None, work_args=(), work_out=None):
     ns, nd = mesh_shape["shard"], mesh_shape["dp"]
     modes = tuple(mode for _, mode in items)
-    lead = {"z": (ns,), "plane": (nd,), "all": (ns, nd, 2), "swap": (), "spread": ()}
+    lead = {"z": (ns,), "plane": (nd,), "all": (ns, nd, 2), "swap": ()}
     shapes = [jax.ShapeDtypeStruct(lead[mode] + a.shape, a.dtype) for a, mode in items]
     sems = []
     dma = pltpu.SemaphoreType.DMA
@@ -266,15 +273,17 @@
         sems += [dma((2, ns)), dma((ns,)), dma((ns, max(nd, 6))), dma((ns, nd, 2)), dma((ns, nd)), dma((ns, nd)),
                  dma(())]
     return pl.pallas_call(
-        partial(gather_kernel, ns, nd, modes),
-        out_shape=shapes,
-        in_specs=[pl.BlockSpec(memory_space=pl.ANY)] * len(items),
-        out_specs=[pl.BlockSpec(memory_space=pl.ANY)] * len(items),
+        partial(gather_kernel, ns, nd, modes, work, len(work_args)),
+        out_shape=shapes + ([work_out] if work else []),
+        in_specs=[pl.BlockSpec(memory_space=pl.ANY)] * len(items)
+        + [pl.BlockSpec(memory_space=pltpu.VMEM)] * len(work_args),
+        out_specs=[pl.BlockSpec(memory_space=pl.ANY)] * len(items)
+        + ([pl.BlockSpec(memory_space=pltpu.VMEM)] if work else []),
         scratch_shapes=sems,
         compiler_params=pltpu.CompilerParams(
             collective_id=collective, has_side_effects=True, vmem_limit_bytes=VMEM_LIMIT),
         cost_estimate=pl.CostEstimate(flops=0, bytes_accessed=1 << 20, transcendentals=0),
-    )(*[a for a, _ in items])
+    )(*[a for a, _ in items], *work_args)
 
 
 def reduce_kernel(ns, nd, share, spans, *refs):
@@ -291,7 +300,16 @@
     if relay:
         x, y, across = square(d)
         peers = [across, x, y]
-    order = [lax.rem(s + k, ns) for k in sorted(range(1, ns), key=lambda k: abs(k - ns // 2))] + [s]
+    chain = bool(spans)
+    if chain:
+        order = []
+        for k in range(ns - 1):
+            up = jnp.where(k < ns - 1 - s, ns - 1 - k, k - (ns - 1 - s))
+            down = jnp.where(k < s, k, ns - 1 - (k - s))
+            order.append(jnp.where(2 * s < ns, up, down))
+        order.append(s)
+    else:
+        order = [lax.rem(s + k, ns) for k in sorted(range(1, ns), key=lambda k: abs(k - ns // 2))] + [s]
     items = [(a, k, order[k]) for k in range(ns) for a in range(count)]
 
     def score(a, k, b):
@@ -409,9 +427,37 @@
             def store(at, v):
                 mid[a, b, at] = v
             sum_rows(0, h, plane_terms(a, b), store)
-            zcopy(a, b, s).start()
-
-    stages = [zero, one, two, three]
+            if not chain:
+                zcopy(a, b, s).start()
+
+    def hop(a, b, way):
+        slot = jnp.where(s + way == b, jnp.where(way > 0, b, ns), b)
+        return pltpu.make_async_remote_copy(
+            mid.at[a, b], zgot.at[a, slot], zs.at[a, b], zr.at[a, slot],
+            device_id={"shard": s + way}, device_id_type=MESH)
+
+    def came(a, slot):
+        return pltpu.make_async_remote_copy(
+            mid.at[a, s], zgot.at[a, slot], zs.at[a, s], zr.at[a, slot], device_id={"mp": 1 - m},
+            device_id_type=MESH)
+
+    def four(a, k, b):
+        if k == ns - 1:
+            return
+
+        def add():
+            came(a, b).wait_recv()
+
+            def store(at, v):
+                mid[a, b, at] = v
+            sum_rows(0, h, [lambda at: mid[a, b, at], lambda at: zgot[a, b, at]], store)
+
+        upward = b > s
+        pl.when(jnp.where(upward, s > 0, s < ns - 1))(add)
+        pl.when(upward)(lambda: hop(a, b, 1).start())
+        pl.when(jnp.logical_not(upward))(lambda: hop(a, b, -1).start())
+
+    stages = [zero, one, two, three] + ([four] if chain else [])
     if not spans:
         for item in items:
             zero(*item)
@@ -430,13 +476,22 @@
 
     others = order[:-1]
     for a in range(count):
-        for b in others:
-            zcopy(a, b, b).wait_recv()
-
         def store(at, v, a=a):
             fin[a, at] = v
 
-        sum_rows(0, h, plane_terms(a, s) + [lambda at, b=b: zgot[a, b, at] for b in others], store)
+        if chain:
+            sum_rows(0, h, plane_terms(a, s), store)
+            for slot, ok in ((s, s > 0), (ns, s < ns - 1)):
+
+                def add(slot=slot):
+                    came(a, slot).wait_recv()
+                    sum_rows(0, h, [lambda at: fin[a, at], lambda at: zgot[a, slot, at]], store)
+
+                pl.when(ok)(add)
+        else:
+            for b in others:
+                zcopy(a, b, b).wait_recv()
+            sum_rows(0, h, plane_terms(a, s) + [lambda at, b=b: zgot[a, b, at] for b in others], store)
         if share:
             give_out(a, m).start()
         keep(a).start()
@@ -492,16 +547,224 @@
             pltpu.VMEM(give, BF16),
             pltpu.VMEM((count, ns, slots, h, c), BF16),
             pltpu.VMEM((count, ns, h, c), BF16),
-            pltpu.VMEM((count, ns, h, c), BF16),
+            pltpu.VMEM((count, ns + 1, h, c), BF16),
             pltpu.VMEM((count, h, c), BF16),
             dma((count, ns)), dma((count, ns)), dma((count, ns)),
             dma((count, ns, max(nd, 4))), dma((count, ns, max(nd, 4))),
-            dma((count, ns)), dma((count, ns)), dma((count,)), dma((count,)), dma((count,)),
+            dma((count, ns)), dma((count, ns + 1)), dma((count,)), dma((count,)), dma((count,)),
         ],
         compiler_params=pltpu.CompilerParams(
             collective_id=collective, has_side_effects=True, vmem_limit_bytes=VMEM_LIMIT),
         cost_estimate=pl.CostEstimate(flops=0, bytes_accessed=1 << 20, transcendentals=0),
     )(*args)
+
+
+def gelu_both(v):
+    root, cube = 0.7978845608028654, 0.044715
+    t = jnp.tanh(root * (v + cube * v * v * v))
+    slope = 0.5 * (1.0 + t) + 0.5 * v * (1.0 - t * t) * (root * (1.0 + 3.0 * cube * v * v))
+    return 0.5 * v * (1.0 + t), slope
+
+
+def feed_kernel(ns, nd, x, cot, w, act, low, grad, hid, cots, acc, zs, zr, ps, pr, cs, cr, ls, ks):
+    s, d, m = (lax.axis_index(a) for a in ("shard", "dp", "mp"))
+    h, width = x.shape
+    units = w.shape[1] // 3
+    relay = nd == 4 and h % 32 == 0
+    greet(ns, nd, True, True, True, z_all=True)
+    turns = [0] + sorted(range(1, ns), key=lambda k: min(k, ns - k))
+    order = [lax.rem(s + k, ns) for k in turns]
+    peers = [lax.rem(d + k, nd) for k in range(1, nd)]
+    if relay:
+        xn, yn, across = square(d)
+        peers = [xn, yn, across]
+
+    def zsend(b):
+        return pltpu.make_async_remote_copy(
+            x, hid.at[s, d, m], zs.at[b], zr.at[s], device_id={"shard": b}, device_id_type=MESH)
+
+    def zrecv(b):
+        return pltpu.make_async_remote_copy(
+            x, hid.at[b, d, m], zs.at[b], zr.at[b], device_id={"shard": b}, device_id_type=MESH)
+
+    def part(ref, k):
+        return ref if k is None else ref.at[pl.ds(k * (h // 2), h // 2)]
+
+    def source(b, e, first):
+        return x if first else hid.at[b, e, m]
+
+    def psend(b, e, to, slot, k, first):
+        return pltpu.make_async_remote_copy(
+            part(source(b, e, first), k), part(hid.at[b, e, m], k), ps.at[b, slot], pr.at[b, e, k or 0],
+            device_id={"dp": to}, device_id_type=MESH)
+
+    def precv(b, e, k):
+        ref = part(hid.at[b, e, m], k)
+        return pltpu.make_async_remote_copy(
+            ref, ref, ps.at[b, 0], pr.at[b, e, k or 0], device_id={"dp": peers[0]}, device_id_type=MESH)
+
+    def own_sends(b, first):
+        if relay:
+            return [psend(b, d, xn, 0, 0, first), psend(b, d, yn, 1, 1, first),
+                    psend(b, d, xn, 2, 1, first), psend(b, d, yn, 3, 0, first)]
+        return [psend(b, d, e, j, None, first) for j, e in enumerate(peers)]
+
+    def pass_sends(b):
+        if relay:
+            return [(precv(b, xn, 0), psend(b, xn, yn, 4, 0, False)),
+                    (precv(b, yn, 1), psend(b, yn, xn, 5, 1, False))]
+        return []
+
+    def share(b, e, core, first=False):
+        ref = hid.at[b, e, core]
+        return pltpu.make_async_remote_copy(
+            x if first else ref, ref, cs.at[b, e], cr.at[b, e], device_id={"mp": 1 - m}, device_id_type=MESH)
+
+    def load(b):
+        return pltpu.make_async_copy(cot.at[b], cots.at[b], ls.at[b])
+
+    def begin(k):
+        b = order[k]
+        if k > 0:
+            zrecv(b).wait_recv()
+        for c in own_sends(b, k == 0):
+            c.start()
+        share(b, d, m, k == 0).start()
+
+    def hand_on(k):
+        for got, on in pass_sends(order[k]):
+            got.wait_recv()
+            on.start()
+
+    def settle(k):
+        b = order[k]
+        for e in peers:
+            for q in waits(e):
+                precv(b, e, q).wait_recv()
+            share(b, e, m).start()
+
+    def waits(e):
+        if not relay:
+            return [None]
+        return [1] if e is xn else [0] if e is yn else [0, 1]
+
+    def ready(k):
+        b = order[k]
+        for e in [d] + peers:
+            share(b, e, 1 - m).wait_recv()
+        if k == 0:
+            keep.wait()
+        load(b).wait()
+
+    count = nd // 2 if nd % 2 == 0 else nd
+
+    def forward(k, q):
+        b = order[k]
+        at = pl.ds(q * count, count)
+        rows = count * 2 * h
+        pre = product(hid[b, at].reshape(rows, width), w[:, : 2 * units])
+        back = product(cots[b, at].reshape(rows, width), w[:, 2 * units :])
+        value, slope = gelu_both(pre[:, :units])
+        up = pre[:, units:]
+        act[b, at] = (value * up).astype(BF16).reshape(count, 2, h, units)
+        low[b, at, :, :, :units] = (back * up * slope).astype(BF16).reshape(count, 2, h, units)
+        low[b, at, :, :, units:] = (back * value).astype(BF16).reshape(count, 2, h, units)
+
+    def backward(k):
+        b = order[k]
+        rows = nd * 2 * h
+        step = 512 if width % 512 == 0 else 128
+        lows = low[b].reshape(rows, 2 * units)
+        acts = act[b].reshape(rows, units)
+
+        @pl.loop(0, width // step)
+        def _(j):
+            at = pl.ds(pl.multiple_of(j * step, step), step)
+            one = rows_product(hid[b, :, :, :, at].reshape(rows, step), lows)
+            two = rows_product(cots[b, :, :, :, at].reshape(rows, step), acts)
+            if k > 0:
+                one = one + acc[at, : 2 * units]
+                two = two + acc[at, 2 * units :]
+            if k < ns - 1:
+                acc[at, : 2 * units] = one
+                acc[at, 2 * units :] = two
+            else:
+                grad[at, : 2 * units] = one.astype(BF16)
+                grad[at, 2 * units :] = two.astype(BF16)
+
+    for b in order[1:]:
+        zsend(b).start()
+    keep = pltpu.make_async_copy(x, hid.at[s, d, m], ks)
+    keep.start()
+    begin(0)
+    for b in order:
+        load(b).start()
+    if ns > 1:
+        begin(1)
+    hand_on(0)
+    if ns > 2:
+        begin(2)
+    for k in range(ns):
+        settle(k)
+        ready(k)
+        forward(k, 0)
+        if k + 1 < ns:
+            hand_on(k + 1)
+        if k + 3 < ns:
+            begin(k + 3)
+        if count < nd:
+            forward(k, 1)
+        backward(k)
+    for k, b in enumerate(order):
+        for c in own_sends(b, k == 0):
+            c.wait_send()
+        for _, c in pass_sends(b):
+            c.wait_send()
+        for e in [d] + peers:
+            share(b, e, m).wait_send()
+        if k > 0:
+            zsend(b).wait_send()
+
+
+def feed(collective, mesh_shape, x, cot, w):
+    ns, nd = mesh_shape["shard"], mesh_shape["dp"]
+    h, width = x.shape
+    units = w.shape[1] // 3
+    rows = (ns, nd, 2, h)
+    if 2 * cot.size * 2 > (24 << 20):
+        (hid,) = gather(collective, mesh_shape, [(x, "all")])
+        hid, cot = hid.reshape(-1, width), cot.reshape(-1, width)
+        pre = product(hid, w[:, : 2 * units])
+        back = product(cot, w[:, 2 * units :])
+        value, slope = gelu_both(pre[:, :units])
+        up = pre[:, units:]
+        act = (value * up).astype(BF16)
+        low = jnp.concatenate([back * up * slope, back * value], axis=1).astype(BF16)
+        grad = jnp.concatenate([rows_product(hid, low), rows_product(cot, act)], axis=1).astype(BF16)
+        return act, low, grad
+    dma = pltpu.SemaphoreType.DMA
+    vmem = pl.BlockSpec(memory_space=pltpu.VMEM)
+    act, low, grad = pl.pallas_call(
+        partial(feed_kernel, ns, nd),
+        out_shape=[
+            jax.ShapeDtypeStruct(rows + (units,), BF16),
+            jax.ShapeDtypeStruct(rows + (2 * units,), BF16),
+            jax.ShapeDtypeStruct((width, 3 * units), BF16),
+        ],
+        in_specs=[vmem, pl.BlockSpec(memory_space=pl.ANY), vmem],
+        out_specs=[vmem] * 3,
+        scratch_shapes=[
+            pltpu.VMEM(rows + (width,), BF16),
+            pltpu.VMEM(rows + (width,), BF16),
+            pltpu.VMEM((width, 3 * units), F32),
+            dma((ns,)), dma((ns,)), dma((ns, max(nd, 6))), dma((ns, nd, 2)), dma((ns, nd)), dma((ns, nd)),
+            dma((ns,)), dma(()),
+        ],
+        compiler_params=pltpu.CompilerParams(
+            collective_id=collective, has_side_effects=True, vmem_limit_bytes=VMEM_LIMIT),
+        cost_estimate=pl.CostEstimate(flops=0, bytes_accessed=1 << 20, transcendentals=0),
+    )(x, cot, w)
+    return act.reshape(-1, units), low.reshape(-1, 2 * units), grad
 
 
 def plane_kernel(ns, nd, p, out, own, sib, ls, ss, sr, ps, pr, fs, fr, ks):
@@ -603,32 +866,21 @@
     return jnp.dot(left_side, right_side, preferred_element_type=F32)
 
 
-def pack_kernel(full, gateup, down, out):
-    units = down.shape[1]
-    here = pl.program_id(0) < full
-
-    def keep(v):
-        return jnp.where(here, v, jnp.zeros_like(v)).astype(BF16)
-
-    out[0, :, :units] = keep(gateup[:, 0, :].astype(F32))
-    out[0, :, units : 2 * units] = keep(gateup[:, 1, :].astype(F32))
-    out[0, :, 2 * units :] = keep(down[...].astype(F32))
-
-
-def pack(n, units, gateup_weight, down_cols):
-    own_d, _, ff_local = gateup_weight.shape
-    full = ff_local // units
-    return pl.pallas_call(
-        partial(pack_kernel, full),
-        out_shape=jax.ShapeDtypeStruct((n, own_d, 3 * units), BF16),
-        grid=(n,),
-        in_specs=[
-            pl.BlockSpec((own_d, 2, units), lambda j: (0, 0, jnp.minimum(j, full - 1))),
-            pl.BlockSpec((own_d, units), lambda j: (0, jnp.minimum(j, full - 1))),
-        ],
-        out_specs=pl.BlockSpec((1, own_d, 3 * units), lambda j: (j, 0, 0)),
-        compiler_params=pltpu.CompilerParams(vmem_limit_bytes=VMEM_LIMIT),
-    )(gateup_weight, down_cols)
+def pack(part, parts, ins, outs):
+    gateup, down = ins
+    (out,) = outs
+    n, _, columns = out.shape
+    units = columns // 3
+    full = down.shape[1] // units
+    share = -(-n // parts)
+    for j in range(part * share, min((part + 1) * share, n)):
+        if j >= full:
+            out[j] = jnp.zeros(out.shape[1:], BF16)
+            continue
+        at = pl.ds(j * units, units)
+        out[j, :, :units] = gateup[:, 0, at]
+        out[j, :, units : 2 * units] = gateup[:, 1, at]
+        out[j, :, 2 * units :] = down[:, at]
 
 
 def adam_step(rates, grad, weight, first, second, decay):
@@ -711,8 +963,6 @@
     plane_tok = nd * tok
     plane_d = ns * own_d
 
-    three = pack(n, units, gateup_weight, down_weight.T)
-
     input_rows = tokens_in.astype(F32)
     inverse_one = lax.rsqrt(jnp.mean(input_rows * input_rows, axis=1) + EPS_NORM)
     lanes = max(256, -(-max(own_d, tok) // 128) * 128)
@@ -729,16 +979,15 @@
     def plane_cut(value):
         return value.reshape(tok, ns, nd, own_d).transpose(2, 0, 1, 3).reshape(nd, tok, plane_d)
 
-    small_all, tokens_plane, cot_all, qkv_plane = gather(
+    small_all, tokens_plane, cot_all, qkv_plane, three = gather(
         0, mesh_shape,
         [(small, "all"), (plane_cut(tokens_in), "swap"),
-         (lax.dynamic_slice_in_dim(block_cotangent, m * half, half, 0), "all"), (qkv_weight, "z")])
+         (lax.dynamic_slice_in_dim(block_cotangent, m * half, half, 0), "all"), (qkv_weight, "z")],
+        pack, (gateup_weight, down_weight.T), jax.ShapeDtypeStruct((n, own_d, 3 * units), BF16))
     tokens_plane = tokens_plane.reshape(plane_tok, plane_d)
     three, tokens_plane = lax.optimization_barrier((three, tokens_plane))
     three = lax.all_to_all(three, TOK, 0, 0, tiled=True).reshape(width, 3 * units)
-    gateup_mine, down_mine = three[:, : 2 * units], three[:, 2 * units :]
     qkv_plane = qkv_plane.reshape(plane_d, q_cols + HEAD_DIM)
-    cot_all = cot_all.reshape(n * tok, width)
     small_all = small_all[:, :, 0]
     gains_by = small_all[:, :, :2, :own_d]
     full_gains = gains_by.transpose(2, 0, 1, 3).reshape(2, width)
@@ -746,9 +995,6 @@
     plane_scale = lax.dynamic_index_in_dim(small_all[:, :, 3, :tok], s, 0, False).reshape(plane_tok, 1)
     plane_gain = lax.dynamic_index_in_dim(gains_by[:, :, 0], d, 1, False).reshape(1, plane_d)
 
-    def to_plane(collective, value):
-        (got,) = gather(collective, mesh_shape, [(plane_cut(value), "swap")])
-        return got.reshape(plane_tok, plane_d)
 
     def from_plane(collective, value):
         got = plane_reduce(collective, mesh_shape, value.reshape(nd, 2, half, plane_d))
@@ -801,19 +1047,9 @@
     gain_two = full_gains[1]
     inverse_two = lax.rsqrt(jnp.mean(residual * residual, axis=1, keepdims=True) + EPS_NORM)
     hidden_two = (residual * inverse_two * gain_two).astype(BF16)
-    (hidden_all,) = gather(
-        3, mesh_shape, [(lax.dynamic_slice_in_dim(hidden_two, m * half, half, 0), "all")])
-    hidden_all = hidden_all.reshape(n * tok, width)
-
-    gateup_pre = product(hidden_all, gateup_mine)
-    gate_pre, up_pre = gateup_pre[:, :units], gateup_pre[:, units:]
-    gelu_val, gelu_pull = jax.vjp(partial(jax.nn.gelu, approximate=True), gate_pre)
-    act_low = (gelu_val * up_pre).astype(BF16)
-    act_grad = product(cot_all, down_mine)
-    gateup_low = jnp.concatenate(
-        [gelu_pull(act_grad * up_pre)[0], act_grad * gelu_val], axis=1).astype(BF16)
-    three_grad = jnp.concatenate(
-        [rows_product(hidden_all, gateup_low).astype(BF16), rows_product(cot_all, act_low).astype(BF16)], axis=1)
+
+    act_low, gateup_low, three_grad = feed(
+        3, mesh_shape, lax.dynamic_slice_in_dim(hidden_two, m * half, half, 0), cot_all, three)
     three_grad, act_low, gateup_low = lax.optimization_barrier((three_grad, act_low, gateup_low))
     three_grad = lax.all_to_all(three_grad.reshape(n, own_d, 3 * units), TOK, 0, 0, tiled=True)
     hidden_two_grad, ffn_sum = reduce_scatter(
@@ -831,7 +1067,12 @@
 
     residual_from, gain_two_grad = norm_back(residual, inverse_two, gain_two, hidden_two_grad)
     residual_grad = block_cotangent.astype(F32) + residual_from
-    attn_low = to_plane(10, residual_grad.astype(BF16))
+    gain_cut = gain_two_grad.reshape(1, ns, nd, own_d).transpose(2, 0, 1, 3).reshape(nd, 1, plane_d)
+    attn_low, gain_two_part = gather(
+        10, mesh_shape,
+        [(plane_cut(residual_grad.astype(BF16)), "swap"), (jnp.pad(gain_cut, ((0, 0), (0, 7), (0, 0))), "swap")])
+    attn_low = attn_low.reshape(plane_tok, plane_d)
+    gain_two_part = jnp.where(m == 0, jnp.sum(gain_two_part[:, 0], axis=0), 0.0)
     mixed_grad = plane_sum(11, product(attn_low, outproj_plane).astype(BF16))
     mixed_grad = mixed_grad.astype(BF16).reshape(tok, heads_local, HEAD_DIM)
 
@@ -861,23 +1102,25 @@
     qkv_low = jnp.concatenate([query_low, kv_low], axis=1).astype(BF16)
     (qkv_low_plane,) = gather(7, mesh_shape, [(qkv_low, "plane")])
     qkv_low_plane = qkv_low_plane.reshape(plane_tok, q_cols + HEAD_DIM)
-    hidden_one_grad = from_plane(12, cols_product(qkv_low_plane, qkv_plane).astype(BF16))
-    qkv_grad = rows_product(hidden_plane, qkv_low_plane).astype(BF16)
-    own_qkv = z_sum(qkv_grad.reshape(ns, own_d, q_cols + HEAD_DIM))
+    hidden_one_part = cols_product(qkv_low_plane, qkv_plane).astype(BF16)
+    gain_one_part = jnp.sum(hidden_one_part.astype(F32) * (tokens_plane.astype(F32) * plane_scale), axis=0)
+    hidden_one_grad = from_plane(12, hidden_one_part)
+    gain_parts = jnp.stack([gain_one_part, gain_two_part], axis=1)
+    qkv_grad = jnp.concatenate(
+        [rows_product(hidden_plane, qkv_low_plane), jnp.pad(gain_parts, ((0, 0), (0, 126)))], axis=1).astype(BF16)
+    qkv_grad, own_outproj = lax.optimization_barrier((qkv_grad, own_outproj))
+    own_qkv = z_sum(qkv_grad.reshape(ns, own_d, -1))
     own_query = own_qkv[:, :q_cols]
-    kv_own = own_qkv[:, q_cols:]
-    kv_other = lax.ppermute(kv_own, "mp", [(0, 1), (1, 0)])
+    rest = own_qkv[:, q_cols:]
+    rest_other = lax.ppermute(rest, "mp", [(0, 1), (1, 0)])
+    kv_own, kv_other = rest[:, :HEAD_DIM], rest_other[:, :HEAD_DIM]
     own_keyval = jnp.where(
         m == 0, jnp.concatenate([kv_own, kv_other], axis=1), jnp.concatenate([kv_other, kv_own], axis=1))
+    own_gains = (rest + rest_other)[:, HEAD_DIM : HEAD_DIM + 2].T
 
     inverse_col = inverse_one[:, None]
-    input_from, gain_one_grad = norm_back(input_rows, inverse_col, full_gains[0], hidden_one_grad)
+    input_from, _ = norm_back(input_rows, inverse_col, full_gains[0], hidden_one_grad)
     input_grad = residual_grad + input_from
-    gains_cut = jnp.stack([gain_one_grad, gain_two_grad], axis=0).reshape(2, n, own_d).transpose(1, 0, 2)
-    gains_cut = jnp.pad(gains_cut, ((0, 0), (0, 6), (0, lanes - own_d)))
-    (gains_got,) = gather(13, mesh_shape, [(gains_cut, "spread")])
-    own_gains = jnp.sum(gains_got[:, :2, :own_d], axis=0)
-
     step_value = step_count[0].astype(F32)
     bias_first = 1.0 - jnp.power(BETA_ONE, step_value)
     bias_second = 1.0 - jnp.power(BETA_TWO, step_value)

time: 762 us -> 707 us (0.928)
  matrix products: 77 us -> 42.4 us
  starting transfers between devices: 47.9 us -> 37 us
  local copies, waits for them, and re-layouts: 50.1 us -> 42.4 us
    dot_general x4 -> x2, matrix products: 25.9 us -> 6.49 us  [product(): return jnp.dot(left_side, right_side, preferred_element_type=F32)]
    dot_general x4 -> x2, matrix products: 19.8 us -> 6.65 us  [rows_product(): lax.dot_general(left_side, right_side, (((0,), (0,)), ((), ())), preferre...]
    optimization_barrier x3 -> x0, local copies, waits for them, and re-layouts: 12.4 us -> none  [shards(): lax.optimization_barrier((three_grad, act_low, gateup_low))]
    all_to_all x1, starting transfers between devices: 18.8 us -> 7.5 us  [shards(): lax.all_to_all(three_grad.reshape(n, own_d, 3 * units), TOK, 0, 0, tiled=...]
    pallas_call x10 -> x8, Pallas kernels: 325 us -> 326 us  [the longest x7 253 us: gather(): pl.pallas_call(partial(gather_kernel, ns, nd, modes, work, len(work_args)...]
  transfers between devices with their start and end apart: 5 -> 5, of which waited for: 0 -> 1; matrix products, arithmetic and copies ran while one was open for 16% -> 15% of each run, Pallas kernels for 61% -> 55%
where the time goes in v3:
time: 707 us; the launch traced here: 697 us
  Pallas kernels  528 us (75%)
  local copies, waits for them, and re-layouts  42.4 us (6%)
  matrix products  42.4 us (6%)
  other arithmetic  42.3 us (6%)
  starting transfers between devices  37 us (5%)
    pallas_call x7, Pallas kernels, gather(): pl.pallas_call(partial(gather_kernel, ns, nd, modes, work, len(work_args)...  253 us
    pallas_call x2, Pallas kernels, reduce_scatter(): pl.pallas_call(partial(reduce_kernel, ns, nd, share, spans), out_shape=[j...  156 us
    pallas_call x1, Pallas kernels, feed(): pl.pallas_call(partial(feed_kernel, ns, nd), out_shape=[jax.ShapeDtypeStr...  73 us
    pallas_call x1, Pallas kernels, unpack_adam(): pl.pallas_call(unpack_kernel, out_shape=[shape3] * 4 + [shape2] * 4, grid...  26.3 us
    pallas_call x2, Pallas kernels, plane_reduce(): pl.pallas_call(partial(plane_kernel, ns, nd), out_shape=jax.ShapeDtypeStr...  20.7 us
    all_to_all x1, starting transfers between devices, shards(): lax.all_to_all(three, TOK, 0, 0, tiled=True).reshape(width, 3 * units)  15.3 us
  transfers between devices with their start and end apart: 5, of which 1 were waited for; matrix products, arithmetic and copies ran while one was open for 15% of the time, Pallas kernels for 55%

profile of v3, /device:TPU:14, one launch (start us, length us, event | category | flops | bytes accessed | tf_op | source)
XLA Modules:
  0.0 696.8 jit_solution(6285586910151007532)
XLA Ops:
  7.5 68.8 %shard_map.413 = (f32[4,4,2,8,256]{4,3,2,1,0:T(8,128)}, bf16[4,128,640]{2,1,0:T(8,128)(2,1)}, bf16[4,4,2,64,2560]{4,3,2,1,0:T(8,128)(2,1)}, bf16[4,160,1536]{2,1,0:T(8,128)(2,1)}, bf16[16,160,768]{2,1,0:T(8,128)(2,1)}) custom-call(f32[8,256]{1,0:T(8,128)} %fusion.69.refs_0_, bf16[4,128,640]{2,1,0:T(8,128)(2,1)} %copy.156.refs_1_, ...), custom_call_target="tpu_custom_call" | custom-call | bytes 1048576 | tf_op jit(solution)/shard_map/pallas_call | solution.py:275
  76.4 15.3 %all-to-all-start = ((bf16[16,160,768]{2,1,0:T(8,128)(2,1)}), bf16[16,160,768]{2,1,0:T(8,128)(2,1)}, u32[]{:S(2)}, u32[]{:S(2)}) async-start(bf16[16,160,768]{2,1,0:T(8,128)(2,1)} %get-tuple-element.65), calls=%async_computation | async-start | bytes 7864320 | tf_op jit(solution)/shard_map/all_to_all | solution.py:989
  94.6 37.6 %shard_map.414 = bf16[4,128,1536]{2,1,0:T(8,128)(2,1)} custom-call(bf16[4,128,1536]{2,1,0:T(8,128)(2,1)} %bitcast.215), custom_call_target="tpu_custom_call" | custom-call | bytes 1048576 | tf_op jit(solution)/shard_map/pallas_call | solution.py:275
  135.7 63.9 %shard_map.415 = bf16[4,4,2,128,256]{4,3,2,1,0:T(8,128)(2,1)} custom-call(bf16[128,256]{1,0:T(8,128)(2,1)} %fusion.54.refs_0_), custom_call_target="tpu_custom_call" | custom-call | bytes 1048576 | tf_op jit(solution)/shard_map/pallas_call | solution.py:275
  206.0 34.2 %shard_map.416 = (bf16[4,128,1280]{2,1,0:T(8,128)(2,1)}, bf16[4,160,1280]{2,1,0:T(8,128)(2,1)}) custom-call(bf16[128,1280]{1,0:T(8,128)(2,1)} %copy.163.refs_0_, bf16[160,1280]{1,0:T(8,128)(2,1)} %bitcast.213), custom_call_target="tpu_custom_call" | custom-call | bytes 1048576 | tf_op jit(solution)/shard_map/pallas_call | solution.py:275
  240.2 3.9 convolution_convert_fusion.4
  244.1 10.7 %shard_map.417 = bf16[4,2,64,640]{3,2,1,0:T(8,128)(2,1)} custom-call(bf16[4,2,64,640]{3,2,1,0:T(8,128)(2,1)} %bitcast.221), custom_call_target="tpu_custom_call" | custom-call | bytes 1048576 | tf_op jit(solution)/shard_map/pallas_call | solution.py:828
  254.7 2.8 reshape.412
  261.8 73.0 %shard_map.418 = (bf16[4,4,2,64,256]{4,3,2,1,0:T(8,128)(2,1)}, bf16[4,4,2,64,512]{4,3,2,1,0:T(8,128)(2,1)}, bf16[2560,768]{1,0:T(8,128)(2,1)}) custom-call(bf16[64,2560]{1,0:T(8,128)(2,1)} %fusion.49.x, bf16[4,4,2,64,2560]{4,3,2,1,0:T(8,128)(2,1)} %get-tuple-element.64.cot, bf16[2560,768]{1,0:T(8,128)(2,1)} %bitcast.28.w.refs_2_), custom_call_target="tpu_custom_call" | custom-call | bytes 1048576 | tf_op jit(solution)/shard_map/pallas_call | solution.py:747
  334.8 7.5 %all-to-all-start.1 = ((bf16[16,160,768]{2,1,0:T(8,128)(2,1)}), bf16[16,160,768]{2,1,0:T(8,128)(2,1)}, u32[]{:S(2)}, u32[]{:S(2)}) async-start(bf16[16,160,768]{2,1,0:T(8,128)(2,1)} %bitcast.202), calls=%async_computation.1 | async-start | bytes 7864320 | tf_op jit(solution)/shard_map/all_to_all | solution.py:1054
  342.6 3.6 fusion.9
  346.1 135.1 %shard_map.419 = (bf16[2,64,2560]{2,1,0:T(8,128)(2,1)}, bf16[2,64,2560]{2,1,0:T(8,128)(2,1)}) custom-call(bf16[4,4,2,64,512]{4,3,2,1,0:T(8,128)(2,1)} %get-tuple-element.68, bf16[4,4,2,64,256]{4,3,2,1,0:T(8,128)(2,1)} %get-tuple-element.67, bf16[2560,768]{1,0:T(8,128)(2,1)} %bitcast.28.w.refs_2_), custom_call_target="tpu_custom_call" | custom-call | bytes 1048576 | tf_op jit(solution)/shard_map/pallas_call | solution.py:539
  491.3 13.9 %shard_map.420 = (bf16[4,128,640]{2,1,0:T(8,128)(2,1)}, f32[4,8,640]{2,1,0:T(8,128)}) custom-call(bf16[4,128,640]{2,1,0:T(8,128)(2,1)} %copy.169.refs_0_, f32[4,8,640]{2,1,0:T(8,128)} %pad.25.refs_1_), custom_call_target="tpu_custom_call" | custom-call | bytes 1048576 | tf_op jit(solution)/shard_map/pallas_call | solution.py:275
  505.2 3.9 convolution_convert_fusion.1
  509.1 18.3 %shard_map.421 = bf16[4,128,1280]{2,1,0:T(8,128)(2,1)} custom-call(bf16[4,128,1280]{2,1,0:T(8,128)(2,1)} %bitcast.218), custom_call_target="tpu_custom_call" | custom-call | bytes 1048576 | tf_op jit(solution)/shard_map/pallas_call | solution.py:275
  531.6 3.0 fusion.43
  536.8 7.3 %fusion.12 = bf16[1152,256]{1,0:T(8,128)(2,1)} fusion(f32[5,128,1152]{1,2,0:T(8,128)} %convolution_bitcast_fusion.1, bf16[128,5,128]{2,0,1:T(8,128)(2,1)} %copy-done.35, bf16[128,5,128]{2,0,1:T(8,128)(2,1)} %copy-done.34, f32[1152,128,5]{1,0,2:T(8,128)} %copy-done.1, f32[5,128]{1,0:T(8,128)S(1)} %copy-done.44, f32[5,128]{1,0:T(8,128)S(1)} %copy-done.42, ...), kind=kOutput, calls=%fused_computation.29 | convolution fusion | flops 386549504 | bytes 6968320 | tf_op jit(solution)/shard_map/htk,thd->kd/dot_general | solution.py:1092
  547.0 20.4 %shard_map.422 = bf16[128,256]{1,0:T(8,128)(2,1)} custom-call(bf16[4,4,2,128,256]{4,3,2,1,0:T(8,128)(2,1)} %bitcast.193), custom_call_target="tpu_custom_call" | custom-call | bytes 1048576 | tf_op jit(solution)/shard_map/pallas_call | solution.py:539
  568.9 7.6 %fusion.40 = f32[128,5,256]{2,0,1:T(8,128)} fusion(bf16[1152,256,1]{1,0,2:T(8,128)(2,1)} %bitcast.224, f32[5,128,1152]{1,2,0:T(8,128)} %convolution_bitcast_fusion.1, f32[1152,128,5]{1,0,2:T(8,128)} %copy-done.1, f32[5,128]{1,0:T(8,128)S(1)} %copy-done.44, f32[5,128]{1,0:T(8,128)S(1)} %copy-done.42, pred[128,1152]{0,1:T(8,128)(4,1)S(1)} %compare_and_fusion), kind=kOutput, calls=%fused_computation.66 | convolution fusion | flops 385599232 | bytes 7296000 | tf_op jit(solution)/shard_map/htk,kd->thd/dot_general | solution.py:1091
  576.5 3.7 fusion.6
  580.2 5.8 all-to-all-start.2
  594.2 16.1 %shard_map.423 = bf16[4,128,1536]{2,1,0:T(8,128)(2,1)} custom-call(bf16[128,1536]{1,0:T(8,128)(2,1)} %pad_maximum_fusion.2.refs_0_), custom_call_target="tpu_custom_call" | custom-call | bytes 1048576 | tf_op jit(solution)/shard_map/pallas_call | solution.py:275
  611.3 3.7 multiply_reduce_fusion.1
  615.2 2.9 convolution_convert_fusion
  621.2 2.6 convert_reduce_fusion.1
  623.8 8.0 %all-to-all-start.3 = ((bf16[4,160,1664]{2,1,0:T(8,128)(2,1)}), bf16[4,160,1664]{2,1,0:T(8,128)(2,1)}, u32[]{:S(2)}, u32[]{:S(2)}) async-start(bf16[4,160,1664]{2,1,0:T(8,128)(2,1)} %bitcast.191), calls=%async_computation.3 | async-start | bytes 4259840 | tf_op jit(solution)/shard_map/all_to_all | solution.py:1080
  633.7 10.0 %shard_map.424 = bf16[4,2,64,640]{3,2,1,0:T(8,128)(2,1)} custom-call(bf16[4,2,64,640]{3,2,1,0:T(8,128)(2,1)} %bitcast.220), custom_call_target="tpu_custom_call" | custom-call | bytes 1048576 | tf_op jit(solution)/shard_map/pallas_call | solution.py:828
  643.7 3.7 reshape.413
  647.4 2.7 copy.179
  650.1 2.8 copy.180
  654.8 3.5 fusion.33
  658.4 26.3 %shard_map.425 = (f32[160,2,3840]{2,1,0:T(2,128)}, f32[160,2,3840]{2,1,0:T(2,128)}, f32[160,2,3840]{2,1,0:T(2,128)}, f32[160,2,3840]{2,1,0:T(2,128)}, f32[160,38...) custom-call(f32[2]{0:T(128)} %pad_maximum_fusion.8.rates, ...), custom_call_target="tpu_custom_call" | custom-call | tf_op jit(solution)/shard_map/pallas_call | solution.py:912
  (255 shorter events, 71.3 us)
Async XLA Ops:
  4.0 128.2 %copy-start.45 = (f32[128]{0:T(128)}, f32[128]{0:T(128)S(1)}, u32[]{:S(2)}) copy-start(f32[128]{0:T(128)S(1)} %get-tuple-element.232) | copy-start | bytes 1540
  4.1 128.2 %copy-start.48 = (s32[128]{0:T(128)}, s32[128]{0:T(128)S(1)}, u32[]{:S(2)}) copy-start(s32[128]{0:T(128)S(1)} %get-tuple-element.238) | copy-start | bytes 1540
  76.4 15.4 %copy-start.39 = (f32[4,4,2,8,256]{4,3,2,1,0:T(8,128)S(1)}, f32[4,4,2,8,256]{4,3,2,1,0:T(8,128)}, u32[]{:S(2)}) copy-start(f32[4,4,2,8,256]{4,3,2,1,0:T(8,128)} %get-tuple-element.60) | copy-start | bytes 786436
  76.4 15.6 %copy-start.69 = (bf16[4,160,1536]{2,1,0:T(8,128)(2,1)S(1)}, bf16[4,160,1536]{2,1,0:T(8,128)(2,1)}, u32[]{:S(2)}) copy-start(bf16[4,160,1536]{2,1,0:T(8,128)(2,1)} %get-tuple-element.61) | copy-start | bytes 5898244
  76.4 15.6 %copy-start.71 = (bf16[4,128,640]{2,1,0:T(8,128)(2,1)S(1)}, bf16[4,128,640]{2,1,0:T(8,128)(2,1)}, u32[]{:S(2)}) copy-start(bf16[4,128,640]{2,1,0:T(8,128)(2,1)} %get-tuple-element.58) | copy-start | bytes 1966084
  76.4 185.4 %all-to-all-start = ((bf16[16,160,768]{2,1,0:T(8,128)(2,1)}), bf16[16,160,768]{2,1,0:T(8,128)(2,1)}, u32[]{:S(2)}, u32[]{:S(2)}) async-start(bf16[16,160,768]{2,1,0:T(8,128)(2,1)} %get-tuple-element.65), calls=%async_computation | async-start | bytes 7864320 | tf_op jit(solution)/shard_map/all_to_all | solution.py:989
  132.9 67.4 %copy-start.51 = (f32[128]{0:T(128)}, f32[128]{0:T(128)S(1)}, u32[]{:S(2)}) copy-start(f32[128]{0:T(128)S(1)} %convert_element_type.161) | copy-start | bytes 1540
  134.7 65.6 %copy-start.53 = (f32[128]{0:T(128)}, f32[128]{0:T(128)S(1)}, u32[]{:S(2)}) copy-start(f32[128]{0:T(128)S(1)} %multiply_power_fusion) | copy-start | bytes 1540
  260.5 222.3 %copy-start.30 = (f32[2560]{0:T(1024)}, f32[2560]{0:T(1024)S(1)}, u32[]{:S(2)}) copy-start(f32[2560]{0:T(1024)S(1)} %mul.452) | copy-start | bytes 30724
  260.8 222.1 %copy-start.55 = (f32[128]{0:T(128)}, f32[128]{0:T(128)S(1)}, u32[]{:S(2)}) copy-start(f32[128]{0:T(128)S(1)} %add_rsqrt_fusion) | copy-start | bytes 1540
  334.7 7.6 %copy-start.38 = (f32[1152]{0:T(1024)S(1)}, f32[1152]{0:T(1024)}, u32[]{:S(2)}) copy-start(f32[1152]{0:T(1024)} %copy-done.36) | copy-start | bytes 13828
  334.7 7.6 %copy-start.47 = (f32[128]{0:T(128)S(1)}, f32[128]{0:T(128)}, u32[]{:S(2)}) copy-start(f32[128]{0:T(128)} %copy-done.45) | copy-start | bytes 1540
  334.7 7.6 %copy-start.50 = (s32[128]{0:T(128)S(1)}, s32[128]{0:T(128)}, u32[]{:S(2)}) copy-start(s32[128]{0:T(128)} %copy-done.48) | copy-start | bytes 1540
  334.8 7.8 %copy-start.42 = (f32[5,128]{1,0:T(8,128)S(1)}, f32[5,128]{1,0:T(8,128)}, u32[]{:S(2)}) copy-start(f32[5,128]{1,0:T(8,128)} %copy-done.41) | copy-start | bytes 7684
  334.8 7.8 %copy-start.44 = (f32[5,128]{1,0:T(8,128)S(1)}, f32[5,128]{1,0:T(8,128)}, u32[]{:S(2)}) copy-start(f32[5,128]{1,0:T(8,128)} %copy-done.43) | copy-start | bytes 7684
  334.8 245.4 %all-to-all-start.1 = ((bf16[16,160,768]{2,1,0:T(8,128)(2,1)}), bf16[16,160,768]{2,1,0:T(8,128)(2,1)}, u32[]{:S(2)}, u32[]{:S(2)}) async-start(bf16[16,160,768]{2,1,0:T(8,128)(2,1)} %bitcast.202), calls=%async_computation.1 | async-start | bytes 7864320 | tf_op jit(solution)/shard_map/all_to_all | solution.py:1054
  580.2 41.0 %all-to-all-start.2 = ((bf16[4,160,1280]{2,1,0:T(8,128)(2,1)}), bf16[4,160,1280]{2,1,0:T(8,128)(2,1)}, u32[]{:S(2)}, u32[]{:S(2)}) async-start(bf16[4,160,1280]{2,1,0:T(8,128)(2,1)} %bitcast.214), calls=%async_computation.2 | async-start | bytes 3276800 | tf_op jit(solution)/shard_map/all_to_all | solution.py:1080
  590.0 21.3 %copy-start.67 = (f32[1,4,1,128]{3,2,1,0:T(1,128)S(1)}, f32[1,4,1,128]{3,2,1,0:T(1,128)}, u32[]{:S(2)}) copy-start(f32[1,4,1,128]{3,2,1,0:T(1,128)} %copy-done.66) | copy-start | bytes 6148
  591.9 19.4 %copy-start.70 = (bf16[4,160,1536]{2,1,0:T(8,128)(2,1)S(1)}, bf16[4,160,1536]{2,1,0:T(8,128)(2,1)}, u32[]{:S(2)}) copy-start(bf16[4,160,1536]{2,1,0:T(8,128)(2,1)} %get-tuple-element.61) | copy-start | bytes 5898244
  591.9 19.4 %copy-start.72 = (bf16[4,128,640]{2,1,0:T(8,128)(2,1)S(1)}, bf16[4,128,640]{2,1,0:T(8,128)(2,1)}, u32[]{:S(2)}) copy-start(bf16[4,128,640]{2,1,0:T(8,128)(2,1)} %get-tuple-element.58) | copy-start | bytes 1966084
  623.8 8.0 %copy-start.40 = (f32[4,4,160]{2,1,0:T(4,128)S(1)}, f32[4,4,160]{2,1,0:T(4,128)}, u32[]{:S(2)}) copy-start(f32[4,4,160]{2,1,0:T(4,128)} %get-tuple-element.194) | copy-start | bytes 30724
  623.8 8.9 %copy-start.58 = (bf16[2,160]{1,0:T(2,128)(2,1)S(1)}, bf16[2,160]{1,0:T(2,128)(2,1)}, u32[]{:S(2)}) copy-start(bf16[2,160]{1,0:T(2,128)(2,1)} %param.30) | copy-start | bytes 1924
  623.8 9.0 %copy-start.64 = (f32[2,160]{1,0:T(2,128)S(1)}, f32[2,160]{1,0:T(2,128)}, u32[]{:S(2)}) copy-start(f32[2,160]{1,0:T(2,128)} %param.42) | copy-start | bytes 3844
  623.8 9.1 %copy-start.65 = (f32[2,160]{1,0:T(2,128)S(1)}, f32[2,160]{1,0:T(2,128)}, u32[]{:S(2)}) copy-start(f32[2,160]{1,0:T(2,128)} %param.36) | copy-start | bytes 3844
  623.8 62.7 %all-to-all-start.3 = ((bf16[4,160,1664]{2,1,0:T(8,128)(2,1)}), bf16[4,160,1664]{2,1,0:T(8,128)(2,1)}, u32[]{:S(2)}, u32[]{:S(2)}) async-start(bf16[4,160,1664]{2,1,0:T(8,128)(2,1)} %bitcast.191), calls=%async_computation.3 | async-start | bytes 4259840 | tf_op jit(solution)/shard_map/all_to_all | solution.py:1080
  658.4 26.3 %copy-start.9 = (f32[160,1280]{1,0:T(8,128)S(1)}, f32[160,1280]{1,0:T(8,128)}, u32[]{:S(2)}) copy-start(f32[160,1280]{1,0:T(8,128)} %convert_reduce_fusion.1) | copy-start | bytes 2457604
  658.4 26.3 %copy-start.13 = (bf16[1280,160]{0,1:T(8,128)(2,1)S(1)}, bf16[1280,160]{0,1:T(8,128)(2,1)}, u32[]{:S(2)}) copy-start(bf16[1280,160]{0,1:T(8,128)(2,1)} %param.27) | copy-start | bytes 1228804
  658.4 26.4 %copy-start.18 = (f32[1280,160]{0,1:T(8,128)S(1)}, f32[1280,160]{0,1:T(8,128)}, u32[]{:S(2)}) copy-start(f32[1280,160]{0,1:T(8,128)} %param.33) | copy-start | bytes 2457604
  658.4 26.4 %copy-start.19 = (f32[1280,160]{0,1:T(8,128)S(1)}, f32[1280,160]{0,1:T(8,128)}, u32[]{:S(2)}) copy-start(f32[1280,160]{0,1:T(8,128)} %param.39) | copy-start | bytes 2457604
  688.8 6.7 copy-start.27
  688.8 6.6 copy-start.28
  688.8 2.4 collective-permute-start
  (46 other events, 122.0 us)

commit v4 on v3

--- a/solution.py
+++ b/solution.py
@@ -699,22 +699,21 @@
     begin(0)
     for b in order:
         load(b).start()
+    hand_on(0)
     if ns > 1:
         begin(1)
-    hand_on(0)
-    if ns > 2:
-        begin(2)
+        hand_on(1)
     for k in range(ns):
         settle(k)
         ready(k)
         forward(k, 0)
-        if k + 1 < ns:
-            hand_on(k + 1)
-        if k + 3 < ns:
-            begin(k + 3)
         if count < nd:
             forward(k, 1)
+        if k + 2 < ns:
+            begin(k + 2)
         backward(k)
+        if k + 2 < ns:
+            hand_on(k + 2)
     for k, b in enumerate(order):
         for c in own_sends(b, k == 0):
             c.wait_send()
@@ -866,6 +865,202 @@
     return jnp.dot(left_side, right_side, preferred_element_type=F32)
 
 
+def turn(v, cosine, sine):
+    half_dim = HEAD_DIM // 2
+    front, back = v[:, :half_dim], v[:, half_dim:]
+    return front * cosine - back * sine, back * cosine + front * sine
+
+
+def window(nd, kv, keys, values):
+    me = lax.axis_index("shard") * nd + lax.axis_index("dp")
+    tok = kv.shape[2]
+    for j in range(KV_BLOCKS + 1):
+        b = jnp.maximum(me + (j - KV_BLOCKS), 0)
+        keys[j * tok : (j + 1) * tok] = kv[b, 0]
+        values[j * tok : (j + 1) * tok] = kv[b, 1]
+
+
+def attend_kernel(nd, got, kv, allowed, cosine, sine, mixed, queries, probs, keys, values):
+    window(nd, kv, keys, values)
+    scale = HEAD_DIM ** (-0.5)
+    half_dim = HEAD_DIM // 2
+    cos, sin = cosine[...], sine[...]
+    for h in range(probs.shape[0]):
+        at = h * HEAD_DIM
+        raw = got[0, :, at : at + HEAD_DIM].astype(F32)
+        for e in range(1, got.shape[0]):
+            raw = raw + got[e, :, at : at + HEAD_DIM].astype(F32)
+        front, back = turn(raw, cos, sin)
+        queries[:, at : at + half_dim] = front.astype(BF16)
+        queries[:, at + half_dim : at + HEAD_DIM] = back.astype(BF16)
+        scores = cols_product(queries[:, at : at + HEAD_DIM], keys[...]) * scale
+        scores = jnp.where(allowed[...] > 0.0, scores, -jnp.inf)
+        raised = jnp.exp(scores - jnp.max(scores, axis=1, keepdims=True))
+        prob = raised / jnp.sum(raised, axis=1, keepdims=True)
+        probs[h] = prob
+        mixed[:, at : at + HEAD_DIM] = product(prob.astype(BF16), values[...]).astype(BF16)
+
+
+def attend(nd, heads, got, kv, allowed, cosine, sine):
+    tok = got.shape[1]
+    span = allowed.shape[1]
+    return pl.pallas_call(
+        partial(attend_kernel, nd),
+        out_shape=[
+            jax.ShapeDtypeStruct((tok, heads * HEAD_DIM), BF16),
+            jax.ShapeDtypeStruct((tok, heads * HEAD_DIM), BF16),
+            jax.ShapeDtypeStruct((heads, tok, span), F32),
+        ],
+        in_specs=[pl.BlockSpec(memory_space=pltpu.VMEM)] * 5,
+        out_specs=[pl.BlockSpec(memory_space=pltpu.VMEM)] * 3,
+        scratch_shapes=[pltpu.VMEM((span, HEAD_DIM), BF16)] * 2,
+        compiler_params=pltpu.CompilerParams(vmem_limit_bytes=VMEM_LIMIT),
+    )(got, kv, allowed, cosine, sine)
+
+
+def attend_back_kernel(nd, got, kv, queries, probs, cosine, sine, kv_grad, low, keys, values, key_sum, value_sum):
+    window(nd, kv, keys, values)
+    me = lax.axis_index("shard") * nd + lax.axis_index("dp")
+    scale = HEAD_DIM ** (-0.5)
+    half_dim = HEAD_DIM // 2
+    n, _, tok, _ = kv.shape
+    cos, sin = cosine[...], sine[...]
+    for h in range(probs.shape[0]):
+        at = h * HEAD_DIM
+        raw = got[0, :, at : at + HEAD_DIM].astype(F32)
+        for e in range(1, got.shape[0]):
+            raw = raw + got[e, :, at : at + HEAD_DIM].astype(F32)
+        mixed_grad = raw.astype(BF16)
+        prob = probs[h]
+        prob_grad = cols_product(mixed_grad, values[...])
+        inner = jnp.sum(prob * prob_grad, axis=1, keepdims=True)
+        scores_low = (prob * (prob_grad - inner) * scale).astype(BF16)
+        front, back = turn(product(scores_low, keys[...]), cos, -sin)
+        low[:, at : at + half_dim] = front.astype(BF16)
+        low[:, at + half_dim : at + HEAD_DIM] = back.astype(BF16)
+        key_part = rows_product(scores_low, queries[:, at : at + HEAD_DIM])
+        value_part = rows_product(prob.astype(BF16), mixed_grad)
+        if h == 0:
+            key_sum[...] = key_part
+            value_sum[...] = value_part
+        else:
+            key_sum[...] += key_part
+            value_sum[...] += value_part
+
+    @pl.loop(0, n)
+    def _(b):
+        kv_grad[b] = jnp.zeros(kv_grad.shape[1:], BF16)
+
+    for j in range(KV_BLOCKS + 1):
+        b = me + (j - KV_BLOCKS)
+
+        @pl.when(b >= 0)
+        def _(j=j, b=b):
+            kv_grad[b, 0] = key_sum[j * tok : (j + 1) * tok].astype(BF16)
+            kv_grad[b, 1] = value_sum[j * tok : (j + 1) * tok].astype(BF16)
+
+
+def attend_back(nd, got, kv, queries, probs, cosine, sine):
+    span = probs.shape[2]
+    return pl.pallas_call(
+        partial(attend_back_kernel, nd),
+        out_shape=[jax.ShapeDtypeStruct(kv.shape, BF16), jax.ShapeDtypeStruct(queries.shape, BF16)],
+        in_specs=[pl.BlockSpec(memory_space=pltpu.VMEM)] * 6,
+        out_specs=[pl.BlockSpec(memory_space=pltpu.VMEM)] * 2,
+        scratch_shapes=[pltpu.VMEM((span, HEAD_DIM), BF16)] * 2 + [pltpu.VMEM((span, HEAD_DIM), F32)] * 2,
+        compiler_params=pltpu.CompilerParams(vmem_limit_bytes=VMEM_LIMIT),
+    )(got, kv, queries, probs, cosine, sine)
+
+
+ROWS = 16
+
+
+def row_tiles(count, body):
+    @pl.loop(0, count // ROWS)
+    def _(r):
+        body(pl.ds(pl.multiple_of(r * ROWS, ROWS), ROWS))
+
+
+def pieces(nd, width, plane_d, own_d):
+    for j in range(width // own_d):
+        yield j * own_d, j % nd, (j // nd) * own_d
+
+
+def inverse_of(rows):
+    return lax.rsqrt(jnp.mean(rows * rows, axis=1, keepdims=True) + EPS_NORM)
+
+
+def norm_back(rows, gain, grad):
+    inverse = inverse_of(rows)
+    normed = rows * inverse
+    scaled = grad * gain
+    inner = jnp.mean(normed * scaled, axis=1, keepdims=True)
+    return inverse * (scaled - normed * inner), grad * normed
+
+
+def join_kernel(own_d, got, tokens, gain, residual, hidden):
+    nd, tok, plane_d = got.shape
+    half = hidden.shape[0]
+    first = lax.axis_index("mp") * half
+
+    def add(at):
+        for c, e, p in pieces(nd, tokens.shape[1], plane_d, own_d):
+            residual[at, c : c + own_d] = (
+                got[e, at, p : p + own_d].astype(F32) + tokens[at, c : c + own_d].astype(F32))
+
+    row_tiles(tok, add)
+
+    @pl.loop(0, half // ROWS)
+    def _(r):
+        rows = residual[pl.ds(pl.multiple_of(first + r * ROWS, ROWS), ROWS)]
+        at = pl.ds(pl.multiple_of(r * ROWS, ROWS), ROWS)
+        hidden[at] = (rows * inverse_of(rows) * gain[...]).astype(BF16)
+
+
+def split_kernel(own_d, grad, ffn, residual, gain, cot, block_out, residual_grad, cut, gain_cut, total):
+    nd, tok, plane_d = cut.shape
+    total[...] = jnp.zeros_like(total)
+
+    def body(at):
+        rows = residual[at]
+        block_out[at] = (rows + ffn[at].astype(F32)).astype(BF16)
+        back, terms = norm_back(rows, gain[...], grad[at].astype(F32))
+        total[...] += terms
+        value = cot[at].astype(F32) + back
+        residual_grad[at] = value
+        for c, e, p in pieces(nd, grad.shape[1], plane_d, own_d):
+            cut[e, at, p : p + own_d] = value[:, c : c + own_d].astype(BF16)
+
+    row_tiles(tok, body)
+    gain_cut[...] = jnp.zeros_like(gain_cut)
+    sums = jnp.sum(total[...], axis=0, keepdims=True)
+    for c, e, p in pieces(nd, grad.shape[1], plane_d, own_d):
+        gain_cut[e, 0:1, p : p + own_d] = sums[:, c : c + own_d]
+
+
+def last_kernel(own_d, got, tokens, gain, residual_grad, out, grad):
+    nd, tok, plane_d = got.shape
+
+    def body(at):
+        for c, e, p in pieces(nd, tokens.shape[1], plane_d, own_d):
+            grad[:, c : c + own_d] = got[e, at, p : p + own_d].astype(F32)
+        back, _ = norm_back(tokens[at].astype(F32), gain[...], grad[...])
+        out[at] = residual_grad[at] + back
+
+    row_tiles(tok, body)
+
+
+def local(kernel, outs, args, scratch=()):
+    return pl.pallas_call(
+        kernel,
+        out_shape=[jax.ShapeDtypeStruct(shape, dtype) for shape, dtype in outs],
+        in_specs=[pl.BlockSpec(memory_space=pltpu.VMEM)] * len(args),
+        out_specs=[pl.BlockSpec(memory_space=pltpu.VMEM)] * len(outs),
+        scratch_shapes=[pltpu.VMEM(shape, dtype) for shape, dtype in scratch],
+        compiler_params=pltpu.CompilerParams(vmem_limit_bytes=VMEM_LIMIT),
+    )(*args)
+
+
 def pack(part, parts, ins, outs):
     gateup, down = ins
     (out,) = outs
@@ -998,14 +1193,13 @@
 
     def from_plane(collective, value):
         got = plane_reduce(collective, mesh_shape, value.reshape(nd, 2, half, plane_d))
-        return got.reshape(nd, tok, ns, own_d).transpose(1, 2, 0, 3).reshape(tok, width).astype(F32)
-
-    def plane_sum(collective, value):
-        (got,) = gather(collective, mesh_shape, [(value.reshape(nd, tok, -1), "swap")])
-        return jnp.sum(got.astype(F32), axis=0)
+        return got.reshape(nd, tok, plane_d)
+
+    def plane_terms(collective, value):
+        return gather(collective, mesh_shape, [(value.reshape(nd, tok, -1), "swap")])[0]
 
     hidden_plane = (tokens_plane.astype(F32) * plane_scale * plane_gain).astype(BF16)
-    qkv_raw = plane_sum(8, product(hidden_plane, qkv_plane).astype(BF16))
+    qkv_terms = plane_terms(8, product(hidden_plane, qkv_plane).astype(BF16))
 
     pad = KV_BLOCKS * tok
     key_span = pad + tok
@@ -1020,61 +1214,37 @@
     positions = jnp.sum(
         (same_segment & (key_index[None, :] < query_index[:, None])).astype(jnp.int32), axis=1)
     cosine, sine_rows = rope_tables(positions)
-    cos_h, sin_h = cosine[:, None, :], sine_rows[:, None, :]
-    score_scale = HEAD_DIM ** (-0.5)
-    queries = rotate(qkv_raw[:, :q_cols].reshape(tok, heads_local, HEAD_DIM), cos_h, sin_h).astype(BF16)
-    kv_raw = qkv_raw[:, q_cols:]
+    kv_raw = jnp.sum(qkv_terms[:, :, q_cols:].astype(F32), axis=0)
     kv_mine = jnp.where(m == 0, rotate(kv_raw, cosine, sine_rows), kv_raw).astype(BF16)
     (kv_all,) = gather(1, mesh_shape, [(kv_mine, "all")])
     kv_all = kv_all.reshape(n, 2, tok, HEAD_DIM)
-    kv_pad = jnp.concatenate([jnp.zeros((KV_BLOCKS, 2, tok, HEAD_DIM), BF16), kv_all], axis=0)
-    kv_window = lax.dynamic_slice_in_dim(kv_pad, me, KV_BLOCKS + 1, 0)
-    key_rows = kv_window[:, 0].reshape(key_span, HEAD_DIM)
-    value_rows = kv_window[:, 1].reshape(key_span, HEAD_DIM)
-    scores = jnp.einsum("thd,kd->htk", queries, key_rows, preferred_element_type=F32) * score_scale
-    scores = jnp.where(allowed[None], scores, -jnp.inf)
-    row_max = jnp.max(scores, axis=2, keepdims=True)
-    raw = jnp.exp(scores - row_max)
-    probs = raw / jnp.sum(raw, axis=2, keepdims=True)
-    probs_low = probs.astype(BF16)
-    mixed = jnp.einsum("htk,kd->thd", probs_low, value_rows, preferred_element_type=F32)
-    mixed_low = mixed.reshape(tok, q_cols).astype(BF16)
+    mixed_low, queries, probs = attend(
+        nd, heads_local, qkv_terms, kv_all, allowed.astype(F32), cosine, sine_rows)
     mixed_plane, outproj_z = gather(
         2, mesh_shape, [(mixed_low, "plane"), (outproj_weight.T, "z")])
     mixed_plane = mixed_plane.reshape(plane_tok, q_cols)
     outproj_plane = outproj_z.reshape(plane_d, q_cols)
-    residual = input_rows + from_plane(9, cols_product(mixed_plane, outproj_plane).astype(BF16))
-    gain_two = full_gains[1]
-    inverse_two = lax.rsqrt(jnp.mean(residual * residual, axis=1, keepdims=True) + EPS_NORM)
-    hidden_two = (residual * inverse_two * gain_two).astype(BF16)
+    residual, hidden_two = local(
+        partial(join_kernel, own_d), [((tok, width), F32), ((half, width), BF16)],
+        [from_plane(9, cols_product(mixed_plane, outproj_plane).astype(BF16)), tokens_in, full_gains[1:]])
 
     act_low, gateup_low, three_grad = feed(
-        3, mesh_shape, lax.dynamic_slice_in_dim(hidden_two, m * half, half, 0), cot_all, three)
+        3, mesh_shape, hidden_two, cot_all, three)
     three_grad, act_low, gateup_low = lax.optimization_barrier((three_grad, act_low, gateup_low))
     three_grad = lax.all_to_all(three_grad.reshape(n, own_d, 3 * units), TOK, 0, 0, tiled=True)
     hidden_two_grad, ffn_sum = reduce_scatter(
         4, mesh_shape, True, (tok, width),
         factors=[(gateup_low, 0, 2 * units), (act_low, 2 * units, 3 * units)], weight=three)
-    hidden_two_grad = hidden_two_grad.reshape(tok, width).astype(F32)
-    ffn_sum = ffn_sum.reshape(tok, width).astype(F32)
-    block_out = (residual + ffn_sum).astype(BF16)
-
-    def norm_back(rows, inverse, gain_row, grad):
-        normed = rows * inverse
-        scaled = grad * gain_row
-        inner = jnp.mean(normed * scaled, axis=1, keepdims=True)
-        return inverse * (scaled - normed * inner), jnp.sum(grad * normed, axis=0)
-
-    residual_from, gain_two_grad = norm_back(residual, inverse_two, gain_two, hidden_two_grad)
-    residual_grad = block_cotangent.astype(F32) + residual_from
-    gain_cut = gain_two_grad.reshape(1, ns, nd, own_d).transpose(2, 0, 1, 3).reshape(nd, 1, plane_d)
-    attn_low, gain_two_part = gather(
-        10, mesh_shape,
-        [(plane_cut(residual_grad.astype(BF16)), "swap"), (jnp.pad(gain_cut, ((0, 0), (0, 7), (0, 0))), "swap")])
+    block_out, residual_grad, attn_cut, gain_cut = local(
+        partial(split_kernel, own_d),
+        [((tok, width), BF16), ((tok, width), F32), ((nd, tok, plane_d), BF16), ((nd, 8, plane_d), F32)],
+        [hidden_two_grad.reshape(tok, width), ffn_sum.reshape(tok, width), residual, full_gains[1:],
+         block_cotangent],
+        [((ROWS, width), F32)])
+    attn_low, gain_two_part = gather(10, mesh_shape, [(attn_cut, "swap"), (gain_cut, "swap")])
     attn_low = attn_low.reshape(plane_tok, plane_d)
     gain_two_part = jnp.where(m == 0, jnp.sum(gain_two_part[:, 0], axis=0), 0.0)
-    mixed_grad = plane_sum(11, product(attn_low, outproj_plane).astype(BF16))
-    mixed_grad = mixed_grad.astype(BF16).reshape(tok, heads_local, HEAD_DIM)
+    mixed_terms = plane_terms(11, product(attn_low, outproj_plane).astype(BF16))
 
     def z_sum(value):
         got = lax.all_to_all(value, "shard", 0, 0, tiled=True)
@@ -1084,27 +1254,19 @@
     outproj_grad, three_grad = lax.optimization_barrier((outproj_grad, three_grad))
     own_outproj = z_sum(outproj_grad.reshape(ns, own_d, q_cols))
 
-    probs_grad = jnp.einsum("thd,kd->htk", mixed_grad, value_rows, preferred_element_type=F32)
-    value_grad = jnp.einsum("htk,thd->kd", probs_low, mixed_grad, preferred_element_type=F32)
-    inner_sum = jnp.sum(probs * probs_grad, axis=2, keepdims=True)
-    scores_low = (probs * (probs_grad - inner_sum) * score_scale).astype(BF16)
-    query_rot_grad = jnp.einsum("htk,kd->thd", scores_low, key_rows, preferred_element_type=F32)
-    key_rot_grad = jnp.einsum("htk,thd->kd", scores_low, queries, preferred_element_type=F32)
-    window_grad = jnp.stack(
-        [key_rot_grad.reshape(KV_BLOCKS + 1, tok, HEAD_DIM), value_grad.reshape(KV_BLOCKS + 1, tok, HEAD_DIM)],
-        axis=1).astype(BF16)
-    kv_grad_pad = lax.dynamic_update_slice_in_dim(
-        jnp.zeros((KV_BLOCKS + n, 2, tok, HEAD_DIM), BF16), window_grad, me, 0)
-    (kv_grad,) = reduce_scatter(6, mesh_shape, False, (2 * tok, HEAD_DIM), terms=kv_grad_pad[KV_BLOCKS:])
+    kv_terms, query_low = attend_back(nd, mixed_terms, kv_all, queries, probs, cosine, sine_rows)
+    (kv_grad,) = reduce_scatter(6, mesh_shape, False, (2 * tok, HEAD_DIM), terms=kv_terms)
     kv_grad = kv_grad.astype(F32)
     kv_low = jnp.where(m == 0, rotate(kv_grad, cosine, -sine_rows), kv_grad)
-    query_low = rotate(query_rot_grad, cos_h, -sin_h).reshape(tok, q_cols)
-    qkv_low = jnp.concatenate([query_low, kv_low], axis=1).astype(BF16)
+    qkv_low = jnp.concatenate([query_low, kv_low.astype(BF16)], axis=1)
     (qkv_low_plane,) = gather(7, mesh_shape, [(qkv_low, "plane")])
     qkv_low_plane = qkv_low_plane.reshape(plane_tok, q_cols + HEAD_DIM)
     hidden_one_part = cols_product(qkv_low_plane, qkv_plane).astype(BF16)
     gain_one_part = jnp.sum(hidden_one_part.astype(F32) * (tokens_plane.astype(F32) * plane_scale), axis=0)
     hidden_one_grad = from_plane(12, hidden_one_part)
+    (input_grad,) = local(
+        partial(last_kernel, own_d), [((tok, width), F32)],
+        [hidden_one_grad, tokens_in, full_gains[:1], residual_grad], [((ROWS, width), F32)])
     gain_parts = jnp.stack([gain_one_part, gain_two_part], axis=1)
     qkv_grad = jnp.concatenate(
         [rows_product(hidden_plane, qkv_low_plane), jnp.pad(gain_parts, ((0, 0), (0, 126)))], axis=1).astype(BF16)
@@ -1118,9 +1280,6 @@
         m == 0, jnp.concatenate([kv_own, kv_other], axis=1), jnp.concatenate([kv_other, kv_own], axis=1))
     own_gains = (rest + rest_other)[:, HEAD_DIM : HEAD_DIM + 2].T
 
-    inverse_col = inverse_one[:, None]
-    input_from, _ = norm_back(input_rows, inverse_col, full_gains[0], hidden_one_grad)
-    input_grad = residual_grad + input_from
     step_value = step_count[0].astype(F32)
     bias_first = 1.0 - jnp.power(BETA_ONE, step_value)
     bias_second = 1.0 - jnp.power(BETA_TWO, step_value)

time: 707 us -> 651 us (0.921)
  local copies, waits for them, and re-layouts: 42.4 us -> 11 us
  Pallas kernels: 528 us -> 555 us
  other arithmetic: 42.3 us -> 18.4 us
  matrix products: 42.4 us -> 20.9 us
    pallas_call x0 -> x5, Pallas kernels: none -> 30.7 us  [the longest x3 15.1 us: local(): pl.pallas_call(kernel, out_shape=[jax.ShapeDtypeStruct(shape, dtype) for...]
    dot_general x6 -> x0, matrix products: 21.7 us -> none  [the longest x1 7.58 us: shards(): jnp.einsum('htk,kd->thd', scores_low, key_rows, preferred_element_type=F32)]
    convert_element_type x8 -> x0, local copies, waits for them, and re-layouts: 16.4 us -> none  [the longest x6 13.3 us: from_plane(): got.reshape(nd, tok, ns, own_d).transpose(1, 2, 0, 3).reshape(tok, width)]
    reduce_sum x6 -> x1, other arithmetic: 8.2 us -> 1.01 us  [shards(): kv_raw = jnp.sum(qkv_terms[:, :, q_cols:].astype(F32), axis=0)]
  transfers between devices with their start and end apart: 5 -> 5, of which waited for: 1 -> 0; matrix products, arithmetic and copies ran while one was open for 15% -> 6% of each run, Pallas kernels for 55% -> 65%
where the time goes in v4:
time: 651 us; the launch traced here: 640 us
  Pallas kernels  555 us (85%)
  starting transfers between devices  33 us (5%)
  matrix products  20.9 us (3%)
  other arithmetic  18.4 us (3%)
  local copies, waits for them, and re-layouts  11 us (2%)
    pallas_call x7, Pallas kernels, gather(): pl.pallas_call(partial(gather_kernel, ns, nd, modes, work, len(work_args)...  255 us
    pallas_call x2, Pallas kernels, reduce_scatter(): pl.pallas_call(partial(reduce_kernel, ns, nd, share, spans), out_shape=[j...  155 us
    pallas_call x1, Pallas kernels, feed(): pl.pallas_call(partial(feed_kernel, ns, nd), out_shape=[jax.ShapeDtypeStr...  68.1 us
    pallas_call x1, Pallas kernels, unpack_adam(): pl.pallas_call(unpack_kernel, out_shape=[shape3] * 4 + [shape2] * 4, grid...  26.3 us
    pallas_call x2, Pallas kernels, plane_reduce(): pl.pallas_call(partial(plane_kernel, ns, nd), out_shape=jax.ShapeDtypeStr...  19.8 us
    all_to_all x1, starting transfers between devices, shards(): lax.all_to_all(three, TOK, 0, 0, tiled=True).reshape(width, 3 * units)  15.2 us
    pallas_call x3, Pallas kernels, local(): pl.pallas_call(kernel, out_shape=[jax.ShapeDtypeStruct(shape, dtype) for...  15.1 us
  transfers between devices with their start and end apart: 5, of which 0 were waited for; matrix products, arithmetic and copies ran while one was open for 6% of the time, Pallas kernels for 65%

profile of v4, /device:TPU:14, one launch (start us, length us, event | category | flops | bytes accessed | tf_op | source)
XLA Modules:
  0.0 640.3 jit_solution(1131659876120391367)
XLA Ops:
  2.0 1.4 copy.91
  7.0 68.8 %shard_map.413 = (f32[4,4,2,8,256]{4,3,2,1,0:T(8,128)}, bf16[4,128,640]{2,1,0:T(8,128)(2,1)}, bf16[4,4,2,64,2560]{4,3,2,1,0:T(8,128)(2,1)}, bf16[4,160,1536]{2,1,0:T(8,128)(2,1)}, bf16[16,160,768]{2,1,0:T(8,128)(2,1)}) custom-call(f32[8,256]{1,0:T(8,128)} %fusion.26.refs_0_, bf16[4,128,640]{2,1,0:T(8,128)(2,1)} %copy.93.refs_1_, ...), custom_call_target="tpu_custom_call" | custom-call | bytes 1048576 | tf_op jit(solution)/shard_map/pallas_call | solution.py:275
  75.8 15.2 %all-to-all-start = ((bf16[16,160,768]{2,1,0:T(8,128)(2,1)}), bf16[16,160,768]{2,1,0:T(8,128)(2,1)}, u32[]{:S(2)}, u32[]{:S(2)}) async-start(bf16[16,160,768]{2,1,0:T(8,128)(2,1)} %get-tuple-element.78), calls=%async_computation | async-start | bytes 7864320 | tf_op jit(solution)/shard_map/all_to_all | solution.py:1184
  91.2 3.7 convolution_convert_fusion.2
  94.9 36.6 %shard_map.414.got = bf16[4,128,1536]{2,1,0:T(8,128)(2,1)} custom-call(bf16[4,128,1536]{2,1,0:T(8,128)(2,1)} %bitcast.100), custom_call_target="tpu_custom_call" | custom-call | bytes 1048576 | tf_op jit(solution)/shard_map/pallas_call | solution.py:275
  133.8 65.5 %shard_map.415 = bf16[4,4,2,128,256]{4,3,2,1,0:T(8,128)(2,1)} custom-call(bf16[128,256]{1,0:T(8,128)(2,1)} %fusion.9.refs_0_), custom_call_target="tpu_custom_call" | custom-call | bytes 1048576 | tf_op jit(solution)/shard_map/pallas_call | solution.py:275
  201.3 6.8 %shard_map.416 = (bf16[128,1280]{1,0:T(8,128)(2,1)}, bf16[128,1280]{1,0:T(8,128)(2,1)}, f32[5,128,1152]{2,1,0:T(8,128)}) custom-call(bf16[4,128,1536]{2,1,0:T(8,128)(2,1)} %shard_map.414.got, bf16[16,2,128,256]{3,2,1,0:T(8,128)(2,1)} %bitcast.85, f32[128,1152]{1,0:T(8,128)} %fusion.5.allowed, f32[128,128]{1,0:T(8,128)} %get-tuple-element.238.cosine, ...), custom_call_target="tpu_custom_call" | custom-call | tf_op jit(solution)/shard_map/pallas_call | solution.py:907
  208.1 34.5 %shard_map.417 = (bf16[4,128,1280]{2,1,0:T(8,128)(2,1)}, bf16[4,160,1280]{2,1,0:T(8,128)(2,1)}) custom-call(bf16[128,1280]{1,0:T(8,128)(2,1)} %get-tuple-element.73.refs_0_, bf16[160,1280]{1,0:T(8,128)(2,1)} %bitcast.98), custom_call_target="tpu_custom_call" | custom-call | bytes 1048576 | tf_op jit(solution)/shard_map/pallas_call | solution.py:275
  242.6 3.9 convolution_convert_fusion.4
  246.5 10.0 %shard_map.418 = bf16[4,2,64,640]{3,2,1,0:T(8,128)(2,1)} custom-call(bf16[4,2,64,640]{3,2,1,0:T(8,128)(2,1)} %bitcast.105), custom_call_target="tpu_custom_call" | custom-call | bytes 1048576 | tf_op jit(solution)/shard_map/pallas_call | solution.py:827
  257.3 4.4 shard_map.419
  261.7 68.1 %shard_map.420 = (bf16[4,4,2,64,256]{4,3,2,1,0:T(8,128)(2,1)}, bf16[4,4,2,64,512]{4,3,2,1,0:T(8,128)(2,1)}, bf16[2560,768]{1,0:T(8,128)(2,1)}) custom-call(bf16[64,2560]{1,0:T(8,128)(2,1)} %get-tuple-element.76.x, bf16[4,4,2,64,2560]{4,3,2,1,0:T(8,128)(2,1)} %get-tuple-element.77.cot, bf16[2560,768]{1,0:T(8,128)(2,1)} %bitcast.19.w.refs_2_), custom_call_target="tpu_custom_call" | custom-call | bytes 1048576 | tf_op jit(solution)/shard_map/pallas_call | solution.py:746
  329.8 6.9 %all-to-all-start.1 = ((bf16[16,160,768]{2,1,0:T(8,128)(2,1)}), bf16[16,160,768]{2,1,0:T(8,128)(2,1)}, u32[]{:S(2)}, u32[]{:S(2)}) async-start(bf16[16,160,768]{2,1,0:T(8,128)(2,1)} %bitcast.89), calls=%async_computation.1 | async-start | bytes 7864320 | tf_op jit(solution)/shard_map/all_to_all | solution.py:1234
  336.7 135.5 %shard_map.421 = (bf16[2,64,2560]{2,1,0:T(8,128)(2,1)}, bf16[2,64,2560]{2,1,0:T(8,128)(2,1)}) custom-call(bf16[4,4,2,64,512]{4,3,2,1,0:T(8,128)(2,1)} %get-tuple-element.81, bf16[4,4,2,64,256]{4,3,2,1,0:T(8,128)(2,1)} %get-tuple-element.80, bf16[2560,768]{1,0:T(8,128)(2,1)} %bitcast.19.w.refs_2_), custom_call_target="tpu_custom_call" | custom-call | bytes 1048576 | tf_op jit(solution)/shard_map/pallas_call | solution.py:539
  472.2 5.9 shard_map.422
  478.1 15.3 %shard_map.423 = (bf16[4,128,640]{2,1,0:T(8,128)(2,1)}, f32[4,8,640]{2,1,0:T(8,128)}) custom-call(bf16[4,128,640]{2,1,0:T(8,128)(2,1)} %get-tuple-element.88.refs_0_, f32[4,8,640]{2,1,0:T(8,128)} %get-tuple-element.89.refs_1_), custom_call_target="tpu_custom_call" | custom-call | bytes 1048576 | tf_op jit(solution)/shard_map/pallas_call | solution.py:275
  493.5 3.3 fusion.1
  496.8 5.2 all-to-all-start.2
  502.0 3.7 convolution_convert_fusion.1
  505.7 18.0 %shard_map.424.got = bf16[4,128,1280]{2,1,0:T(8,128)(2,1)} custom-call(bf16[4,128,1280]{2,1,0:T(8,128)(2,1)} %bitcast.103), custom_call_target="tpu_custom_call" | custom-call | bytes 1048576 | tf_op jit(solution)/shard_map/pallas_call | solution.py:275
  523.7 8.9 %shard_map.425 = (bf16[16,2,128,256]{3,2,1,0:T(8,128)(2,1)}, bf16[128,1280]{1,0:T(8,128)(2,1)}) custom-call(bf16[4,128,1280]{2,1,0:T(8,128)(2,1)} %shard_map.424.got, bf16[16,2,128,256]{3,2,1,0:T(8,128)(2,1)} %bitcast.86, bf16[128,1280]{1,0:T(8,128)(2,1)} %get-tuple-element.91.queries, f32[5,128,1152]{2,1,0:T(8,128)} %get-tuple-element.92.probs, ...), custom_call_target="tpu_custom_call" | custom-call | tf_op jit(solution)/shard_map/pallas_call | solution.py:965
  532.6 19.0 %shard_map.426 = bf16[128,256]{1,0:T(8,128)(2,1)} custom-call(bf16[4,4,2,128,256]{4,3,2,1,0:T(8,128)(2,1)} %bitcast.97), custom_call_target="tpu_custom_call" | custom-call | bytes 1048576 | tf_op jit(solution)/shard_map/pallas_call | solution.py:539
  554.6 16.6 %shard_map.427 = bf16[4,128,1536]{2,1,0:T(8,128)(2,1)} custom-call(bf16[128,1536]{1,0:T(8,128)(2,1)} %pad_maximum_fusion.1.refs_0_), custom_call_target="tpu_custom_call" | custom-call | bytes 1048576 | tf_op jit(solution)/shard_map/pallas_call | solution.py:275
  572.2 3.7 multiply_reduce_fusion
  576.1 2.7 convolution_convert_fusion
  578.8 1.5 fusion.2
  580.6 5.2 all-to-all-start.3
  590.2 9.8 %shard_map.428 = bf16[4,2,64,640]{3,2,1,0:T(8,128)(2,1)} custom-call(bf16[4,2,64,640]{3,2,1,0:T(8,128)(2,1)} %bitcast.104), custom_call_target="tpu_custom_call" | custom-call | bytes 1048576 | tf_op jit(solution)/shard_map/pallas_call | solution.py:827
  600.0 4.8 shard_map.429
  604.7 26.3 %shard_map.430 = (f32[160,2,3840]{2,1,0:T(2,128)}, f32[160,2,3840]{2,1,0:T(2,128)}, f32[160,2,3840]{2,1,0:T(2,128)}, f32[160,2,3840]{2,1,0:T(2,128)}, f32[160,38...) custom-call(f32[2]{0:T(128)} %pad_maximum_fusion.3.rates, ...), custom_call_target="tpu_custom_call" | custom-call | tf_op jit(solution)/shard_map/pallas_call | solution.py:1107
  631.1 1.8 multiply_bitcast_fusion
  634.3 1.9 add_multiply_fusion
  (115 shorter events, 23.2 us)
Async XLA Ops:
  0.7 2.8 copy-start.19
  0.7 2.8 copy-start.16
  3.4 1.3 copy-start.3
  3.5 2.0 copy-start.8
  3.5 2.0 copy-start.2
  75.8 15.3 %copy-start.15 = (f32[4,4,2,8,256]{4,3,2,1,0:T(8,128)S(1)}, f32[4,4,2,8,256]{4,3,2,1,0:T(8,128)}, u32[]{:S(2)}) copy-start(f32[4,4,2,8,256]{4,3,2,1,0:T(8,128)} %get-tuple-element.71) | copy-start | bytes 786436
  75.8 15.4 %copy-start.20 = (bf16[4,160,1536]{2,1,0:T(8,128)(2,1)S(1)}, bf16[4,160,1536]{2,1,0:T(8,128)(2,1)}, u32[]{:S(2)}) copy-start(bf16[4,160,1536]{2,1,0:T(8,128)(2,1)} %get-tuple-element.72) | copy-start | bytes 5898244
  75.8 185.9 %all-to-all-start = ((bf16[16,160,768]{2,1,0:T(8,128)(2,1)}), bf16[16,160,768]{2,1,0:T(8,128)(2,1)}, u32[]{:S(2)}, u32[]{:S(2)}) async-start(bf16[16,160,768]{2,1,0:T(8,128)(2,1)} %get-tuple-element.78), calls=%async_computation | async-start | bytes 7864320 | tf_op jit(solution)/shard_map/all_to_all | solution.py:1184
  329.8 166.9 %all-to-all-start.1 = ((bf16[16,160,768]{2,1,0:T(8,128)(2,1)}), bf16[16,160,768]{2,1,0:T(8,128)(2,1)}, u32[]{:S(2)}, u32[]{:S(2)}) async-start(bf16[16,160,768]{2,1,0:T(8,128)(2,1)} %bitcast.89), calls=%async_computation.1 | async-start | bytes 7864320 | tf_op jit(solution)/shard_map/all_to_all | solution.py:1234
  472.2 21.3 %copy-start.22 = (bf16[4,128,1280]{2,1,0:T(8,128)(2,1)S(1)}, bf16[4,128,1280]{2,1,0:T(8,128)(2,1)}, u32[]{:S(2)}) copy-start(bf16[4,128,1280]{2,1,0:T(8,128)(2,1)} %get-tuple-element.74) | copy-start | bytes 3932164
  496.8 5.2 copy-start.24
  496.8 83.5 %all-to-all-start.2 = ((bf16[4,160,1280]{2,1,0:T(8,128)(2,1)}), bf16[4,160,1280]{2,1,0:T(8,128)(2,1)S(1)}, u32[]{:S(2)}, u32[]{:S(2)}) async-start(bf16[4,160,1280]{2,1,0:T(8,128)(2,1)} %bitcast.99), calls=%async_computation.2 | async-start | bytes 3276800 | tf_op jit(solution)/shard_map/all_to_all | solution.py:1250
  532.6 21.2 %copy-start.11 = (bf16[128,1280]{1,0:T(8,128)(2,1)S(1)}, bf16[128,1280]{1,0:T(8,128)(2,1)}, u32[]{:S(2)}) copy-start(bf16[128,1280]{1,0:T(8,128)(2,1)} %get-tuple-element.93) | copy-start | bytes 983044
  551.6 20.6 %copy-start.21 = (bf16[4,160,1536]{2,1,0:T(8,128)(2,1)S(1)}, bf16[4,160,1536]{2,1,0:T(8,128)(2,1)}, u32[]{:S(2)}) copy-start(bf16[4,160,1536]{2,1,0:T(8,128)(2,1)} %get-tuple-element.72) | copy-start | bytes 5898244
  551.6 20.6 %copy-start.23 = (bf16[4,128,640]{2,1,0:T(8,128)(2,1)S(1)}, bf16[4,128,640]{2,1,0:T(8,128)(2,1)}, u32[]{:S(2)}) copy-start(bf16[4,128,640]{2,1,0:T(8,128)(2,1)} %get-tuple-element.69) | copy-start | bytes 1966084
  580.5 50.5 %copy-start = (f32[160,1280]{1,0:T(8,128)}, f32[160,1280]{1,0:T(8,128)S(1)}, u32[]{:S(2)}) copy-start(f32[160,1280]{1,0:T(8,128)S(1)} %convert_reduce_fusion.1) | copy-start | bytes 2457604
  580.5 7.5 %copy-start.17 = (f32[2,160]{1,0:T(2,128)S(1)}, f32[2,160]{1,0:T(2,128)}, u32[]{:S(2)}) copy-start(f32[2,160]{1,0:T(2,128)} %param.42) | copy-start | bytes 3844
  580.5 8.3 %copy-start.18 = (f32[2,160]{1,0:T(2,128)S(1)}, f32[2,160]{1,0:T(2,128)}, u32[]{:S(2)}) copy-start(f32[2,160]{1,0:T(2,128)} %param.36) | copy-start | bytes 3844
  580.6 52.3 %all-to-all-start.3 = ((bf16[4,160,1664]{2,1,0:T(8,128)(2,1)}), bf16[4,160,1664]{2,1,0:T(8,128)(2,1)S(1)}, u32[]{:S(2)}, u32[]{:S(2)}) async-start(bf16[4,160,1664]{2,1,0:T(8,128)(2,1)} %bitcast.35), calls=%async_computation.3 | async-start | bytes 4259840 | tf_op jit(solution)/shard_map/all_to_all | solution.py:1250
  604.7 26.3 %copy-start.1 = (bf16[1280,160]{0,1:T(8,128)(2,1)S(1)}, bf16[1280,160]{0,1:T(8,128)(2,1)}, u32[]{:S(2)}) copy-start(bf16[1280,160]{0,1:T(8,128)(2,1)} %param.27) | copy-start | bytes 1228804
  604.7 26.3 %copy-start.6 = (f32[1280,160]{0,1:T(8,128)S(1)}, f32[1280,160]{0,1:T(8,128)}, u32[]{:S(2)}) copy-start(f32[1280,160]{0,1:T(8,128)} %param.33) | copy-start | bytes 2457604
  604.7 26.3 %copy-start.7 = (f32[1280,160]{0,1:T(8,128)S(1)}, f32[1280,160]{0,1:T(8,128)}, u32[]{:S(2)}) copy-start(f32[1280,160]{0,1:T(8,128)} %param.39) | copy-start | bytes 2457604
  632.9 1.1 copy-start.4
  632.9 1.4 copy-start.5
  633.2 3.0 copy-start.12
  633.2 3.0 copy-start.13
  633.2 3.0 copy-start.14
  633.2 2.9 collective-permute-start
  636.1 2.8 copy-start.9
  636.1 2.8 copy-start.10

commit v5 on v4

--- a/solution.py
+++ b/solution.py
@@ -76,7 +76,7 @@
 def gather_kernel(ns, nd, modes, work, n_work, *refs):
     n = len(modes)
     ins, more_in = refs[:n], refs[n : n + n_work]
-    outs, more_out = refs[n + n_work : 2 * n + n_work], refs[2 * n + n_work : 2 * n + 2 * n_work - (n_work > 0)]
+    outs, more_out = refs[n + n_work : 2 * n + n_work], refs[2 * n + n_work : -7 * n]
     sems = refs[-7 * n :]
     s, d, m = (lax.axis_index(a) for a in ("shard", "dp", "mp"))
     use_z = any(k in ("z", "all") for k in modes)
@@ -262,7 +262,7 @@
     each(levels[0] + straight, lambda i, t: direct[i], finish)
 
 
-def gather(collective, mesh_shape, items, work=None, work_args=(), work_out=None):
+def gather(collective, mesh_shape, items, work=None, work_args=(), work_outs=()):
     ns, nd = mesh_shape["shard"], mesh_shape["dp"]
     modes = tuple(mode for _, mode in items)
     lead = {"z": (ns,), "plane": (nd,), "all": (ns, nd, 2), "swap": ()}
@@ -274,11 +274,11 @@
                  dma(())]
     return pl.pallas_call(
         partial(gather_kernel, ns, nd, modes, work, len(work_args)),
-        out_shape=shapes + ([work_out] if work else []),
+        out_shape=shapes + list(work_outs),
         in_specs=[pl.BlockSpec(memory_space=pl.ANY)] * len(items)
         + [pl.BlockSpec(memory_space=pltpu.VMEM)] * len(work_args),
         out_specs=[pl.BlockSpec(memory_space=pl.ANY)] * len(items)
-        + ([pl.BlockSpec(memory_space=pltpu.VMEM)] if work else []),
+        + [pl.BlockSpec(memory_space=pltpu.VMEM)] * len(work_outs),
         scratch_shapes=sems,
         compiler_params=pltpu.CompilerParams(
             collective_id=collective, has_side_effects=True, vmem_limit_bytes=VMEM_LIMIT),
@@ -286,9 +286,8 @@
     )(*[a for a, _ in items], *work_args)
 
 
-def reduce_kernel(ns, nd, share, spans, *refs):
-    count = len(spans) if spans else 1
-    n_in = count + 1 if spans else 1
+def reduce_kernel(ns, nd, share, count, made, *refs):
+    n_in = 2 * count if made else 1
     ins, outs, scratch = refs[:n_in], refs[n_in : n_in + count], refs[n_in + count :]
     own, sib, give, got, mid, zgot, fin, lsem, ss, sr, ps, pr, zs, zr, fs, fr, ks = scratch
     s, d, m = (lax.axis_index(a) for a in ("shard", "dp", "mp"))
@@ -300,7 +299,7 @@
     if relay:
         x, y, across = square(d)
         peers = [across, x, y]
-    chain = bool(spans)
+    chain = bool(made)
     if chain:
         order = []
         for k in range(ns - 1):
@@ -313,7 +312,7 @@
     items = [(a, k, order[k]) for k in range(ns) for a in range(count)]
 
     def score(a, k, b):
-        src = give.at[a, k % 2] if spans else ins[0].at[b, :, 1 - m]
+        src = give.at[a, k % 2] if made else ins[0].at[b, :, 1 - m]
         return pltpu.make_async_remote_copy(
             src, sib.at[a, b], ss.at[a, b], sr.at[a, b], device_id={"mp": 1 - m}, device_id_type=MESH)
 
@@ -321,18 +320,17 @@
         return pltpu.make_async_copy(ins[0].at[b, :, m], own.at[a, b], lsem.at[a, b])
 
     def multiply(a, b, core, store):
-        lo, hi = spans[a]
         step = 512 if c % 512 == 0 else 128
-        left = ins[a][b, :, core].reshape(nd * h, hi - lo)
+        left = ins[a][b, :, core].reshape(nd * h, ins[a].shape[-1])
 
         @pl.loop(0, c // step)
         def _(j):
             cols = pl.ds(pl.multiple_of(j * step, step), step)
-            term = cols_product(left, ins[count][cols, lo:hi])
+            term = cols_product(left, ins[count + a][cols])
             store(cols, term.astype(BF16).reshape(nd, h, step))
 
     def zero(a, k, b):
-        if not spans:
+        if not made:
             score(a, k, b).start()
             load(a, b).start()
             return
@@ -387,7 +385,7 @@
 
     def one(a, k, b):
         score(a, k, b).wait_recv()
-        if not spans:
+        if not made:
             load(a, b).wait()
         out_now = sends(a, b)
         for j, e in enumerate(peers + [d]):
@@ -458,7 +456,7 @@
         pl.when(jnp.logical_not(upward))(lambda: hop(a, b, -1).start())
 
     stages = [zero, one, two, three] + ([four] if chain else [])
-    if not spans:
+    if not made:
         for item in items:
             zero(*item)
         stages = stages[1:]
@@ -501,7 +499,7 @@
             give_out(a, m).wait_send()
         keep(a).wait()
         for k, b in enumerate(order):
-            if not spans or k >= ns - 2:
+            if not made or k >= ns - 2:
                 score(a, k, b).wait_send()
             for w in sends(a, b):
                 w.wait_send()
@@ -509,7 +507,7 @@
             zcopy(a, b, s).wait_send()
 
 
-def reduce_scatter(collective, mesh_shape, share, blocks, terms=None, factors=None, weight=None):
+def reduce_scatter(collective, mesh_shape, share, blocks, terms=None, factors=None):
     ns, nd = mesh_shape["shard"], mesh_shape["dp"]
     rows, c = blocks
     h = rows // 2
@@ -517,7 +515,7 @@
     size = ns * nd * h * c * 2
     if size * count * 3 > (40 << 20):
         whole = [terms] if factors is None else [
-            cols_product(x, weight[:, lo:hi]).astype(BF16) for x, lo, hi in factors]
+            cols_product(x, w).astype(BF16) for x, w in factors]
         sums = []
         for p in whole:
             total = lax.psum_scatter(p.reshape(ns * nd, 2, h, c), TOK, scatter_dimension=0, tiled=True)[0]
@@ -525,19 +523,19 @@
             sums.append(total if share else lax.dynamic_index_in_dim(total, lax.axis_index("mp"), 0, False))
         return sums
     if factors is None:
-        spans = None
+        made = False
         args = [terms.reshape(ns, nd, 2, h, c)]
         in_specs = [pl.BlockSpec(memory_space=pl.ANY)]
         give = (1, 1, 1, 16, 128)
     else:
-        spans = tuple((lo, hi) for _, lo, hi in factors)
-        args = [x.reshape(ns, nd, 2, h, hi - lo) for x, lo, hi in factors] + [weight]
-        in_specs = [pl.BlockSpec(memory_space=pltpu.VMEM)] * (count + 1)
+        made = True
+        args = [x.reshape(ns, nd, 2, h, -1) for x, _ in factors] + [w for _, w in factors]
+        in_specs = [pl.BlockSpec(memory_space=pltpu.VMEM)] * (2 * count)
         give = (count, 2, nd, h, c)
     slots = 3 if nd == 4 and h % 32 == 0 else nd
     dma = pltpu.SemaphoreType.DMA
     return pl.pallas_call(
-        partial(reduce_kernel, ns, nd, share, spans),
+        partial(reduce_kernel, ns, nd, share, count, made),
         out_shape=[jax.ShapeDtypeStruct((2, h, c) if share else (h, c), BF16)] * count,
         in_specs=in_specs,
         out_specs=[pl.BlockSpec(memory_space=pl.ANY)] * count,
@@ -566,10 +564,11 @@
     return 0.5 * v * (1.0 + t), slope
 
 
-def feed_kernel(ns, nd, x, cot, w, act, low, grad, hid, cots, acc, zs, zr, ps, pr, cs, cr, ls, ks):
+def feed_kernel(ns, nd, x, cot, wide, thin, act, low, wide_grad, thin_grad, hid, cots, acc, more, zs, zr, ps, pr, cs, cr,
+                ls, ks):
     s, d, m = (lax.axis_index(a) for a in ("shard", "dp", "mp"))
     h, width = x.shape
-    units = w.shape[1] // 3
+    units = thin.shape[1]
     relay = nd == 4 and h % 32 == 0
     greet(ns, nd, True, True, True, z_all=True)
     turns = [0] + sorted(range(1, ns), key=lambda k: min(k, ns - k))
@@ -662,8 +661,8 @@
         b = order[k]
         at = pl.ds(q * count, count)
         rows = count * 2 * h
-        pre = product(hid[b, at].reshape(rows, width), w[:, : 2 * units])
-        back = product(cots[b, at].reshape(rows, width), w[:, 2 * units :])
+        pre = product(hid[b, at].reshape(rows, width), wide[...])
+        back = product(cots[b, at].reshape(rows, width), thin[...])
         value, slope = gelu_both(pre[:, :units])
         up = pre[:, units:]
         act[b, at] = (value * up).astype(BF16).reshape(count, 2, h, units)
@@ -683,14 +682,14 @@
             one = rows_product(hid[b, :, :, :, at].reshape(rows, step), lows)
             two = rows_product(cots[b, :, :, :, at].reshape(rows, step), acts)
             if k > 0:
-                one = one + acc[at, : 2 * units]
-                two = two + acc[at, 2 * units :]
+                one = one + acc[at]
+                two = two + more[at]
             if k < ns - 1:
-                acc[at, : 2 * units] = one
-                acc[at, 2 * units :] = two
+                acc[at] = one
+                more[at] = two
             else:
-                grad[at, : 2 * units] = one.astype(BF16)
-                grad[at, 2 * units :] = two.astype(BF16)
+                wide_grad[at] = one.astype(BF16)
+                thin_grad[at] = two.astype(BF16)
 
     for b in order[1:]:
         zsend(b).start()
@@ -725,45 +724,46 @@
             zsend(b).wait_send()
 
 
-def feed(collective, mesh_shape, x, cot, w):
+def feed(collective, mesh_shape, x, cot, wide, thin):
     ns, nd = mesh_shape["shard"], mesh_shape["dp"]
     h, width = x.shape
-    units = w.shape[1] // 3
+    units = thin.shape[1]
     rows = (ns, nd, 2, h)
     if 2 * cot.size * 2 > (24 << 20):
         (hid,) = gather(collective, mesh_shape, [(x, "all")])
         hid, cot = hid.reshape(-1, width), cot.reshape(-1, width)
-        pre = product(hid, w[:, : 2 * units])
-        back = product(cot, w[:, 2 * units :])
+        pre = product(hid, wide)
+        back = product(cot, thin)
         value, slope = gelu_both(pre[:, :units])
         up = pre[:, units:]
         act = (value * up).astype(BF16)
         low = jnp.concatenate([back * up * slope, back * value], axis=1).astype(BF16)
-        grad = jnp.concatenate([rows_product(hid, low), rows_product(cot, act)], axis=1).astype(BF16)
-        return act, low, grad
+        return act, low, rows_product(hid, low).astype(BF16), rows_product(cot, act).astype(BF16)
     dma = pltpu.SemaphoreType.DMA
     vmem = pl.BlockSpec(memory_space=pltpu.VMEM)
-    act, low, grad = pl.pallas_call(
+    act, low, wide_grad, thin_grad = pl.pallas_call(
         partial(feed_kernel, ns, nd),
         out_shape=[
             jax.ShapeDtypeStruct(rows + (units,), BF16),
             jax.ShapeDtypeStruct(rows + (2 * units,), BF16),
-            jax.ShapeDtypeStruct((width, 3 * units), BF16),
+            jax.ShapeDtypeStruct((width, 2 * units), BF16),
+            jax.ShapeDtypeStruct((width, units), BF16),
         ],
-        in_specs=[vmem, pl.BlockSpec(memory_space=pl.ANY), vmem],
-        out_specs=[vmem] * 3,
+        in_specs=[vmem, pl.BlockSpec(memory_space=pl.ANY), vmem, vmem],
+        out_specs=[vmem] * 4,
         scratch_shapes=[
             pltpu.VMEM(rows + (width,), BF16),
             pltpu.VMEM(rows + (width,), BF16),
-            pltpu.VMEM((width, 3 * units), F32),
+            pltpu.VMEM((width, 2 * units), F32),
+            pltpu.VMEM((width, units), F32),
             dma((ns,)), dma((ns,)), dma((ns, max(nd, 6))), dma((ns, nd, 2)), dma((ns, nd)), dma((ns, nd)),
             dma((ns,)), dma(()),
         ],
         compiler_params=pltpu.CompilerParams(
             collective_id=collective, has_side_effects=True, vmem_limit_bytes=VMEM_LIMIT),
         cost_estimate=pl.CostEstimate(flops=0, bytes_accessed=1 << 20, transcendentals=0),
-    )(x, cot, w)
-    return act.reshape(-1, units), low.reshape(-1, 2 * units), grad
+    )(x, cot, wide, thin)
+    return act.reshape(-1, units), low.reshape(-1, 2 * units), wide_grad, thin_grad
 
 
 def plane_kernel(ns, nd, p, out, own, sib, ls, ss, sr, ps, pr, fs, fr, ks):
@@ -1063,19 +1063,19 @@
 
 def pack(part, parts, ins, outs):
     gateup, down = ins
-    (out,) = outs
-    n, _, columns = out.shape
-    units = columns // 3
+    pair, single = outs
+    n, _, units = single.shape
     full = down.shape[1] // units
     share = -(-n // parts)
     for j in range(part * share, min((part + 1) * share, n)):
         if j >= full:
-            out[j] = jnp.zeros(out.shape[1:], BF16)
+            pair[j] = jnp.zeros(pair.shape[1:], BF16)
+            single[j] = jnp.zeros(single.shape[1:], BF16)
             continue
         at = pl.ds(j * units, units)
-        out[j, :, :units] = gateup[:, 0, at]
-        out[j, :, units : 2 * units] = gateup[:, 1, at]
-        out[j, :, 2 * units :] = down[:, at]
+        pair[j, :, :units] = gateup[:, 0, at]
+        pair[j, :, units:] = gateup[:, 1, at]
+        single[j] = down[:, at]
 
 
 def adam_step(rates, grad, weight, first, second, decay):
@@ -1085,20 +1085,20 @@
     return first_new, second_new, -LEARN_RATE * (direction + decay * weight.astype(F32))
 
 
-def unpack_kernel(rates, got, gw, gf, gs, dw, df, ds, gg, gfn, gsn, gu, dg, dfn, dsn, du):
+def unpack_kernel(rates, pair_got, got, gw, gf, gs, dw, df, ds, gg, gfn, gsn, gu, dg, dfn, dsn, du):
     units = dw.shape[1]
     pair = (rates[0], rates[1])
     for k in range(2):
-        grad = got[0, :, k * units : (k + 1) * units].astype(F32)
+        grad = pair_got[0, :, k * units : (k + 1) * units].astype(F32)
         gg[:, k, :] = grad
         gfn[:, k, :], gsn[:, k, :], gu[:, k, :] = adam_step(
             pair, grad, gw[:, k, :], gf[:, k, :], gs[:, k, :], DECAY_RATE)
-    grad = got[0, :, 2 * units :].astype(F32)
+    grad = got[0].astype(F32)
     dg[...] = grad
     dfn[...], dsn[...], du[...] = adam_step(pair, grad, dw[...], df[...], ds[...], DECAY_RATE)
 
 
-def unpack_adam(units, rates, got, gateup, down):
+def unpack_adam(units, rates, pair_got, got, gateup, down):
     own_d, _, ff_local = gateup[0].shape
     three = pl.BlockSpec((own_d, 2, units), lambda j: (0, 0, j))
     two = pl.BlockSpec((own_d, units), lambda j: (0, j))
@@ -1110,11 +1110,12 @@
         grid=(ff_local // units,),
         in_specs=[
             pl.BlockSpec(memory_space=pltpu.SMEM),
-            pl.BlockSpec((1, own_d, 3 * units), lambda j: (j, 0, 0)),
+            pl.BlockSpec((1, own_d, 2 * units), lambda j: (j, 0, 0)),
+            pl.BlockSpec((1, own_d, units), lambda j: (j, 0, 0)),
         ] + [three] * 3 + [two] * 3,
         out_specs=[three] * 4 + [two] * 4,
         compiler_params=pltpu.CompilerParams(vmem_limit_bytes=VMEM_LIMIT),
-    )(rates, got, *gateup, *down)
+    )(rates, pair_got, got, *gateup, *down)
     return out[:4], out[4:]
 
 
@@ -1174,14 +1175,19 @@
     def plane_cut(value):
         return value.reshape(tok, ns, nd, own_d).transpose(2, 0, 1, 3).reshape(nd, tok, plane_d)
 
-    small_all, tokens_plane, cot_all, qkv_plane, three = gather(
+    small_all, tokens_plane, cot_all, qkv_plane, pair, single = gather(
         0, mesh_shape,
         [(small, "all"), (plane_cut(tokens_in), "swap"),
          (lax.dynamic_slice_in_dim(block_cotangent, m * half, half, 0), "all"), (qkv_weight, "z")],
-        pack, (gateup_weight, down_weight.T), jax.ShapeDtypeStruct((n, own_d, 3 * units), BF16))
+        pack, (gateup_weight, down_weight.T),
+        (jax.ShapeDtypeStruct((n, own_d, 2 * units), BF16), jax.ShapeDtypeStruct((n, own_d, units), BF16)))
     tokens_plane = tokens_plane.reshape(plane_tok, plane_d)
-    three, tokens_plane = lax.optimization_barrier((three, tokens_plane))
-    three = lax.all_to_all(three, TOK, 0, 0, tiled=True).reshape(width, 3 * units)
+
+    def trade(value):
+        return lax.all_to_all(value.reshape(n, own_d, -1), TOK, 0, 0, tiled=True)
+
+    pair, tokens_plane = lax.optimization_barrier((pair, tokens_plane))
+    pair = trade(pair).reshape(width, 2 * units)
     qkv_plane = qkv_plane.reshape(plane_d, q_cols + HEAD_DIM)
     small_all = small_all[:, :, 0]
     gains_by = small_all[:, :, :2, :own_d]
@@ -1217,6 +1223,8 @@
     kv_raw = jnp.sum(qkv_terms[:, :, q_cols:].astype(F32), axis=0)
     kv_mine = jnp.where(m == 0, rotate(kv_raw, cosine, sine_rows), kv_raw).astype(BF16)
     (kv_all,) = gather(1, mesh_shape, [(kv_mine, "all")])
+    single, pair, kv_all = lax.optimization_barrier((single, pair, kv_all))
+    single = trade(single).reshape(width, units)
     kv_all = kv_all.reshape(n, 2, tok, HEAD_DIM)
     mixed_low, queries, probs = attend(
         nd, heads_local, qkv_terms, kv_all, allowed.astype(F32), cosine, sine_rows)
@@ -1228,13 +1236,13 @@
         partial(join_kernel, own_d), [((tok, width), F32), ((half, width), BF16)],
         [from_plane(9, cols_product(mixed_plane, outproj_plane).astype(BF16)), tokens_in, full_gains[1:]])
 
-    act_low, gateup_low, three_grad = feed(
-        3, mesh_shape, hidden_two, cot_all, three)
-    three_grad, act_low, gateup_low = lax.optimization_barrier((three_grad, act_low, gateup_low))
-    three_grad = lax.all_to_all(three_grad.reshape(n, own_d, 3 * units), TOK, 0, 0, tiled=True)
+    act_low, gateup_low, pair_grad, single_grad = feed(3, mesh_shape, hidden_two, cot_all, pair, single)
+    pair_grad, act_low, gateup_low = lax.optimization_barrier((pair_grad, act_low, gateup_low))
+    pair_grad = trade(pair_grad)
     hidden_two_grad, ffn_sum = reduce_scatter(
-        4, mesh_shape, True, (tok, width),
-        factors=[(gateup_low, 0, 2 * units), (act_low, 2 * units, 3 * units)], weight=three)
+        4, mesh_shape, True, (tok, width), factors=[(gateup_low, pair), (act_low, single)])
+    hidden_two_grad, single_grad, pair_grad = lax.optimization_barrier((hidden_two_grad, single_grad, pair_grad))
+    single_grad = trade(single_grad)
     block_out, residual_grad, attn_cut, gain_cut = local(
         partial(split_kernel, own_d),
         [((tok, width), BF16), ((tok, width), F32), ((nd, tok, plane_d), BF16), ((nd, 8, plane_d), F32)],
@@ -1251,7 +1259,7 @@
         return jnp.sum(got.astype(F32), axis=0)
 
     outproj_grad = rows_product(attn_low, mixed_plane).astype(BF16)
-    outproj_grad, three_grad = lax.optimization_barrier((outproj_grad, three_grad))
+    outproj_grad, single_grad = lax.optimization_barrier((outproj_grad, single_grad))
     own_outproj = z_sum(outproj_grad.reshape(ns, own_d, q_cols))
 
     kv_terms, query_low = attend_back(nd, mixed_terms, kv_all, queries, probs, cosine, sine_rows)
@@ -1285,7 +1293,7 @@
     bias_second = 1.0 - jnp.power(BETA_TWO, step_value)
     rates = jnp.stack([1.0 / bias_first, 1.0 / bias_second])
     gateup_news, down_news = unpack_adam(
-        units, rates, three_grad, (gateup_weight, gateup_first, gateup_second),
+        units, rates, pair_grad, single_grad, (gateup_weight, gateup_first, gateup_second),
         (down_weight.T, down_first.T, down_second.T))
     down_news = [x.T for x in down_news]
 

time: 651 us -> 647 us (level)
  Pallas kernels: 555 us -> 528 us
  starting transfers between devices: 33 us -> 55.2 us
    all_to_all x2 -> x4, starting transfers between devices: 22.1 us -> 43.6 us  [trade(): return lax.all_to_all(value.reshape(n, own_d, -1), TOK, 0, 0, tiled=True)]
    pallas_call x7, Pallas kernels: 255 us -> 242 us  [gather(): pl.pallas_call(partial(gather_kernel, ns, nd, modes, work, len(work_args)...]
    pallas_call x2, Pallas kernels: 155 us -> 141 us  [reduce_scatter(): pl.pallas_call(partial(reduce_kernel, ns, nd, share, count, made), out_sh...]
  transfers between devices with their start and end apart: 5 -> 7, of which waited for: 0 -> 1; matrix products, arithmetic and copies ran while one was open for 6% -> 6% of each run, Pallas kernels for 65% -> 61%
where the time goes in v5:
time: 647 us; the launch traced here: 638 us
  Pallas kernels  528 us (82%)
  starting transfers between devices  55.2 us (9%)
  matrix products  21.6 us (3%)
  other arithmetic  18.4 us (3%)
  local copies, waits for them, and re-layouts  11.9 us (2%)
    pallas_call x7, Pallas kernels, gather(): pl.pallas_call(partial(gather_kernel, ns, nd, modes, work, len(work_args)...  242 us
    pallas_call x2, Pallas kernels, reduce_scatter(): pl.pallas_call(partial(reduce_kernel, ns, nd, share, count, made), out_sh...  141 us
    pallas_call x1, Pallas kernels, feed(): pl.pallas_call(partial(feed_kernel, ns, nd), out_shape=[jax.ShapeDtypeStr...  68.1 us
    all_to_all x4, starting transfers between devices, trade(): return lax.all_to_all(value.reshape(n, own_d, -1), TOK, 0, 0, tiled=True)  43.6 us
    pallas_call x1, Pallas kernels, unpack_adam(): pl.pallas_call(unpack_kernel, out_shape=[shape3] * 4 + [shape2] * 4, grid...  25.1 us
    pallas_call x2, Pallas kernels, plane_reduce(): pl.pallas_call(partial(plane_kernel, ns, nd), out_shape=jax.ShapeDtypeStr...  20.7 us
    pallas_call x3, Pallas kernels, local(): pl.pallas_call(kernel, out_shape=[jax.ShapeDtypeStruct(shape, dtype) for...  15.1 us
  transfers between devices with their start and end apart: 7, of which 1 were waited for; matrix products, arithmetic and copies ran while one was open for 6% of the time, Pallas kernels for 61%

profile of v5, /device:TPU:14, one launch (start us, length us, event | category | flops | bytes accessed | tf_op | source)
XLA Modules:
  0.0 638.0 jit_solution(6368162659169419855)
XLA Ops:
  7.0 68.9 %shard_map.413 = (f32[4,4,2,8,256]{4,3,2,1,0:T(8,128)}, bf16[4,128,640]{2,1,0:T(8,128)(2,1)}, bf16[4,4,2,64,2560]{4,3,2,1,0:T(8,128)(2,1)}, bf16[4,160,1536]{2,1...) custom-call(f32[8,256]{1,0:T(8,128)} %fusion.26.refs_0_, ...), custom_call_target="tpu_custom_call" | custom-call | bytes 1048576 | tf_op jit(solution)/shard_map/pallas_call | solution.py:275
  75.9 14.7 %all-to-all-start = ((bf16[16,160,512]{2,1,0:T(8,128)(2,1)}), bf16[16,160,512]{2,1,0:T(8,128)(2,1)S(1)}, u32[]{:S(2)}, u32[]{:S(2)}) async-start(bf16[16,160,512]{2,1,0:T(8,128)(2,1)} %get-tuple-element.82), calls=%async_computation | async-start | bytes 5242880 | tf_op jit(solution)/shard_map/all_to_all | solution.py:1187
  91.7 4.4 convolution_convert_fusion.2
  96.0 35.9 %shard_map.414.got = bf16[4,128,1536]{2,1,0:T(8,128)(2,1)} custom-call(bf16[4,128,1536]{2,1,0:T(8,128)(2,1)} %bitcast.104), custom_call_target="tpu_custom_call" | custom-call | bytes 1048576 | tf_op jit(solution)/shard_map/pallas_call | solution.py:275
  134.3 32.7 %shard_map.415 = bf16[4,4,2,128,256]{4,3,2,1,0:T(8,128)(2,1)} custom-call(bf16[128,256]{1,0:T(8,128)(2,1)} %fusion.9.refs_0_), custom_call_target="tpu_custom_call" | custom-call | bytes 1048576 | tf_op jit(solution)/shard_map/pallas_call | solution.py:275
  167.1 6.8 %all-to-all-start.1 = ((bf16[16,160,256]{2,1,0:T(8,128)(2,1)}), bf16[16,160,256]{2,1,0:T(8,128)(2,1)}, u32[]{:S(2)}, u32[]{:S(2)}) async-start(bf16[16,160,256]{2,1,0:T(8,128)(2,1)} %get-tuple-element.90), calls=%async_computation.1 | async-start | bytes 2621440 | tf_op jit(solution)/shard_map/all_to_all | solution.py:1187
  176.7 6.8 %shard_map.416 = (bf16[128,1280]{1,0:T(8,128)(2,1)}, bf16[128,1280]{1,0:T(8,128)(2,1)}, f32[5,128,1152]{2,1,0:T(8,128)}) custom-call(bf16[4,128,1536]{2,1,0:T(8,128)(2,1)} %shard_map.414.got, bf16[16,2,128,256]{3,2,1,0:T(8,128)(2,1)} %bitcast.89, f32[128,1152]{1,0:T(8,128)} %fusion.5.allowed, f32[128,128]{1,0:T(8,128)} %get-tuple-element.254.cosine, ...), custom_call_target="tpu_custom_call" | custom-call | tf_op jit(solution)/shard_map/pallas_call | solution.py:907
  183.5 49.4 %shard_map.417 = (bf16[4,128,1280]{2,1,0:T(8,128)(2,1)}, bf16[4,160,1280]{2,1,0:T(8,128)(2,1)}) custom-call(bf16[128,1280]{1,0:T(8,128)(2,1)} %get-tuple-element.84.refs_0_, bf16[160,1280]{1,0:T(8,128)(2,1)} %bitcast.102), custom_call_target="tpu_custom_call" | custom-call | bytes 1048576 | tf_op jit(solution)/shard_map/pallas_call | solution.py:275
  232.9 3.9 convolution_convert_fusion.4
  236.7 10.1 %shard_map.418 = bf16[4,2,64,640]{3,2,1,0:T(8,128)(2,1)} custom-call(bf16[4,2,64,640]{3,2,1,0:T(8,128)(2,1)} %bitcast.110), custom_call_target="tpu_custom_call" | custom-call | bytes 1048576 | tf_op jit(solution)/shard_map/pallas_call | solution.py:827
  246.8 4.4 shard_map.419
  251.2 68.1 %shard_map.420 = (bf16[4,4,2,64,256]{4,3,2,1,0:T(8,128)(2,1)}, bf16[4,4,2,64,512]{4,3,2,1,0:T(8,128)(2,1)}, bf16[2560,512]{1,0:T(8,128)(2,1)}, bf16[2560,256]{1,0:T(8,128)(2,1)}) custom-call(bf16[64,2560]{1,0:T(8,128)(2,1)} %get-tuple-element.87.x, bf16[4,4,2,64,2560]{4,3,2,1,0:T(8,128)(2,1)} %get-tuple-element.88.cot, bf16[2560,512]{1,0:T(8,128)(2,1)} %bitcast.87, ...), custom_call_target="tpu_custom_call" | custom-call | bytes 1048576 | tf_op jit(solution)/shard_map/pallas_call | solution.py:744
  319.4 15.7 %all-to-all-start.2 = ((bf16[16,160,512]{2,1,0:T(8,128)(2,1)}), bf16[16,160,512]{2,1,0:T(8,128)(2,1)S(1)}, u32[]{:S(2)}, u32[]{:S(2)}) async-start(bf16[16,160,512]{2,1,0:T(8,128)(2,1)} %bitcast.95), calls=%async_computation.2 | async-start | bytes 5242880 | tf_op jit(solution)/shard_map/all_to_all | solution.py:1187
  335.0 122.5 %shard_map.421 = (bf16[2,64,2560]{2,1,0:T(8,128)(2,1)}, bf16[2,64,2560]{2,1,0:T(8,128)(2,1)}) custom-call(bf16[4,4,2,64,512]{4,3,2,1,0:T(8,128)(2,1)} %get-tuple-element.93, bf16[4,4,2,64,256]{4,3,2,1,0:T(8,128)(2,1)} %get-tuple-element.92, bf16[2560,512]{1,0:T(8,128)(2,1)} %bitcast.88, bf16[2560,256]{1,0:T(8,128)(2,1)} %bitcast.20.thin.refs_3_), custom_call_target="tpu_custom_call" | custom-call | bytes 1048576 | tf_op jit(solution)/shard_map/pallas_call | solution.py:537
  457.6 6.3 all-to-all-start.3
  463.9 5.9 shard_map.422
  469.8 21.9 %shard_map.423 = (bf16[4,128,640]{2,1,0:T(8,128)(2,1)}, f32[4,8,640]{2,1,0:T(8,128)}) custom-call(bf16[4,128,640]{2,1,0:T(8,128)(2,1)} %get-tuple-element.103.refs_0_, f32[4,8,640]{2,1,0:T(8,128)} %get-tuple-element.104.refs_1_), custom_call_target="tpu_custom_call" | custom-call | bytes 1048576 | tf_op jit(solution)/shard_map/pallas_call | solution.py:275
  491.8 3.3 fusion.1
  495.9 6.0 all-to-all-start.4
  501.8 3.7 convolution_convert_fusion.1
  505.5 17.1 %shard_map.424.got = bf16[4,128,1280]{2,1,0:T(8,128)(2,1)} custom-call(bf16[4,128,1280]{2,1,0:T(8,128)(2,1)} %bitcast.108), custom_call_target="tpu_custom_call" | custom-call | bytes 1048576 | tf_op jit(solution)/shard_map/pallas_call | solution.py:275
  522.6 8.9 %shard_map.425 = (bf16[16,2,128,256]{3,2,1,0:T(8,128)(2,1)}, bf16[128,1280]{1,0:T(8,128)(2,1)}) custom-call(bf16[4,128,1280]{2,1,0:T(8,128)(2,1)} %shard_map.424.got, bf16[16,2,128,256]{3,2,1,0:T(8,128)(2,1)} %bitcast.90, bf16[128,1280]{1,0:T(8,128)(2,1)} %get-tuple-element.106.queries, f32[5,128,1152]{2,1,0:T(8,128)} %get-tuple-element.107.probs, ...), custom_call_target="tpu_custom_call" | custom-call | tf_op jit(solution)/shard_map/pallas_call | solution.py:965
  531.5 18.9 %shard_map.426 = bf16[128,256]{1,0:T(8,128)(2,1)} custom-call(bf16[4,4,2,128,256]{4,3,2,1,0:T(8,128)(2,1)} %bitcast.101), custom_call_target="tpu_custom_call" | custom-call | bytes 1048576 | tf_op jit(solution)/shard_map/pallas_call | solution.py:537
  553.4 16.0 %shard_map.427 = bf16[4,128,1536]{2,1,0:T(8,128)(2,1)} custom-call(bf16[128,1536]{1,0:T(8,128)(2,1)} %pad_maximum_fusion.1.refs_0_), custom_call_target="tpu_custom_call" | custom-call | bytes 1048576 | tf_op jit(solution)/shard_map/pallas_call | solution.py:275
  570.3 3.7 multiply_reduce_fusion
  574.2 2.7 convolution_convert_fusion
  578.7 5.2 all-to-all-start.5
  588.3 10.6 %shard_map.428 = bf16[4,2,64,640]{3,2,1,0:T(8,128)(2,1)} custom-call(bf16[4,2,64,640]{3,2,1,0:T(8,128)(2,1)} %bitcast.109), custom_call_target="tpu_custom_call" | custom-call | bytes 1048576 | tf_op jit(solution)/shard_map/pallas_call | solution.py:827
  598.9 4.8 shard_map.429
  603.7 25.1 %shard_map.430 = (f32[160,2,3840]{2,1,0:T(2,128)}, f32[160,2,3840]{2,1,0:T(2,128)}, f32[160,2,3840]{2,1,0:T(2,128)}, f32[160,2,3840]{2,1,0:T(2,128)}, f32[160,38...) custom-call(f32[2]{0:T(128)} %pad_maximum_fusion.3.rates, ...), custom_call_target="tpu_custom_call" | custom-call | tf_op jit(solution)/shard_map/pallas_call | solution.py:1107
  628.8 1.8 multiply_bitcast_fusion
  632.0 1.9 add_multiply_fusion
  (119 shorter events, 27.8 us)
Async XLA Ops:
  0.7 2.8 copy-start.20
  0.7 2.8 copy-start.17
  3.4 1.3 copy-start.5
  3.5 2.0 copy-start.10
  3.5 2.0 copy-start.4
  75.9 91.2 %all-to-all-start = ((bf16[16,160,512]{2,1,0:T(8,128)(2,1)}), bf16[16,160,512]{2,1,0:T(8,128)(2,1)S(1)}, u32[]{:S(2)}, u32[]{:S(2)}) async-start(bf16[16,160,512]{2,1,0:T(8,128)(2,1)} %get-tuple-element.82), calls=%async_computation | async-start | bytes 5242880 | tf_op jit(solution)/shard_map/all_to_all | solution.py:1187
  167.1 9.6 %copy-start = (bf16[16,160,512]{2,1,0:T(8,128)(2,1)}, bf16[16,160,512]{2,1,0:T(8,128)(2,1)S(1)}, u32[]{:S(2)}) copy-start(bf16[16,160,512]{2,1,0:T(8,128)(2,1)S(1)} %all-to-all-done) | copy-start | bytes 7864324
  167.1 84.1 %all-to-all-start.1 = ((bf16[16,160,256]{2,1,0:T(8,128)(2,1)}), bf16[16,160,256]{2,1,0:T(8,128)(2,1)}, u32[]{:S(2)}, u32[]{:S(2)}) async-start(bf16[16,160,256]{2,1,0:T(8,128)(2,1)} %get-tuple-element.90), calls=%async_computation.1 | async-start | bytes 2621440 | tf_op jit(solution)/shard_map/all_to_all | solution.py:1187
  319.4 138.2 %all-to-all-start.2 = ((bf16[16,160,512]{2,1,0:T(8,128)(2,1)}), bf16[16,160,512]{2,1,0:T(8,128)(2,1)S(1)}, u32[]{:S(2)}, u32[]{:S(2)}) async-start(bf16[16,160,512]{2,1,0:T(8,128)(2,1)} %bitcast.95), calls=%async_computation.2 | async-start | bytes 5242880 | tf_op jit(solution)/shard_map/all_to_all | solution.py:1187
  457.6 12.3 %copy-start.1 = (bf16[16,160,512]{2,1,0:T(8,128)(2,1)}, bf16[16,160,512]{2,1,0:T(8,128)(2,1)S(1)}, u32[]{:S(2)}) copy-start(bf16[16,160,512]{2,1,0:T(8,128)(2,1)S(1)} %all-to-all-done.2.pair_got) | copy-start | bytes 7864324
  457.6 38.3 %all-to-all-start.3 = ((bf16[16,160,256]{2,1,0:T(8,128)(2,1)}), bf16[16,160,256]{2,1,0:T(8,128)(2,1)}, u32[]{:S(2)}, u32[]{:S(2)}) async-start(bf16[16,160,256]{2,1,0:T(8,128)(2,1)} %bitcast.107), calls=%async_computation.3 | async-start | bytes 2621440 | tf_op jit(solution)/shard_map/all_to_all | solution.py:1187
  463.9 27.9 %copy-start.22 = (bf16[4,128,1280]{2,1,0:T(8,128)(2,1)S(1)}, bf16[4,128,1280]{2,1,0:T(8,128)(2,1)}, u32[]{:S(2)}) copy-start(bf16[4,128,1280]{2,1,0:T(8,128)(2,1)} %get-tuple-element.85) | copy-start | bytes 3932164
  495.9 6.0 copy-start.24
  495.9 82.6 %all-to-all-start.4 = ((bf16[4,160,1280]{2,1,0:T(8,128)(2,1)}), bf16[4,160,1280]{2,1,0:T(8,128)(2,1)S(1)}, u32[]{:S(2)}, u32[]{:S(2)}) async-start(bf16[4,160,1280]{2,1,0:T(8,128)(2,1)} %bitcast.103), calls=%async_computation.4 | async-start | bytes 3276800 | tf_op jit(solution)/shard_map/all_to_all | solution.py:1258
  531.5 21.1 %copy-start.13 = (bf16[128,1280]{1,0:T(8,128)(2,1)S(1)}, bf16[128,1280]{1,0:T(8,128)(2,1)}, u32[]{:S(2)}) copy-start(bf16[128,1280]{1,0:T(8,128)(2,1)} %get-tuple-element.108) | copy-start | bytes 983044
  550.4 19.9 %copy-start.21 = (bf16[4,160,1536]{2,1,0:T(8,128)(2,1)S(1)}, bf16[4,160,1536]{2,1,0:T(8,128)(2,1)}, u32[]{:S(2)}) copy-start(bf16[4,160,1536]{2,1,0:T(8,128)(2,1)} %get-tuple-element.80) | copy-start | bytes 5898244
  550.4 19.9 %copy-start.23 = (bf16[4,128,640]{2,1,0:T(8,128)(2,1)S(1)}, bf16[4,128,640]{2,1,0:T(8,128)(2,1)}, u32[]{:S(2)}) copy-start(bf16[4,128,640]{2,1,0:T(8,128)(2,1)} %get-tuple-element.77) | copy-start | bytes 1966084
  578.7 50.1 %copy-start.2 = (f32[160,1280]{1,0:T(8,128)}, f32[160,1280]{1,0:T(8,128)S(1)}, u32[]{:S(2)}) copy-start(f32[160,1280]{1,0:T(8,128)S(1)} %convert_reduce_fusion.1) | copy-start | bytes 2457604
  578.7 7.5 %copy-start.18 = (f32[2,160]{1,0:T(2,128)S(1)}, f32[2,160]{1,0:T(2,128)}, u32[]{:S(2)}) copy-start(f32[2,160]{1,0:T(2,128)} %param.42) | copy-start | bytes 3844
  578.7 8.2 %copy-start.19 = (f32[2,160]{1,0:T(2,128)S(1)}, f32[2,160]{1,0:T(2,128)}, u32[]{:S(2)}) copy-start(f32[2,160]{1,0:T(2,128)} %param.36) | copy-start | bytes 3844
  578.7 51.9 %all-to-all-start.5 = ((bf16[4,160,1664]{2,1,0:T(8,128)(2,1)}), bf16[4,160,1664]{2,1,0:T(8,128)(2,1)S(1)}, u32[]{:S(2)}, u32[]{:S(2)}) async-start(bf16[4,160,1664]{2,1,0:T(8,128)(2,1)} %bitcast.37), calls=%async_computation.5 | async-start | bytes 4259840 | tf_op jit(solution)/shard_map/all_to_all | solution.py:1258
  603.7 25.1 %copy-start.3 = (bf16[1280,160]{0,1:T(8,128)(2,1)S(1)}, bf16[1280,160]{0,1:T(8,128)(2,1)}, u32[]{:S(2)}) copy-start(bf16[1280,160]{0,1:T(8,128)(2,1)} %param.27) | copy-start | bytes 1228804
  603.7 25.1 %copy-start.8 = (f32[1280,160]{0,1:T(8,128)S(1)}, f32[1280,160]{0,1:T(8,128)}, u32[]{:S(2)}) copy-start(f32[1280,160]{0,1:T(8,128)} %param.33) | copy-start | bytes 2457604
  603.7 25.1 %copy-start.9 = (f32[1280,160]{0,1:T(8,128)S(1)}, f32[1280,160]{0,1:T(8,128)}, u32[]{:S(2)}) copy-start(f32[1280,160]{0,1:T(8,128)} %param.39) | copy-start | bytes 2457604
  630.6 1.1 copy-start.6
  630.6 1.4 copy-start.7
  630.9 3.0 copy-start.14
  630.9 3.0 copy-start.15
  630.9 3.0 copy-start.16
  630.9 2.9 collective-permute-start
  633.8 2.8 copy-start.11
  633.8 2.8 copy-start.12

commit v6 on v5

--- a/solution.py
+++ b/solution.py
@@ -152,6 +152,12 @@
 
     planes_off = [lax.rem(s + k, ns) for k in range(1, ns)]
 
+    def bcopy(i, b, core):
+        ref = outs[i].at[b, :, core]
+        return pltpu.make_async_remote_copy(
+            ref, ref, sems[7 * i + 4].at[b, 0], sems[7 * i + 5].at[b, 0],
+            device_id={"mp": 1 - m}, device_id_type=MESH)
+
     def lcopy(i):
         src = ins[i].at[d] if modes[i] == "swap" else ins[i]
         return pltpu.make_async_copy(src, place(i, s, d, m), sems[7 * i + 6])
@@ -172,7 +178,7 @@
         if in_plane(i, t):
             for c in own_copies(i, b, first):
                 c.start()
-        if modes[i] == "all":
+        if modes[i] == "all" and not direct[i]:
             ccopy(i, b, d, first).start()
         if first and direct[i]:
             for p in planes_off:
@@ -189,7 +195,7 @@
             got.wait_recv()
             on.start()
 
-    def settle(i, b):
+    def settle(i, b, t):
         if relay[i]:
             waits = [(x, [precv(i, b, x, 1)]), (y, [precv(i, b, y, 0)]),
                      (across, [precv(i, b, across, 0), precv(i, b, across, 1)])]
@@ -198,8 +204,12 @@
         for e, got in waits:
             for w in got:
                 w.wait_recv()
-            if modes[i] == "all":
+            if modes[i] == "all" and not direct[i]:
                 ccopy(i, b, e, False).start()
+        if direct[i]:
+            if t == 0:
+                lcopy(i).wait()
+            bcopy(i, b, m).start()
 
     def finish(i, b, t, way):
         first = t == 0
@@ -217,11 +227,14 @@
         if direct[i] and first:
             for p in planes_off:
                 dcopy(i, p, s).wait_send()
-        if modes[i] == "all":
+        if direct[i]:
+            bcopy(i, b, 1 - m).wait_recv()
+            bcopy(i, b, m).wait_send()
+        elif modes[i] == "all":
             for e in [d] + peers:
                 crecv(i, b, e).wait_recv()
                 ccopy(i, b, e, False).wait_send()
-        if first:
+        if first and not direct[i]:
             lcopy(i).wait()
 
     def each(steps, chosen, fn):
@@ -256,8 +269,8 @@
             each(levels[t - 1], lambda i, t: relay[i] and in_plane(i, t), lambda i, b, t, way: pass_on(i, b))
         if 1 <= t - lag:
             each(levels[t - lag], lambda i, t: late[i], arrive)
-    each(steps, lambda i, t: in_plane(i, t) and not direct[i], lambda i, b, t, way: settle(i, b))
-    each(levels[0] + straight, lambda i, t: direct[i], lambda i, b, t, way: settle(i, b))
+    each(steps, lambda i, t: in_plane(i, t) and not direct[i], lambda i, b, t, way: settle(i, b, t))
+    each(levels[0] + straight, lambda i, t: direct[i], lambda i, b, t, way: settle(i, b, t))
     each(steps, lambda i, t: (t == 0 or in_z(i)) and not direct[i], finish)
     each(levels[0] + straight, lambda i, t: direct[i], finish)
 

time: 647 us -> 647 us (level)
  no operation moved by 1% of the time
where the time goes in v6:
time: 647 us; the launch traced here: 638 us
  Pallas kernels  528 us (82%)
  starting transfers between devices  55.2 us (9%)
  matrix products  21.6 us (3%)
  other arithmetic  18.4 us (3%)
  local copies, waits for them, and re-layouts  11.9 us (2%)
    pallas_call x7, Pallas kernels, gather(): pl.pallas_call(partial(gather_kernel, ns, nd, modes, work, len(work_args)...  242 us
    pallas_call x2, Pallas kernels, reduce_scatter(): pl.pallas_call(partial(reduce_kernel, ns, nd, share, count, made), out_sh...  141 us
    pallas_call x1, Pallas kernels, feed(): pl.pallas_call(partial(feed_kernel, ns, nd), out_shape=[jax.ShapeDtypeStr...  68.1 us
    all_to_all x4, starting transfers between devices, trade(): return lax.all_to_all(value.reshape(n, own_d, -1), TOK, 0, 0, tiled=True)  43.6 us
    pallas_call x1, Pallas kernels, unpack_adam(): pl.pallas_call(unpack_kernel, out_shape=[shape3] * 4 + [shape2] * 4, grid...  25.1 us
    pallas_call x2, Pallas kernels, plane_reduce(): pl.pallas_call(partial(plane_kernel, ns, nd), out_shape=jax.ShapeDtypeStr...  20.7 us
    pallas_call x3, Pallas kernels, local(): pl.pallas_call(kernel, out_shape=[jax.ShapeDtypeStruct(shape, dtype) for...  15.1 us
  transfers between devices with their start and end apart: 7, of which 1 were waited for; matrix products, arithmetic and copies ran while one was open for 6% of the time, Pallas kernels for 61%

profile of v6, /device:TPU:14, one launch (start us, length us, event | category | flops | bytes accessed | tf_op | source)
XLA Modules:
  0.0 638.1 jit_solution(5149471403023581137)
XLA Ops:
  7.0 68.8 %shard_map.413 = (f32[4,4,2,8,256]{4,3,2,1,0:T(8,128)}, bf16[4,128,640]{2,1,0:T(8,128)(2,1)}, bf16[4,4,2,64,2560]{4,3,2,1,0:T(8,128)(2,1)}, bf16[4,160,1536]{2,1...) custom-call(f32[8,256]{1,0:T(8,128)} %fusion.26.refs_0_, ...), custom_call_target="tpu_custom_call" | custom-call | bytes 1048576 | tf_op jit(solution)/shard_map/pallas_call | solution.py:288
  75.8 14.8 %all-to-all-start = ((bf16[16,160,512]{2,1,0:T(8,128)(2,1)}), bf16[16,160,512]{2,1,0:T(8,128)(2,1)S(1)}, u32[]{:S(2)}, u32[]{:S(2)}) async-start(bf16[16,160,512]{2,1,0:T(8,128)(2,1)} %get-tuple-element.82), calls=%async_computation | async-start | bytes 5242880 | tf_op jit(solution)/shard_map/all_to_all | solution.py:1200
  91.7 4.4 convolution_convert_fusion.2
  96.1 35.9 %shard_map.414.got = bf16[4,128,1536]{2,1,0:T(8,128)(2,1)} custom-call(bf16[4,128,1536]{2,1,0:T(8,128)(2,1)} %bitcast.104), custom_call_target="tpu_custom_call" | custom-call | bytes 1048576 | tf_op jit(solution)/shard_map/pallas_call | solution.py:288
  134.4 32.9 %shard_map.415 = bf16[4,4,2,128,256]{4,3,2,1,0:T(8,128)(2,1)} custom-call(bf16[128,256]{1,0:T(8,128)(2,1)} %fusion.9.refs_0_), custom_call_target="tpu_custom_call" | custom-call | bytes 1048576 | tf_op jit(solution)/shard_map/pallas_call | solution.py:288
  167.3 6.8 %all-to-all-start.1 = ((bf16[16,160,256]{2,1,0:T(8,128)(2,1)}), bf16[16,160,256]{2,1,0:T(8,128)(2,1)}, u32[]{:S(2)}, u32[]{:S(2)}) async-start(bf16[16,160,256]{2,1,0:T(8,128)(2,1)} %get-tuple-element.90), calls=%async_computation.1 | async-start | bytes 2621440 | tf_op jit(solution)/shard_map/all_to_all | solution.py:1200
  176.9 6.8 %shard_map.416 = (bf16[128,1280]{1,0:T(8,128)(2,1)}, bf16[128,1280]{1,0:T(8,128)(2,1)}, f32[5,128,1152]{2,1,0:T(8,128)}) custom-call(bf16[4,128,1536]{2,1,0:T(8,128)(2,1)} %shard_map.414.got, bf16[16,2,128,256]{3,2,1,0:T(8,128)(2,1)} %bitcast.89, f32[128,1152]{1,0:T(8,128)} %fusion.5.allowed, f32[128,128]{1,0:T(8,128)} %get-tuple-element.254.cosine, ...), custom_call_target="tpu_custom_call" | custom-call | tf_op jit(solution)/shard_map/pallas_call | solution.py:920
  183.6 49.4 %shard_map.417 = (bf16[4,128,1280]{2,1,0:T(8,128)(2,1)}, bf16[4,160,1280]{2,1,0:T(8,128)(2,1)}) custom-call(bf16[128,1280]{1,0:T(8,128)(2,1)} %get-tuple-element.84.refs_0_, bf16[160,1280]{1,0:T(8,128)(2,1)} %bitcast.102), custom_call_target="tpu_custom_call" | custom-call | bytes 1048576 | tf_op jit(solution)/shard_map/pallas_call | solution.py:288
  233.0 3.9 convolution_convert_fusion.4
  236.9 10.1 %shard_map.418 = bf16[4,2,64,640]{3,2,1,0:T(8,128)(2,1)} custom-call(bf16[4,2,64,640]{3,2,1,0:T(8,128)(2,1)} %bitcast.110), custom_call_target="tpu_custom_call" | custom-call | bytes 1048576 | tf_op jit(solution)/shard_map/pallas_call | solution.py:840
  247.0 4.4 shard_map.419
  251.4 68.1 %shard_map.420 = (bf16[4,4,2,64,256]{4,3,2,1,0:T(8,128)(2,1)}, bf16[4,4,2,64,512]{4,3,2,1,0:T(8,128)(2,1)}, bf16[2560,512]{1,0:T(8,128)(2,1)}, bf16[2560,256]{1,0:T(8,128)(2,1)}) custom-call(bf16[64,2560]{1,0:T(8,128)(2,1)} %get-tuple-element.87.x, bf16[4,4,2,64,2560]{4,3,2,1,0:T(8,128)(2,1)} %get-tuple-element.88.cot, bf16[2560,512]{1,0:T(8,128)(2,1)} %bitcast.87, ...), custom_call_target="tpu_custom_call" | custom-call | bytes 1048576 | tf_op jit(solution)/shard_map/pallas_call | solution.py:757
  319.5 15.7 %all-to-all-start.2 = ((bf16[16,160,512]{2,1,0:T(8,128)(2,1)}), bf16[16,160,512]{2,1,0:T(8,128)(2,1)S(1)}, u32[]{:S(2)}, u32[]{:S(2)}) async-start(bf16[16,160,512]{2,1,0:T(8,128)(2,1)} %bitcast.95), calls=%async_computation.2 | async-start | bytes 5242880 | tf_op jit(solution)/shard_map/all_to_all | solution.py:1200
  335.2 122.5 %shard_map.421 = (bf16[2,64,2560]{2,1,0:T(8,128)(2,1)}, bf16[2,64,2560]{2,1,0:T(8,128)(2,1)}) custom-call(bf16[4,4,2,64,512]{4,3,2,1,0:T(8,128)(2,1)} %get-tuple-element.93, bf16[4,4,2,64,256]{4,3,2,1,0:T(8,128)(2,1)} %get-tuple-element.92, bf16[2560,512]{1,0:T(8,128)(2,1)} %bitcast.88, bf16[2560,256]{1,0:T(8,128)(2,1)} %bitcast.20.thin.refs_3_), custom_call_target="tpu_custom_call" | custom-call | bytes 1048576 | tf_op jit(solution)/shard_map/pallas_call | solution.py:550
  457.7 6.3 all-to-all-start.3
  464.1 5.9 shard_map.422
  470.0 21.9 %shard_map.423 = (bf16[4,128,640]{2,1,0:T(8,128)(2,1)}, f32[4,8,640]{2,1,0:T(8,128)}) custom-call(bf16[4,128,640]{2,1,0:T(8,128)(2,1)} %get-tuple-element.103.refs_0_, f32[4,8,640]{2,1,0:T(8,128)} %get-tuple-element.104.refs_1_), custom_call_target="tpu_custom_call" | custom-call | bytes 1048576 | tf_op jit(solution)/shard_map/pallas_call | solution.py:288
  492.0 3.3 fusion.1
  496.0 6.0 all-to-all-start.4
  502.0 3.7 convolution_convert_fusion.1
  505.7 17.1 %shard_map.424.got = bf16[4,128,1280]{2,1,0:T(8,128)(2,1)} custom-call(bf16[4,128,1280]{2,1,0:T(8,128)(2,1)} %bitcast.108), custom_call_target="tpu_custom_call" | custom-call | bytes 1048576 | tf_op jit(solution)/shard_map/pallas_call | solution.py:288
  522.7 8.9 %shard_map.425 = (bf16[16,2,128,256]{3,2,1,0:T(8,128)(2,1)}, bf16[128,1280]{1,0:T(8,128)(2,1)}) custom-call(bf16[4,128,1280]{2,1,0:T(8,128)(2,1)} %shard_map.424.got, bf16[16,2,128,256]{3,2,1,0:T(8,128)(2,1)} %bitcast.90, bf16[128,1280]{1,0:T(8,128)(2,1)} %get-tuple-element.106.queries, f32[5,128,1152]{2,1,0:T(8,128)} %get-tuple-element.107.probs, ...), custom_call_target="tpu_custom_call" | custom-call | tf_op jit(solution)/shard_map/pallas_call | solution.py:978
  531.6 18.9 %shard_map.426 = bf16[128,256]{1,0:T(8,128)(2,1)} custom-call(bf16[4,4,2,128,256]{4,3,2,1,0:T(8,128)(2,1)} %bitcast.101), custom_call_target="tpu_custom_call" | custom-call | bytes 1048576 | tf_op jit(solution)/shard_map/pallas_call | solution.py:550
  553.5 16.0 %shard_map.427 = bf16[4,128,1536]{2,1,0:T(8,128)(2,1)} custom-call(bf16[128,1536]{1,0:T(8,128)(2,1)} %pad_maximum_fusion.1.refs_0_), custom_call_target="tpu_custom_call" | custom-call | bytes 1048576 | tf_op jit(solution)/shard_map/pallas_call | solution.py:288
  570.5 3.7 multiply_reduce_fusion
  574.3 2.7 convolution_convert_fusion
  578.9 5.2 all-to-all-start.5
  588.4 10.6 %shard_map.428 = bf16[4,2,64,640]{3,2,1,0:T(8,128)(2,1)} custom-call(bf16[4,2,64,640]{3,2,1,0:T(8,128)(2,1)} %bitcast.109), custom_call_target="tpu_custom_call" | custom-call | bytes 1048576 | tf_op jit(solution)/shard_map/pallas_call | solution.py:840
  599.0 4.8 shard_map.429
  603.8 25.1 %shard_map.430 = (f32[160,2,3840]{2,1,0:T(2,128)}, f32[160,2,3840]{2,1,0:T(2,128)}, f32[160,2,3840]{2,1,0:T(2,128)}, f32[160,2,3840]{2,1,0:T(2,128)}, f32[160,38...) custom-call(f32[2]{0:T(128)} %pad_maximum_fusion.3.rates, ...), custom_call_target="tpu_custom_call" | custom-call | tf_op jit(solution)/shard_map/pallas_call | solution.py:1120
  628.9 1.8 multiply_bitcast_fusion
  632.1 1.9 add_multiply_fusion
  (119 shorter events, 27.8 us)
Async XLA Ops:
  0.7 2.8 copy-start.20
  0.7 2.8 copy-start.17
  3.4 1.3 copy-start.5
  3.5 2.0 copy-start.10
  3.5 2.0 copy-start.4
  75.8 91.5 %all-to-all-start = ((bf16[16,160,512]{2,1,0:T(8,128)(2,1)}), bf16[16,160,512]{2,1,0:T(8,128)(2,1)S(1)}, u32[]{:S(2)}, u32[]{:S(2)}) async-start(bf16[16,160,512]{2,1,0:T(8,128)(2,1)} %get-tuple-element.82), calls=%async_computation | async-start | bytes 5242880 | tf_op jit(solution)/shard_map/all_to_all | solution.py:1200
  167.3 9.6 %copy-start = (bf16[16,160,512]{2,1,0:T(8,128)(2,1)}, bf16[16,160,512]{2,1,0:T(8,128)(2,1)S(1)}, u32[]{:S(2)}) copy-start(bf16[16,160,512]{2,1,0:T(8,128)(2,1)S(1)} %all-to-all-done) | copy-start | bytes 7864324
  167.3 84.0 %all-to-all-start.1 = ((bf16[16,160,256]{2,1,0:T(8,128)(2,1)}), bf16[16,160,256]{2,1,0:T(8,128)(2,1)}, u32[]{:S(2)}, u32[]{:S(2)}) async-start(bf16[16,160,256]{2,1,0:T(8,128)(2,1)} %get-tuple-element.90), calls=%async_computation.1 | async-start | bytes 2621440 | tf_op jit(solution)/shard_map/all_to_all | solution.py:1200
  319.5 138.2 %all-to-all-start.2 = ((bf16[16,160,512]{2,1,0:T(8,128)(2,1)}), bf16[16,160,512]{2,1,0:T(8,128)(2,1)S(1)}, u32[]{:S(2)}, u32[]{:S(2)}) async-start(bf16[16,160,512]{2,1,0:T(8,128)(2,1)} %bitcast.95), calls=%async_computation.2 | async-start | bytes 5242880 | tf_op jit(solution)/shard_map/all_to_all | solution.py:1200
  457.7 12.3 %copy-start.1 = (bf16[16,160,512]{2,1,0:T(8,128)(2,1)}, bf16[16,160,512]{2,1,0:T(8,128)(2,1)S(1)}, u32[]{:S(2)}) copy-start(bf16[16,160,512]{2,1,0:T(8,128)(2,1)S(1)} %all-to-all-done.2.pair_got) | copy-start | bytes 7864324
  457.7 38.3 %all-to-all-start.3 = ((bf16[16,160,256]{2,1,0:T(8,128)(2,1)}), bf16[16,160,256]{2,1,0:T(8,128)(2,1)}, u32[]{:S(2)}, u32[]{:S(2)}) async-start(bf16[16,160,256]{2,1,0:T(8,128)(2,1)} %bitcast.107), calls=%async_computation.3 | async-start | bytes 2621440 | tf_op jit(solution)/shard_map/all_to_all | solution.py:1200
  464.1 27.9 %copy-start.22 = (bf16[4,128,1280]{2,1,0:T(8,128)(2,1)S(1)}, bf16[4,128,1280]{2,1,0:T(8,128)(2,1)}, u32[]{:S(2)}) copy-start(bf16[4,128,1280]{2,1,0:T(8,128)(2,1)} %get-tuple-element.85) | copy-start | bytes 3932164
  496.0 6.0 copy-start.24
  496.0 82.6 %all-to-all-start.4 = ((bf16[4,160,1280]{2,1,0:T(8,128)(2,1)}), bf16[4,160,1280]{2,1,0:T(8,128)(2,1)S(1)}, u32[]{:S(2)}, u32[]{:S(2)}) async-start(bf16[4,160,1280]{2,1,0:T(8,128)(2,1)} %bitcast.103), calls=%async_computation.4 | async-start | bytes 3276800 | tf_op jit(solution)/shard_map/all_to_all | solution.py:1271
  531.6 21.1 %copy-start.13 = (bf16[128,1280]{1,0:T(8,128)(2,1)S(1)}, bf16[128,1280]{1,0:T(8,128)(2,1)}, u32[]{:S(2)}) copy-start(bf16[128,1280]{1,0:T(8,128)(2,1)} %get-tuple-element.108) | copy-start | bytes 983044
  550.5 19.9 %copy-start.21 = (bf16[4,160,1536]{2,1,0:T(8,128)(2,1)S(1)}, bf16[4,160,1536]{2,1,0:T(8,128)(2,1)}, u32[]{:S(2)}) copy-start(bf16[4,160,1536]{2,1,0:T(8,128)(2,1)} %get-tuple-element.80) | copy-start | bytes 5898244
  550.5 19.9 %copy-start.23 = (bf16[4,128,640]{2,1,0:T(8,128)(2,1)S(1)}, bf16[4,128,640]{2,1,0:T(8,128)(2,1)}, u32[]{:S(2)}) copy-start(bf16[4,128,640]{2,1,0:T(8,128)(2,1)} %get-tuple-element.77) | copy-start | bytes 1966084
  578.8 50.1 %copy-start.2 = (f32[160,1280]{1,0:T(8,128)}, f32[160,1280]{1,0:T(8,128)S(1)}, u32[]{:S(2)}) copy-start(f32[160,1280]{1,0:T(8,128)S(1)} %convert_reduce_fusion.1) | copy-start | bytes 2457604
  578.8 7.5 %copy-start.18 = (f32[2,160]{1,0:T(2,128)S(1)}, f32[2,160]{1,0:T(2,128)}, u32[]{:S(2)}) copy-start(f32[2,160]{1,0:T(2,128)} %param.42) | copy-start | bytes 3844
  578.9 8.2 %copy-start.19 = (f32[2,160]{1,0:T(2,128)S(1)}, f32[2,160]{1,0:T(2,128)}, u32[]{:S(2)}) copy-start(f32[2,160]{1,0:T(2,128)} %param.36) | copy-start | bytes 3844
  578.9 51.9 %all-to-all-start.5 = ((bf16[4,160,1664]{2,1,0:T(8,128)(2,1)}), bf16[4,160,1664]{2,1,0:T(8,128)(2,1)S(1)}, u32[]{:S(2)}, u32[]{:S(2)}) async-start(bf16[4,160,1664]{2,1,0:T(8,128)(2,1)} %bitcast.37), calls=%async_computation.5 | async-start | bytes 4259840 | tf_op jit(solution)/shard_map/all_to_all | solution.py:1271
  603.8 25.1 %copy-start.3 = (bf16[1280,160]{0,1:T(8,128)(2,1)S(1)}, bf16[1280,160]{0,1:T(8,128)(2,1)}, u32[]{:S(2)}) copy-start(bf16[1280,160]{0,1:T(8,128)(2,1)} %param.27) | copy-start | bytes 1228804
  603.8 25.1 %copy-start.8 = (f32[1280,160]{0,1:T(8,128)S(1)}, f32[1280,160]{0,1:T(8,128)}, u32[]{:S(2)}) copy-start(f32[1280,160]{0,1:T(8,128)} %param.33) | copy-start | bytes 2457604
  603.8 25.1 %copy-start.9 = (f32[1280,160]{0,1:T(8,128)S(1)}, f32[1280,160]{0,1:T(8,128)}, u32[]{:S(2)}) copy-start(f32[1280,160]{0,1:T(8,128)} %param.39) | copy-start | bytes 2457604
  630.7 1.1 copy-start.6
  630.7 1.4 copy-start.7
  631.0 3.0 copy-start.14
  631.1 3.0 copy-start.15
  631.1 3.0 copy-start.16
  631.1 2.9 collective-permute-start
  634.0 2.8 copy-start.11
  634.0 2.8 copy-start.12
